TPU v7x, 32 devices: a whole 2x2x4 slice. The times are simulated.
32 devices in a mesh: grp: 8 (over y, x, core), aux: 4 (over z).
Axes of the slice: x: 2, y: 2, z: 4, core: 2. Of those that a mesh axis runs over, the one named last changes fastest.
Arguments:
- integral_tiles: bfloat16 [8, 4, 12, 32, 128, 128], P('grp', 'aux'), may hold values from -6 to 6
- row_blocks: int32 [8, 4, 12], P('grp', 'aux'), may hold values from 0 to 31
- col_blocks: int32 [8, 4, 12], P('grp', 'aux'), may hold values from 0 to 3
- aux_blocks: int32 [8, 4, 12], P('grp', 'aux'), may hold values from 0 to 15
- tile_counts: int32 [8, 4], P('grp', 'aux'), may hold values from 1 to 12, as said below
- occ_coeffs: bfloat16 [8, 4096], P(None, 'grp'), may hold values from -0.5 to 0.5
- vir_coeffs: bfloat16 [4096, 1024], P('grp'), may hold values from -0.5 to 0.5
Outputs:
- pair_factors: float32 [8192, 2048], P(('grp', 'aux'))
Inputs may be any that keep to these rules, and one draw needn't show every extreme that they name: `tile_counts`: tile counts of the devices; some device holds exactly 12 kept tiles.
All inputs are finite; a program needn't handle non-finite values.
Results may differ from a plain program's by a relative error of at most 0.0029.
Values may be sent and summed in bfloat16 or wider, within the bound.
No kernel may reach another device: no remote copies, remote signals or barrier semaphores. Data moves between devices by JAX's collectives and lax.ppermute only.
A program may use at most 128 MiB of HBM per device.

v0:
```python
import jax
import jax.numpy as jnp
from jax import lax
from jax.sharding import PartitionSpec as P

O = 8
V = 1024
BLK = 128
PB = 32
PDEV = 512
KMAX = 12


def tile_term(tile, row_block, col_block, occ_whole, vir_coeffs):
    occ_block = lax.dynamic_slice_in_dim(occ_whole, row_block * BLK, BLK, 1)
    half_tile = jnp.einsum(
        "im,pmn->ipn", occ_block, tile, preferred_element_type=jnp.float32
    ).astype(jnp.bfloat16)
    vir_block = lax.dynamic_slice_in_dim(vir_coeffs, col_block * BLK, BLK, 0)
    term = jnp.einsum("na,ipn->iap", vir_block, half_tile, preferred_element_type=jnp.float32)
    return term.reshape(O * V, PB)


def shards(integral_tiles, row_blocks, col_blocks, aux_blocks, tile_counts, occ_coeffs, vir_coeffs):
    occ_whole = lax.all_gather(occ_coeffs, "grp", axis=1, tiled=True)
    my_tiles = integral_tiles[0, 0]
    my_rows = row_blocks[0, 0]
    my_cols = col_blocks[0, 0]
    my_aux = aux_blocks[0, 0]
    my_count = tile_counts[0, 0]
    group_size = lax.axis_size("grp")
    aux_size = lax.axis_size("aux")
    partial_value = jnp.zeros((O * V, PDEV), jnp.float32)

    def add_tile(slot, partial_value, weight):
        term = tile_term(my_tiles[slot], my_rows[slot], my_cols[slot], occ_whole, vir_coeffs)
        start = my_aux[slot] * PB
        current = lax.dynamic_slice_in_dim(partial_value, start, PB, 1)
        return lax.dynamic_update_slice_in_dim(partial_value, current + weight * term, start, 1)

    def padded_step(slot, partial_value):
        weight = (slot < my_count).astype(jnp.float32)
        return add_tile(slot, partial_value, weight)

    partial_value = lax.fori_loop(0, KMAX, padded_step, partial_value)
    share = O * V // (group_size * aux_size)
    reordered = (
        partial_value.reshape(group_size, aux_size, share, PDEV)
        .transpose(1, 0, 2, 3)
        .reshape(O * V, PDEV)
    )
    regrouped = lax.all_to_all(reordered, "aux", split_axis=0, concat_axis=1, tiled=True)
    pair_factors = lax.psum_scatter(regrouped, "grp", scatter_dimension=0, tiled=True)
    return pair_factors


def solution(mesh):
    in_specs = (
        P("grp", "aux", None, None, None, None),
        P("grp", "aux", None),
        P("grp", "aux", None),
        P("grp", "aux", None),
        P("grp", "aux"),
        P(None, "grp"),
        P("grp", None),
    )
    out_specs = P(("grp", "aux"), None)
    return jax.shard_map(shards, mesh=mesh, in_specs=in_specs, out_specs=out_specs, check_vma=False)
```

profile of v0, /device:TPU:0, one launch (start us, length us, event | category | flops | bytes accessed | tf_op | source)
XLA Modules:
  0.0 693.5 jit_solution(12319430988173137480)
XLA Ops:
  6.5 11.0 %all_gather.3 = bf16[8,4096]{1,0:T(8,128)(2,1)S(1)} all-gather(bf16[8,512]{1,0:T(8,128)(2,1)} %param.14), channel_id=1, replica_groups=mesh['grp'=8,'aux'=4] {'grp'}, dimensions={1}, use_global_device_ids=true | all-gather | bytes 73728 | tf_op jit(solution)/shard_map/all_gather | solution.py:25
  17.5 7.8 %broadcast_in_dim.3 = f32[8192,512]{0,1:T(8,128)} broadcast(f32[]{:T(128)} %constant.52.clone.1), dimensions={} | broadcast | bytes 16777220 | tf_op jit(solution)/shard_map/broadcast_in_dim | solution.py:33
  25.3 113.6 %while.13 = (s32[]{:T(128)}, f32[8192,512]{0,1:T(8,128)}, s32[12]{0:T(128)S(1)}, s32[]{:T(128)}, s32[12]{0:T(128)S(1)}, /*index=5*/bf16[8,4096]{1,0:T(8,128)(2,1...) while((s32[]{:T(128)}, f32[8192,512]{0,1:T(8,128)}, ...), condition=%wide.region_1.0_spmd, body=%wide.region_0.0_spmd.sunk | while | flops 76054544 | bytes 7735653 | solution.py:45
  28.4 0.6 dynamic_slice.74
  29.6 1.5 convolution_convert_fusion.2
  31.1 1.2 fusion.19
  32.4 2.3 add_dynamic-update-slice_fusion.2
  36.6 0.6 dynamic_slice.75
  37.8 0.6 dynamic_slice.74
  39.1 1.5 convolution_convert_fusion.2
  40.5 1.2 fusion.19
  41.9 2.3 add_dynamic-update-slice_fusion.2
  48.5 1.5 convolution_convert_fusion.2
  50.0 1.2 fusion.19
  51.3 2.3 add_dynamic-update-slice_fusion.2
  58.0 1.5 convolution_convert_fusion.2
  59.5 1.2 fusion.19
  60.8 2.3 add_dynamic-update-slice_fusion.2
  67.4 1.5 convolution_convert_fusion.2
  68.9 1.2 fusion.19
  70.2 2.4 add_dynamic-update-slice_fusion.2
  76.9 1.5 convolution_convert_fusion.2
  78.4 1.2 fusion.19
  79.7 2.3 add_dynamic-update-slice_fusion.2
  86.4 1.5 convolution_convert_fusion.2
  87.9 1.2 fusion.19
  89.2 2.4 add_dynamic-update-slice_fusion.2
  95.9 1.5 convolution_convert_fusion.2
  97.4 1.2 fusion.19
  98.7 2.3 add_dynamic-update-slice_fusion.2
  105.4 1.5 convolution_convert_fusion.2
  106.8 1.2 fusion.19
  108.2 2.3 add_dynamic-update-slice_fusion.2
  114.8 1.5 convolution_convert_fusion.2
  116.3 1.2 fusion.19
  117.6 2.3 add_dynamic-update-slice_fusion.2
  124.3 1.5 convolution_convert_fusion.2
  125.7 1.2 fusion.19
  127.1 2.3 add_dynamic-update-slice_fusion.2
  133.7 1.5 convolution_convert_fusion.2
  135.2 1.2 fusion.19
  136.5 2.4 add_dynamic-update-slice_fusion.2
  138.9 20.4 %reshape.21 = f32[8,4,256,512]{2,1,0,3:T(4,128)} reshape(f32[8192,512]{0,1:T(8,128)} %get-tuple-element.159) | data formatting | bytes 33554432 | tf_op jit(solution)/shard_map/reshape | solution.py:48
  159.3 19.2 %copy.16 = f32[8,4,256,512]{3,2,0,1:T(8,128)} copy(f32[8,4,256,512]{2,1,0,3:T(4,128)} %reshape.21) | data formatting | bytes 33554432 | tf_op jit(solution)/shard_map/reshape | solution.py:48
  178.5 374.5 %all_to_all.19 = f32[4,2048,512]{2,1,0:T(8,128)} all-to-all(f32[4,2048,512]{2,1,0:T(8,128)} %bitcast.47), channel_id=1, replica_groups=mesh['grp'=8,'aux'=4] {'aux'}, dimensions={0} | all-to-all | bytes 33554432 | tf_op jit(solution)/shard_map/all_to_all | solution.py:52
  553.1 16.4 %copy.17 = f32[4,2048,512]{1,2,0:T(8,128)} copy(f32[4,2048,512]{2,1,0:T(8,128)} %all_to_all.19) | data formatting | bytes 33554432 | tf_op jit(solution)/shard_map/all_to_all | solution.py:52
  569.5 114.3 %reduce-scatter.2.cloned.1.call-done = f32[256,2048]{0,1:T(8,128)} async-done(((f32[2048,2048]{0,1:T(8,128)}), f32[256,2048]{0,1:T(8,128)}) %reduce-scatter.2.cloned.1.call-update) | async-done | bytes 2097168 | tf_op jit(solution)/shard_map/reduce_scatter | solution.py:53
  683.8 2.9 copy.18
  (53 shorter events, 20.6 us)
Async XLA Ops:
  6.5 18.7 %copy-start = (s32[1,1,12]{2,1,0:T(1,128)S(1)}, s32[1,1,12]{2,1,0:T(1,128)}, u32[]{:S(2)}) copy-start(s32[1,1,12]{2,1,0:T(1,128)} %param.12) | copy-start | bytes 148
  6.5 18.7 %copy-start.2 = (s32[1,1,12]{2,1,0:T(1,128)S(1)}, s32[1,1,12]{2,1,0:T(1,128)}, u32[]{:S(2)}) copy-start(s32[1,1,12]{2,1,0:T(1,128)} %param.11) | copy-start | bytes 148
  6.5 18.7 %copy-start.1 = (s32[1,1,12]{2,1,0:T(1,128)S(1)}, s32[1,1,12]{2,1,0:T(1,128)}, u32[]{:S(2)}) copy-start(s32[1,1,12]{2,1,0:T(1,128)} %param.10) | copy-start | bytes 148
  6.5 677.2 %reduce-scatter.2.cloned.1.call-start = ((), (), s32[]{:S(2)}) async-start(), calls=%async_computation.2 | async-start | bytes 18874368 | tf_op jit(solution)/shard_map/reduce_scatter | solution.py:53
Sparse Core Ops, SparseCore 0:
  569.6 114.1 reduce-scatter.1
where the time goes:
time: 697 us; the launch traced here: 693 us
  blocking collectives  386 us (55%)
  waiting for transfers between devices  114 us (16%)
  local copies, waits for them, and re-layouts  89 us (13%)
  matrix products  32.6 us (5%)
  loops' own time  30.7 us (4%)
  other arithmetic  28 us (4%)
  between operations  13.4 us (2%)
    all_to_all x1, blocking collectives, shards(): lax.all_to_all(reordered, 'aux', split_axis=0, concat_axis=1, tiled=True)  375 us
    reduce_scatter x1, waiting for transfers between devices, shards(): lax.psum_scatter(regrouped, 'grp', scatter_dimension=0, tiled=True)  114 us
    reshape x2, local copies, waits for them, and re-layouts, shards(): partial_value.reshape(group_size, aux_size, share, PDEV)  39.6 us
    another operation x1, loops' own time, shards(): partial_value = lax.fori_loop(0, KMAX, padded_step, partial_value)  30.7 us
    dynamic_update_slice x12, other arithmetic, add_tile(): lax.dynamic_update_slice_in_dim(partial_value, current + weight * term, s...  28 us
    dot_general x12, matrix products, tile_term(): jnp.einsum('im,pmn->ipn', occ_block, tile, preferred_element_type=jnp.flo...  17.6 us
    all_to_all x1, local copies, waits for them, and re-layouts, shards(): lax.all_to_all(reordered, 'aux', split_axis=0, concat_axis=1, tiled=True)  16.4 us
    dot_general x12, matrix products, tile_term(): jnp.einsum('na,ipn->iap', vir_block, half_tile, preferred_element_type=jn...  14.9 us
  transfers between devices with their start and end apart: 1, of which 1 were waited for; matrix products, arithmetic and copies ran while one was open for 0% of the time, Pallas kernels for 0%

commit v1 on v0

v1 whole, which is shorter than its diff:
```python
import functools

import jax
import jax.numpy as jnp
from jax import lax
from jax.experimental import pallas as pl
from jax.experimental.pallas import tpu as pltpu
from jax.sharding import PartitionSpec as P

PDEV = 512


def half_kernel(rows_ref, count_ref, occ_ref, tile_ref, half_ref, stage_ref):
    slot = pl.program_id(0)
    orbitals, _, pb, blk = half_ref.shape

    @pl.when(slot < count_ref[0])
    def _():
        occ = occ_ref[...].astype(jnp.float32)[:orbitals]
        zero = jnp.zeros_like(occ)
        upper = jnp.concatenate([occ, zero], axis=1)
        lower = jnp.concatenate([zero, occ], axis=1)
        pair = jnp.concatenate([upper, lower], axis=0).astype(jnp.bfloat16)
        for p in range(0, pb, 2):
            rhs = tile_ref[0, p : p + 2].reshape(2 * blk, blk)
            stage_ref[p * orbitals : (p + 2) * orbitals, :] = jnp.dot(
                pair, rhs, preferred_element_type=jnp.float32
            )
        for i in range(orbitals):
            half_ref[i, 0] = stage_ref[pl.ds(i, pb, stride=orbitals), :].astype(jnp.bfloat16)

    @pl.when(slot >= count_ref[0])
    def _():
        half_ref[...] = jnp.zeros_like(half_ref)


def half_transform(tiles, rows, count, occ_ext, orbitals):
    kmax, pb, blk, _ = tiles.shape
    return pl.pallas_call(
        half_kernel,
        grid_spec=pltpu.PrefetchScalarGridSpec(
            num_scalar_prefetch=2,
            grid=(kmax,),
            in_specs=[
                pl.BlockSpec((occ_ext.shape[0], blk), lambda k, rows, count: (0, rows[k])),
                pl.BlockSpec(
                    (1, pb, blk, blk), lambda k, rows, count: (jnp.minimum(k, count[0] - 1), 0, 0, 0)
                ),
            ],
            out_specs=pl.BlockSpec((orbitals, 1, pb, blk), lambda k, rows, count: (0, k, 0, 0)),
            scratch_shapes=[pltpu.VMEM((pb * orbitals, blk), jnp.float32)],
        ),
        out_shape=jax.ShapeDtypeStruct((orbitals, kmax, pb, blk), jnp.bfloat16),
        compiler_params=pltpu.CompilerParams(vmem_limit_bytes=24 << 20),
        cost_estimate=pl.CostEstimate(
            flops=2 * tiles.size * orbitals * 2, bytes_accessed=tiles.size * 2, transcendentals=0
        ),
        name="half_transform",
    )(rows, count, occ_ext, tiles)


def pair_kernel(kmax, pb, code_ref, where_ref, half_ref, vir_ref, own_ref, send_ref, dense_ref, sum_ref, turn_ref):
    g = pl.program_id(0)
    per_dev = PDEV // pb
    blk = half_ref.shape[2]
    dense_ref[...] = jnp.zeros_like(dense_ref)
    codes = [code_ref[g * kmax + k] for k in range(kmax)]
    again = []
    for k in range(kmax):
        seen = jnp.bool_(False)
        for j in range(k):
            seen = jnp.logical_or(seen, codes[j] == codes[k])
        again.append(seen)
    places = []
    for k in range(kmax):
        at = codes[k] - 1
        col = pl.multiple_of(at // per_dev * blk, blk)
        row = pl.multiple_of(at % per_dev * pb, pb)
        places.append((row, col))

        @pl.when(jnp.logical_and(codes[k] > 0, jnp.logical_not(again[k])))
        def _():
            dense_ref[pl.ds(row, pb), pl.ds(col, blk)] = half_ref[0, k * pb : (k + 1) * pb, :]

    product = jnp.dot(dense_ref[...], vir_ref[...], preferred_element_type=jnp.float32)

    @pl.when(g == 0)
    def _():
        sum_ref[...] = product

    @pl.when(g > 0)
    def _():
        sum_ref[...] += product

    for k in range(kmax):
        row, col = places[k]

        @pl.when(jnp.logical_and(codes[k] > 0, again[k]))
        def _():
            sum_ref[pl.ds(row, pb), :] += jnp.dot(
                half_ref[0, k * pb : (k + 1) * pb, :],
                vir_ref[pl.ds(col, blk), :],
                preferred_element_type=jnp.float32,
            )

    @pl.when(g == pl.num_programs(0) - 1)
    def _():
        turn_ref[...] = sum_ref[...].T
        vb = own_ref.shape[0]
        mine = where_ref[0]
        own_ref[...] = turn_ref[pl.ds(pl.multiple_of(mine * vb, vb), vb), :]
        for j in range(send_ref.shape[0]):
            other = jnp.bitwise_xor(mine, j + 1)
            send_ref[j] = turn_ref[pl.ds(pl.multiple_of(other * vb, vb), vb), :].astype(jnp.bfloat16)


def pair_transform(halves, codes, vir, mine, kmax, pb, vb):
    group = halves.shape[0]
    blk = halves.shape[2]
    depth, width = vir.shape[0] // group, vir.shape[1]
    others = width // vb - 1
    return pl.pallas_call(
        functools.partial(pair_kernel, kmax, pb),
        grid_spec=pltpu.PrefetchScalarGridSpec(
            num_scalar_prefetch=2,
            grid=(group,),
            in_specs=[
                pl.BlockSpec((1, kmax * pb, blk), lambda g, *_: (g, 0, 0)),
                pl.BlockSpec((depth, width), lambda g, *_: (g, 0)),
            ],
            out_specs=[
                pl.BlockSpec((vb, PDEV), lambda g, *_: (0, 0)),
                pl.BlockSpec((others, vb, PDEV), lambda g, *_: (0, 0, 0)),
            ],
            scratch_shapes=[
                pltpu.VMEM((PDEV, depth), jnp.bfloat16),
                pltpu.VMEM((PDEV, width), jnp.float32),
                pltpu.VMEM((width, PDEV), jnp.float32),
            ],
        ),
        out_shape=[
            jax.ShapeDtypeStruct((vb, PDEV), jnp.float32),
            jax.ShapeDtypeStruct((others, vb, PDEV), jnp.bfloat16),
        ],
        compiler_params=pltpu.CompilerParams(vmem_limit_bytes=24 << 20),
        cost_estimate=pl.CostEstimate(
            flops=2 * PDEV * vir.size, bytes_accessed=vir.size * 2 + halves.size * 2, transcendentals=0
        ),
        name="pair_transform",
    )(codes, mine, halves, vir)


def place_kernel(where_ref, first_ref, second_ref, got_first_ref, got_second_ref, out_ref):
    group = pl.program_id(0)
    side = pl.program_id(1)

    @pl.when(jnp.logical_and(group == 0, side == 0))
    def _():
        out_ref[...] = first_ref[...]

    @pl.when(jnp.logical_and(group == 0, side == 1))
    def _():
        out_ref[...] = second_ref[...]

    @pl.when(jnp.logical_and(group > 0, side == 0))
    def _():
        out_ref[...] = got_first_ref[0].astype(jnp.float32)

    @pl.when(jnp.logical_and(group > 0, side == 1))
    def _():
        out_ref[...] = got_second_ref[0].astype(jnp.float32)


def place(where, first, second, got_first, got_second, aux_size):
    vb = first.shape[0]
    half = pl.BlockSpec((vb, PDEV), lambda j, s, where: (0, 0))
    got = pl.BlockSpec((1, vb, PDEV), lambda j, s, where: (jnp.maximum(j - 1, 0), 0, 0))

    def column(j, s, where):
        return 0, jnp.bitwise_xor(where[0], j) * 2 + jnp.bitwise_xor(where[1], s)

    return pl.pallas_call(
        place_kernel,
        grid_spec=pltpu.PrefetchScalarGridSpec(
            num_scalar_prefetch=1,
            grid=(aux_size // 2, 2),
            in_specs=[half, half, got, got],
            out_specs=pl.BlockSpec((vb, PDEV), column),
        ),
        out_shape=jax.ShapeDtypeStruct((vb, aux_size * PDEV), jnp.float32),
        cost_estimate=pl.CostEstimate(
            flops=0, bytes_accessed=vb * aux_size * PDEV * 8, transcendentals=0
        ),
        name="place",
    )(where, first, second, got_first, got_second)


def shards(integral_tiles, row_blocks, col_blocks, aux_blocks, tile_counts, occ_coeffs, vir_coeffs):
    group_size = lax.axis_size("grp")
    aux_size = lax.axis_size("aux")
    aux = lax.axis_index("aux")
    kmax, pb, blk = integral_tiles.shape[2:5]
    orbitals, own_ao = occ_coeffs.shape
    virtuals = vir_coeffs.shape[1]
    vb = virtuals * orbitals // (group_size * aux_size)
    count = tile_counts[0, 0]

    def swap(x, step):
        return lax.ppermute(x, "aux", [(a, a ^ step) for a in range(aux_size)])

    code = col_blocks[0, 0] * (PDEV // pb) + aux_blocks[0, 0] + 1
    code = jnp.where(jnp.arange(kmax) < count, code, 0).astype(jnp.bfloat16)
    extra = jnp.zeros((8, own_ao), jnp.bfloat16).at[0, :kmax].set(code)
    occ_ext = lax.all_gather(
        jnp.concatenate([occ_coeffs, extra], axis=0), "grp", axis=1, tiled=True
    )
    codes = occ_ext[orbitals].reshape(group_size, own_ao)[:, :kmax].astype(jnp.int32).reshape(-1)
    other_codes = swap(codes, 1)

    parity = vir_coeffs.reshape(own_ao, aux_size // 2, 2, vb)
    parity = lax.dynamic_index_in_dim(parity, aux % 2, 2, keepdims=False).reshape(own_ao, -1)
    vir = lax.all_gather(parity, "grp", axis=0, tiled=True)

    halves = half_transform(
        integral_tiles[0, 0], row_blocks[0, 0], tile_counts[0], occ_ext, orbitals
    ).reshape(orbitals, kmax * pb, blk)
    halves = lax.all_to_all(halves, "grp", split_axis=0, concat_axis=0, tiled=True)
    other_halves = swap(halves, 1)

    where = jnp.stack([aux // 2, aux % 2]).astype(jnp.int32)
    first, send_first = pair_transform(halves, codes, vir, where, kmax, pb, vb)
    second, send_second = pair_transform(other_halves, other_codes, vir, where, kmax, pb, vb)

    def trade(send):
        return jnp.stack([swap(send[j - 1], 2 * j) for j in range(1, aux_size // 2)])

    return place(where, first, second, trade(send_first), trade(send_second), aux_size)


def solution(mesh):
    in_specs = (
        P("grp", "aux", None, None, None, None),
        P("grp", "aux", None),
        P("grp", "aux", None),
        P("grp", "aux", None),
        P("grp", "aux"),
        P(None, "grp"),
        P("grp", None),
    )
    out_specs = P(("grp", "aux"), None)
    return jax.shard_map(shards, mesh=mesh, in_specs=in_specs, out_specs=out_specs, check_vma=False)
```

time: 697 us -> 119 us (0.17)
  blocking collectives: 386 us -> 34.7 us
  waiting for transfers between devices: 114 us -> 26.6 us
  local copies, waits for them, and re-layouts: 89 us -> 15.5 us
  matrix products: 32.6 us -> 0 us
  loops' own time: 30.7 us -> 0 us
  other arithmetic: 28 us -> 0.1 us
  Pallas kernels: 0 us -> 21 us
    all_to_all x1, blocking collectives: 375 us -> 24 us  [shards(): lax.all_to_all(halves, 'grp', split_axis=0, concat_axis=0, tiled=True)]
    reduce_scatter x1 -> x0, waiting for transfers between devices: 114 us -> none  [shards(): lax.psum_scatter(regrouped, 'grp', scatter_dimension=0, tiled=True)]
    reshape x2, local copies, waits for them, and re-layouts: 39.6 us -> 1.91 us  [the longest x1 1.83 us: shards(): parity = vir_coeffs.reshape(own_ao, aux_size // 2, 2, vb)]
    dot_general x24 -> x0, matrix products: 32.6 us -> none  [the longest x12 17.6 us: tile_term(): jnp.einsum('im,pmn->ipn', occ_block, tile, preferred_element_type=jnp.flo...]
    another operation x1 -> x0, loops' own time: 30.7 us -> none  [shards(): partial_value = lax.fori_loop(0, KMAX, padded_step, partial_value)]
    dynamic_update_slice x12 -> x0, other arithmetic: 28 us -> none  [add_tile(): lax.dynamic_update_slice_in_dim(partial_value, current + weight * term, s...]
    ppermute x0 -> x4, waiting for transfers between devices: none -> 26.6 us  [swap(): return lax.ppermute(x, 'aux', [(a, a ^ step) for a in range(aux_size)])]
    pallas_call x0 -> x4, Pallas kernels: none -> 21 us  [the longest x2 15.2 us: pair_transform(): pl.pallas_call(functools.partial(pair_kernel, kmax, pb), grid_spec=pltpu....]
  transfers between devices with their start and end apart: 1 -> 5, of which waited for: 1 -> 3; matrix products, arithmetic and copies ran while one was open for 0% -> 0% of each run, Pallas kernels for 0% -> 8%
where the time goes in v1:
time: 119 us
  blocking collectives  34.7 us (29%)
  waiting for transfers between devices  26.6 us (22%)
  Pallas kernels  21 us (18%)
  local copies, waits for them, and re-layouts  15.5 us (13%)
  between operations  14.2 us (12%)
  starting transfers between devices  6.84 us (6%)
    ppermute x4, waiting for transfers between devices, swap(): return lax.ppermute(x, 'aux', [(a, a ^ step) for a in range(aux_size)])  26.6 us
    all_to_all x1, blocking collectives, shards(): lax.all_to_all(halves, 'grp', split_axis=0, concat_axis=0, tiled=True)  24 us
    pallas_call x2, Pallas kernels, pair_transform(): pl.pallas_call(functools.partial(pair_kernel, kmax, pb), grid_spec=pltpu....  15.2 us
    all_gather x1, blocking collectives, shards(): lax.all_gather(jnp.concatenate([occ_coeffs, extra], axis=0), 'grp', axis=...  10.7 us
    unnamed x23, local copies, waits for them, and re-layouts  9.97 us
    ppermute x4, starting transfers between devices, swap(): return lax.ppermute(x, 'aux', [(a, a ^ step) for a in range(aux_size)])  6.81 us
    pallas_call x1, Pallas kernels, place(): pl.pallas_call(place_kernel, grid_spec=pltpu.PrefetchScalarGridSpec(num_s...  3.92 us
    dynamic_slice x1, local copies, waits for them, and re-layouts, shards(): lax.dynamic_index_in_dim(parity, aux % 2, 2, keepdims=False)  3.58 us
  transfers between devices with their start and end apart: 5, of which 3 were waited for; matrix products, arithmetic and copies ran while one was open for 0% of the time, Pallas kernels for 8%

profile of v1, /device:TPU:0, one launch (start us, length us, event | category | flops | bytes accessed | tf_op | source)
XLA Modules:
  0.0 119.0 jit_solution(12956346952901104425)
XLA Ops:
  6.5 0.0 copy-start.9
  6.5 0.0 copy-start.10
  6.5 0.0 copy-start.8
  6.5 0.0 copy-start.3
  6.5 0.0 all-gather.2.cloned.1.call-start
  6.6 1.8 %reshape.76 = bf16[512,2,2,256]{3,2,1,0:T(2,128)(2,1)S(1)} reshape(bf16[512,1024]{1,0:T(8,128)(2,1)} %param.15) | data formatting | bytes 2097152 | tf_op jit(solution)/shard_map/reshape | solution.py:220
  8.4 3.6 %dynamic-slice_reduce_fusion = bf16[512,2,256]{2,1,0:T(2,128)(2,1)S(1)} fusion(bf16[512,2,2,256]{3,2,1,0:T(2,128)(2,1)S(1)} %reshape.76, s32[]{:T(128)S(6)} %select_n.29), kind=kLoop, calls=%fused_computation | loop fusion | bytes 1048580 | tf_op jit(solution)/shard_map/jit(dynamic_index_in_dim)/dynamic_slice | solution.py:221
  12.0 0.9 copy.10
  12.9 0.0 all-gather.2.cloned.1.call-update
  13.6 0.0 copy-done.9
  13.6 0.0 copy-done.10
  13.6 0.0 copy-done.8
  13.6 10.7 %all_gather.6.occ_ref = bf16[16,4096]{1,0:T(8,128)(2,1)S(1)} all-gather(bf16[16,512]{1,0:T(8,128)(2,1)S(1)} %fusion.1), channel_id=1, replica_groups=mesh['grp'=8,'aux'=4] {'grp'}, dimensions={1}, use_global_device_ids=true | all-gather | bytes 147456 | tf_op jit(solution)/shard_map/all_gather | solution.py:214
  24.3 0.0 copy-done.3
  24.4 0.0 copy-start
  24.4 4.6 %copy-done = bf16[1,1,12,32,128,128]{5,4,3,2,1,0:T(8,128)(2,1)S(1)} copy-done((bf16[1,1,12,32,128,128]{5,4,3,2,1,0:T(8,128)(2,1)S(1)}, bf16[1,1,12,32,128,128]{5,4,3,2,1,0:T(8,128)(2,1)}, u32[]{:S(2)}) %copy-start) | copy-done | bytes 12582936
  28.9 1.9 %half_transform.1 = bf16[8,12,32,128]{3,2,1,0:T(8,128)(2,1)S(1)} custom-call(s32[12]{0:T(128)S(1)} %bitcast.19, s32[1]{0:T(128)} %bitcast.16.count_ref, bf16[16,4096]{1,0:T(8,128)(2,1)S(1)} %all_gather.6.occ_ref, bf16[12,32,128,128]{3,2,1,0:T(8,128)(2,1)S(1)} %bitcast.17), custom_call_target="tpu_custom_call" | custom-call | flops 201326592 | bytes 12582912 | tf_op jit(solution)/shard_map/half_transform/pallas_call | solution.py:39
  30.8 24.0 %all_to_all.5.half_ref = bf16[8,384,128]{2,1,0:T(8,128)(2,1)S(1)} all-to-all(bf16[8,384,128]{2,1,0:T(8,128)(2,1)S(1)} %bitcast.18), channel_id=1, replica_groups=mesh['grp'=8,'aux'=4] {'grp'}, dimensions={0} | all-to-all | bytes 1572864 | tf_op jit(solution)/shard_map/all_to_all | solution.py:227
  54.8 3.5 %collective-permute-start.1 = (bf16[8,384,128]{2,1,0:T(8,128)(2,1)S(1)}, bf16[8,384,128]{2,1,0:T(8,128)(2,1)S(1)}, u32[]{:S(2)}, u32[]{:S(2)}) collective-permute-start(bf16[8,384,128]{2,1,0:T(8,128)(2,1)S(1)} %all_to_all.5.half_ref), channel_id=1, source_target_pairs={{0,1},{1,0},{2,3},{3,2},{4,5},{5,4},{6,7},{7,6},{8,9},{9,8},{10,11... | collective-permute-start | bytes 2359304 | tf_op jit(solution)/shard_map/ppermute | solution.py:209
  58.3 0.1 slice_reduce_fusion
  58.4 0.1 reshape.79.code_ref
  58.4 0.0 collective-permute-start
  58.5 0.1 pad_add_fusion.where_ref
  58.5 0.0 copy-start.4
  58.6 15.3 %collective-permute-done.code_ref = s32[96]{0:T(128)S(1)} collective-permute-done((s32[96]{0:T(128)S(1)}, s32[96]{0:T(128)S(1)}, u32[]{:S(2)}, u32[]{:S(2)}) %collective-permute-start) | collective-permute-done | bytes 416 | tf_op jit(solution)/shard_map/ppermute | solution.py:209
  73.8 0.0 collective-permute-done.1.half_ref
  73.8 0.0 all-gather.2.cloned.1.call-done.vir_ref
  73.8 0.0 copy-start.5
  73.8 2.2 %copy-done.5 = bf16[4096,512]{1,0:T(8,128)(2,1)S(1)} copy-done((bf16[4096,512]{1,0:T(8,128)(2,1)S(1)}, bf16[4096,512]{1,0:T(8,128)(2,1)}, u32[]{:S(2)}) %copy-start.5) | copy-done | bytes 4194328
  76.0 7.7 %pair_transform.3 = (f32[256,512]{1,0:T(8,128)S(1)}, bf16[1,256,512]{2,1,0:T(8,128)(2,1)S(1)}) custom-call(s32[96]{0:T(128)S(1)} %collective-permute-done.code_ref, s32[2]{0:T(128)S(1)} %pad_add_fusion.where_ref, bf16[8,384,128]{2,1,0:T(8,128)(2,1)S(1)} %collective-permute-done.1.half_ref, bf16[4096,512]{1,0:T(8,128)(2,1)S(1)} %copy-done.5), custom_call_target="tpu_custom_call" | custom-call | flops 2147483648 | bytes 4980736 | tf_op jit(solution)/shard_map/pair_transform/pallas_call | solution.py:122
  83.7 0.0 copy-start.1
  83.7 0.8 copy-done.1
  84.5 2.5 %collective-permute-start.3 = (bf16[256,512]{1,0:T(8,128)(2,1)S(1)}, bf16[256,512]{1,0:T(8,128)(2,1)S(1)}, u32[]{:S(2)}, u32[]{:S(2)}) collective-permute-start(bf16[256,512]{1,0:T(8,128)(2,1)S(1)} %bitcast.20), channel_id=1, source_target_pairs={{0,2},{1,3},{2,0},{3,1},{4,6},{5,7},{6,4},{7,5},{8,10},{9,11},{10,... | collective-permute-start | bytes 786440 | tf_op jit(solution)/shard_map/ppermute | solution.py:209
  87.0 7.5 %pair_transform.2 = (f32[256,512]{1,0:T(8,128)S(1)}, bf16[1,256,512]{2,1,0:T(8,128)(2,1)S(1)}) custom-call(s32[96]{0:T(128)S(1)} %reshape.79.code_ref, s32[2]{0:T(128)S(1)} %pad_add_fusion.where_ref, bf16[8,384,128]{2,1,0:T(8,128)(2,1)S(1)} %all_to_all.5.half_ref, bf16[4096,512]{1,0:T(8,128)(2,1)S(1)} %copy-done.5), custom_call_target="tpu_custom_call" | custom-call | flops 2147483648 | bytes 4980736 | tf_op jit(solution)/shard_map/pair_transform/pallas_call | solution.py:122
  94.5 0.0 copy-done.4
  94.5 0.0 copy-start.2
  94.5 0.8 copy-done.2
  95.3 0.8 collective-permute-start.2
  96.1 3.6 %collective-permute-done.3 = bf16[256,512]{1,0:T(8,128)(2,1)S(1)} collective-permute-done((bf16[256,512]{1,0:T(8,128)(2,1)S(1)}, bf16[256,512]{1,0:T(8,128)(2,1)S(1)}, u32[]{:S(2)}, u32[]{:S(2)}) %collective-permute-start.3) | collective-permute-done | bytes 262176 | tf_op jit(solution)/shard_map/ppermute | solution.py:209
  99.7 0.0 copy-start.6
  99.7 7.8 %collective-permute-done.2 = bf16[256,512]{1,0:T(8,128)(2,1)S(1)} collective-permute-done((bf16[256,512]{1,0:T(8,128)(2,1)S(1)}, bf16[256,512]{1,0:T(8,128)(2,1)S(1)}, u32[]{:S(2)}, u32[]{:S(2)}) %collective-permute-start.2) | collective-permute-done | bytes 262176 | tf_op jit(solution)/shard_map/ppermute | solution.py:209
  107.5 0.0 copy-start.7
  107.5 0.0 copy-done.6
  107.5 0.7 copy-done.7
  108.2 3.9 %place.1 = f32[256,2048]{1,0:T(8,128)} custom-call(s32[2]{0:T(128)} %copy-done.4, f32[256,512]{1,0:T(8,128)} %copy-done.2, f32[256,512]{1,0:T(8,128)} %copy-done.1, bf16[1,256,512]{2,1,0:T(8,128)(2,1)} %bitcast.25, bf16[1,256,512]{2,1,0:T(8,128)(2,1)} %bitcast.24), custom_call_target="tpu_custom_call" | custom-call | bytes 4194304 | tf_op jit(solution)/shard_map/place/pallas_call | solution.py:182
  (4 shorter events, 0.0 us)
Async XLA Ops:
  6.5 7.1 %copy-start.9 = (s32[1,1,12]{2,1,0:T(1,128)S(1)}, s32[1,1,12]{2,1,0:T(1,128)}, u32[]{:S(2)}) copy-start(s32[1,1,12]{2,1,0:T(1,128)} %param.12) | copy-start | bytes 148
  6.5 7.1 %copy-start.10 = (s32[1,1,12]{2,1,0:T(1,128)S(1)}, s32[1,1,12]{2,1,0:T(1,128)}, u32[]{:S(2)}) copy-start(s32[1,1,12]{2,1,0:T(1,128)} %param.11) | copy-start | bytes 148
  6.5 7.1 %copy-start.8 = (bf16[8,512]{1,0:T(8,128)(2,1)S(1)}, bf16[8,512]{1,0:T(8,128)(2,1)}, u32[]{:S(2)}) copy-start(bf16[8,512]{1,0:T(8,128)(2,1)} %param.14) | copy-start | bytes 24580
  6.5 17.8 %copy-start.3 = (s32[1,1,12]{2,1,0:T(1,128)S(1)}, s32[1,1,12]{2,1,0:T(1,128)}, u32[]{:S(2)}) copy-start(s32[1,1,12]{2,1,0:T(1,128)} %param.10) | copy-start | bytes 148
  6.5 67.3 %all-gather.2.cloned.1.call-start = ((), (), s32[]{:S(2)}) async-start(), calls=%async_computation.1 | async-start | bytes 4718592 | tf_op jit(solution)/shard_map/all_gather | solution.py:222
  24.4 4.6 %copy-start = (bf16[1,1,12,32,128,128]{5,4,3,2,1,0:T(8,128)(2,1)S(1)}, bf16[1,1,12,32,128,128]{5,4,3,2,1,0:T(8,128)(2,1)}, u32[]{:S(2)}) copy-start(bf16[1,1,12,32,128,128]{5,4,3,2,1,0:T(8,128)(2,1)} %param.9) | copy-start | bytes 37748740
  54.8 19.0 %collective-permute-start.1 = (bf16[8,384,128]{2,1,0:T(8,128)(2,1)S(1)}, bf16[8,384,128]{2,1,0:T(8,128)(2,1)S(1)}, u32[]{:S(2)}, u32[]{:S(2)}) collective-permute-start(bf16[8,384,128]{2,1,0:T(8,128)(2,1)S(1)} %all_to_all.5.half_ref), channel_id=1, source_target_pairs={{0,1},{1,0},{2,3},{3,2},{4,5},{5,4},{6,7},{7,6},{8,9},{9,8},{10,11... | collective-permute-start | bytes 2359304 | tf_op jit(solution)/shard_map/ppermute | solution.py:209
  58.4 15.4 %collective-permute-start = (s32[96]{0:T(128)S(1)}, s32[96]{0:T(128)S(1)}, u32[]{:S(2)}, u32[]{:S(2)}) collective-permute-start(s32[96]{0:T(128)S(1)} %reshape.79.code_ref), channel_id=1, source_target_pairs={{0,1},{1,0},{2,3},{3,2},{4,5},{5,4},{6,7},{7,6},{8,9},{9,8},{10,11... | collective-permute-start | bytes 1160 | tf_op jit(solution)/shard_map/ppermute | solution.py:209
  58.5 36.0 %copy-start.4 = (s32[2]{0:T(128)}, s32[2]{0:T(128)S(1)}, u32[]{:S(2)}) copy-start(s32[2]{0:T(128)S(1)} %pad_add_fusion.where_ref) | copy-start | bytes 28
  73.8 2.2 %copy-start.5 = (bf16[4096,512]{1,0:T(8,128)(2,1)S(1)}, bf16[4096,512]{1,0:T(8,128)(2,1)}, u32[]{:S(2)}) copy-start(bf16[4096,512]{1,0:T(8,128)(2,1)} %all-gather.2.cloned.1.call-done.vir_ref) | copy-start | bytes 12582916
  83.7 0.8 copy-start.1
  84.5 15.3 %collective-permute-start.3 = (bf16[256,512]{1,0:T(8,128)(2,1)S(1)}, bf16[256,512]{1,0:T(8,128)(2,1)S(1)}, u32[]{:S(2)}, u32[]{:S(2)}) collective-permute-start(bf16[256,512]{1,0:T(8,128)(2,1)S(1)} %bitcast.20), channel_id=1, source_target_pairs={{0,2},{1,3},{2,0},{3,1},{4,6},{5,7},{6,4},{7,5},{8,10},{9,11},{10,... | collective-permute-start | bytes 786440 | tf_op jit(solution)/shard_map/ppermute | solution.py:209
  94.5 0.8 copy-start.2
  95.3 12.2 %collective-permute-start.2 = (bf16[256,512]{1,0:T(8,128)(2,1)S(1)}, bf16[256,512]{1,0:T(8,128)(2,1)S(1)}, u32[]{:S(2)}, u32[]{:S(2)}) collective-permute-start(bf16[256,512]{1,0:T(8,128)(2,1)S(1)} %bitcast.21), channel_id=1, source_target_pairs={{0,2},{1,3},{2,0},{3,1},{4,6},{5,7},{6,4},{7,5},{8,10},{9,11},{10,... | collective-permute-start | bytes 786440 | tf_op jit(solution)/shard_map/ppermute | solution.py:209
  99.7 7.8 %copy-start.6 = (bf16[256,512]{1,0:T(8,128)(2,1)}, bf16[256,512]{1,0:T(8,128)(2,1)S(1)}, u32[]{:S(2)}) copy-start(bf16[256,512]{1,0:T(8,128)(2,1)S(1)} %collective-permute-done.3) | copy-start | bytes 786436
  107.5 0.7 copy-start.7
Sparse Core Ops, SparseCore 0:
  13.1 46.3 all-gather.1

commit v2 on v0

v2 whole, which is shorter than its diff:
```python
import functools

import jax
import jax.numpy as jnp
from jax import lax
from jax.experimental import pallas as pl
from jax.experimental.pallas import tpu as pltpu
from jax.sharding import PartitionSpec as P

PDEV = 512
META = 16
FIELD = 16


def whole(shape):
    return pl.BlockSpec(shape, lambda n, *_: (0,) * len(shape))


def half_kernel(index_ref, occ_ref, tiles_hbm, half_ref, tile_ref, stage_ref, sems):
    kmax, pb, blk, _ = tile_ref.shape
    rows_ref, cols_ref, aux_ref = (index_ref.at[pl.ds(n * kmax, kmax)] for n in range(3))
    orbitals = half_ref.shape[0]
    ao_blocks = occ_ref.shape[2] // blk
    count = index_ref[3 * kmax]

    def fetch(k):
        return pltpu.make_async_copy(tiles_hbm.at[k], tile_ref.at[k], sems.at[k])

    for k in range(kmax):

        @pl.when(k < count)
        def _():
            fetch(k).start()

    lanes = lax.broadcasted_iota(jnp.int32, (META, blk), 1)
    meta = jnp.zeros((META, blk), jnp.int32)
    for k in range(kmax):
        again = jnp.bool_(False)
        for j in range(k):
            same = jnp.logical_and(cols_ref[j] == cols_ref[k], aux_ref[j] == aux_ref[k])
            again = jnp.logical_or(again, same)
        again = jnp.logical_and(again, k < count)
        row = aux_ref[k] * pb
        first = jnp.where(jnp.logical_or(again, k >= count), PDEV, row)
        for n, value in enumerate((first, cols_ref[k] * blk, again.astype(jnp.int32), row)):
            meta = jnp.where(lanes == n * FIELD + k, value, meta)
    meta = meta.astype(jnp.float32).astype(jnp.bfloat16)
    for i in range(orbitals):
        half_ref[i, kmax * pb :, :] = meta

    for k in range(kmax):

        @pl.when(k < count)
        def _():
            row = rows_ref[k]
            lane = pl.multiple_of(row % ao_blocks * blk, blk)
            occ = occ_ref[row // ao_blocks, :, pl.ds(lane, blk)].astype(jnp.float32)
            zero = jnp.zeros_like(occ)
            upper = jnp.concatenate([occ, zero], axis=1)
            lower = jnp.concatenate([zero, occ], axis=1)
            pair = jnp.concatenate([upper, lower], axis=0).astype(jnp.bfloat16)
            stage = stage_ref.at[k % 2]
            fetch(k).wait()
            for p in range(0, pb, 2):
                rhs = tile_ref[k, p : p + 2].reshape(2 * blk, blk)
                stage[p * orbitals : (p + 2) * orbitals, :] = jnp.dot(
                    pair, rhs, preferred_element_type=jnp.float32
                )
            for i in range(orbitals):
                half_ref[i, k * pb : (k + 1) * pb, :] = stage[
                    pl.ds(i, pb, stride=orbitals), :
                ].astype(jnp.bfloat16)

        @pl.when(k >= count)
        def _():
            half_ref[:, k * pb : (k + 1) * pb, :] = jnp.zeros((orbitals, pb, blk), jnp.bfloat16)


def half_transform(tiles, index, occ):
    kmax, pb, blk, _ = tiles.shape
    orbitals = occ.shape[1]
    out = (orbitals, kmax * pb + META, blk)
    return pl.pallas_call(
        half_kernel,
        grid_spec=pltpu.PrefetchScalarGridSpec(
            num_scalar_prefetch=1,
            grid=(1,),
            in_specs=[whole(occ.shape), pl.BlockSpec(memory_space=pl.ANY)],
            out_specs=whole(out),
            scratch_shapes=[
                pltpu.VMEM(tiles.shape, jnp.bfloat16),
                pltpu.VMEM((2, pb * orbitals, blk), jnp.float32),
                pltpu.SemaphoreType.DMA((kmax,)),
            ],
        ),
        out_shape=jax.ShapeDtypeStruct(out, jnp.bfloat16),
        compiler_params=pltpu.CompilerParams(vmem_limit_bytes=56 << 20),
        cost_estimate=pl.CostEstimate(
            flops=4 * tiles.size * orbitals, bytes_accessed=tiles.size * 2, transcendentals=0
        ),
        name="half_transform",
    )(index, occ, tiles)


def pair_kernel(kmax, pb, group, where_ref, half_ref, *refs):
    vir_refs, refs = refs[:group], refs[group:]
    own_ref, send_ref, dense_ref, sum_ref, turn_ref, meta_ref, code_ref, again_ref, sem = refs
    depth = vir_refs[0].shape[0]
    blk = half_ref.shape[2]
    for g in range(group):
        meta_ref[g : g + 1, :] = half_ref[g, kmax * pb :, :].astype(jnp.float32)[:1].astype(jnp.int32)
    copy = pltpu.make_async_copy(meta_ref, code_ref, sem)
    copy.start()
    dense_ref[:PDEV, :] = jnp.zeros((PDEV, group * depth), jnp.bfloat16)
    copy.wait()

    def scatter(step, repeats):
        g = where_ref[2 + step]
        for k in range(kmax):
            row = pl.multiple_of(code_ref[g, k], pb)
            lane = pl.multiple_of(step * depth + code_ref[g, FIELD + k], blk)
            dense_ref[pl.ds(row, pb), pl.ds(lane, blk)] = half_ref[g, k * pb : (k + 1) * pb, :]
            again_ref[repeats] = step * kmax + k
            repeats = repeats + code_ref[g, 2 * FIELD + k]
        return repeats

    repeats = lax.fori_loop(0, group, scatter, jnp.int32(0))
    vir = jnp.concatenate([ref[...] for ref in vir_refs], axis=0)
    sum_ref[...] = jnp.dot(dense_ref[:PDEV, :], vir, preferred_element_type=jnp.float32)

    def repeat(n, carry):
        slot = again_ref[n]
        step, k = slot // kmax, slot % kmax
        g = where_ref[2 + step]
        row = pl.multiple_of(code_ref[g, 3 * FIELD + k], pb)
        lane = pl.multiple_of(code_ref[g, FIELD + k], blk)
        tile = half_ref[g, pl.ds(pl.multiple_of(k * pb, pb), pb), :]
        for d in range(group):

            @pl.when(step == d)
            def _():
                sum_ref[pl.ds(row, pb), :] += jnp.dot(
                    tile, vir_refs[d][pl.ds(lane, blk), :], preferred_element_type=jnp.float32
                )

        return carry

    lax.fori_loop(0, repeats, repeat, 0)
    turn_ref[...] = sum_ref[...].T
    vb = own_ref.shape[0]
    mine = where_ref[0]
    own_ref[...] = turn_ref[pl.ds(pl.multiple_of(mine * vb, vb), vb), :]
    for j in range(send_ref.shape[0]):
        other = jnp.bitwise_xor(mine, j + 1)
        send_ref[j] = turn_ref[pl.ds(pl.multiple_of(other * vb, vb), vb), :].astype(jnp.bfloat16)


def pair_transform(halves, virs, where, kmax, pb, vb):
    group, _, blk = halves.shape
    depth, width = virs[0].shape
    others = width // vb - 1
    return pl.pallas_call(
        functools.partial(pair_kernel, kmax, pb, group),
        grid_spec=pltpu.PrefetchScalarGridSpec(
            num_scalar_prefetch=1,
            grid=(1,),
            in_specs=[whole(halves.shape)] + [whole((depth, width))] * group,
            out_specs=[whole((vb, PDEV)), whole((others, vb, PDEV))],
            scratch_shapes=[
                pltpu.VMEM((PDEV + pb, group * depth), jnp.bfloat16),
                pltpu.VMEM((PDEV, width), jnp.float32),
                pltpu.VMEM((width, PDEV), jnp.float32),
                pltpu.VMEM((group, blk), jnp.int32),
                pltpu.SMEM((group, blk), jnp.int32),
                pltpu.SMEM((group * kmax + 1,), jnp.int32),
                pltpu.SemaphoreType.DMA,
            ],
        ),
        out_shape=[
            jax.ShapeDtypeStruct((vb, PDEV), jnp.float32),
            jax.ShapeDtypeStruct((others, vb, PDEV), jnp.bfloat16),
        ],
        compiler_params=pltpu.CompilerParams(vmem_limit_bytes=28 << 20),
        cost_estimate=pl.CostEstimate(
            flops=4 * PDEV * group * depth * width,
            bytes_accessed=group * depth * width * 2 + halves.size * 2,
            transcendentals=0,
        ),
        name="pair_transform",
    )(where, halves, *virs)


def place_kernel(where_ref, first_ref, second_ref, got_first_ref, got_second_ref, out_hbm, wide_ref, sems):
    pairs = out_hbm.shape[1] // (2 * PDEV)
    copies = []
    for j in range(pairs):
        for s in range(2):
            if j == 0:
                src = (first_ref, second_ref)[s]
            else:
                n = 2 * (j - 1) + s
                wide_ref[n] = (got_first_ref, got_second_ref)[s][j - 1].astype(jnp.float32)
                src = wide_ref.at[n]
            block = jnp.bitwise_xor(where_ref[0], j) * 2 + jnp.bitwise_xor(where_ref[1], s)
            lane = pl.multiple_of(block * PDEV, PDEV)
            copies.append(
                pltpu.make_async_copy(src, out_hbm.at[:, pl.ds(lane, PDEV)], sems.at[2 * j + s])
            )
            copies[-1].start()
    for copy in copies:
        copy.wait()


def place(where, first, second, got_first, got_second, aux_size):
    vb = first.shape[0]
    return pl.pallas_call(
        place_kernel,
        grid_spec=pltpu.PrefetchScalarGridSpec(
            num_scalar_prefetch=1,
            grid=(1,),
            in_specs=[whole(x.shape) for x in (first, second, got_first, got_second)],
            out_specs=pl.BlockSpec(memory_space=pl.ANY),
            scratch_shapes=[
                pltpu.VMEM((aux_size - 2, vb, PDEV), jnp.float32),
                pltpu.SemaphoreType.DMA((aux_size,)),
            ],
        ),
        out_shape=jax.ShapeDtypeStruct((vb, aux_size * PDEV), jnp.float32),
        cost_estimate=pl.CostEstimate(
            flops=0, bytes_accessed=vb * aux_size * PDEV * 8, transcendentals=0
        ),
        name="place",
    )(where, first, second, got_first, got_second)


def copy_kernel(where_ref, in_ref, out_ref):
    out_ref[...] = in_ref[...]


def vir_columns(vir, aux, aux_size, vb):
    rows = vir.shape[0]
    if vb % 128:
        chosen = vir.reshape(rows, aux_size // 2, 2, vb)
        return lax.dynamic_index_in_dim(chosen, aux % 2, 2, keepdims=False).reshape(rows, -1)
    return pl.pallas_call(
        copy_kernel,
        grid_spec=pltpu.PrefetchScalarGridSpec(
            num_scalar_prefetch=1,
            grid=(aux_size // 2,),
            in_specs=[pl.BlockSpec((rows, vb), lambda j, where: (0, 2 * j + where[0]))],
            out_specs=pl.BlockSpec((rows, vb), lambda j, where: (0, j)),
        ),
        out_shape=jax.ShapeDtypeStruct((rows, aux_size // 2 * vb), vir.dtype),
        name="vir_columns",
    )((aux % 2).astype(jnp.int32)[None], vir)


def shards(integral_tiles, row_blocks, col_blocks, aux_blocks, tile_counts, occ_coeffs, vir_coeffs):
    group_size = lax.axis_size("grp")
    aux_size = lax.axis_size("aux")
    aux = lax.axis_index("aux")
    kmax, pb = integral_tiles.shape[2:4]
    orbitals = occ_coeffs.shape[0]
    virtuals = vir_coeffs.shape[1]
    vb = virtuals * orbitals // (group_size * aux_size)

    def swap(x, step):
        return lax.ppermute(x, "aux", [(a, a ^ step) for a in range(aux_size)])

    def hop(x, steps):
        return lax.ppermute(x, "grp", [(g, g ^ steps[g % 2]) for g in range(group_size)])

    occ = jnp.broadcast_to(occ_coeffs[None], (group_size, *occ_coeffs.shape))
    occ = lax.all_to_all(occ, "grp", split_axis=0, concat_axis=0, tiled=True)

    core = lax.axis_index("grp") % 2
    own = vir_columns(vir_coeffs, aux, aux_size, vb)
    near = hop(own, (2, 4))
    far = hop(own, (4, 2))
    occ, near, far = lax.optimization_barrier((occ, near, far))
    across = hop(near, (4, 2))
    virs = [own, near, far, across]
    virs = virs + [hop(vir, (1, 1)) for vir in virs]

    index = [x[0, 0] for x in (row_blocks, col_blocks, aux_blocks)] + [tile_counts[0]]
    halves = half_transform(integral_tiles[0, 0], jnp.concatenate(index), occ)
    halves = lax.all_to_all(halves, "grp", split_axis=0, concat_axis=0, tiled=True)
    other_halves = swap(halves, 1)

    moved = [0, 2 + 2 * core, 4 - 2 * core, 6, 1, 5 - 2 * core, 3 + 2 * core, 7]
    moved = [jnp.bitwise_xor(lax.axis_index("grp"), step) for step in moved]
    where = jnp.stack([aux // 2, aux % 2] + moved).astype(jnp.int32)
    first, send_first = pair_transform(halves, virs, where, kmax, pb, vb)
    other_halves, _ = lax.optimization_barrier((other_halves, send_first))
    second, send_second = pair_transform(other_halves, virs, where, kmax, pb, vb)

    def trade(send):
        if aux_size == 4:
            return swap(send, 2)
        return jnp.stack([swap(send[j - 1], 2 * j) for j in range(1, aux_size // 2)])

    return place(where, first, second, trade(send_first), trade(send_second), aux_size)


def solution(mesh):
    in_specs = (
        P("grp", "aux", None, None, None, None),
        P("grp", "aux", None),
        P("grp", "aux", None),
        P("grp", "aux", None),
        P("grp", "aux"),
        P(None, "grp"),
        P("grp", None),
    )
    out_specs = P(("grp", "aux"), None)
    return jax.shard_map(shards, mesh=mesh, in_specs=in_specs, out_specs=out_specs, check_vma=False)
```

time: 697 us -> 101 us (0.14)
  blocking collectives: 386 us -> 0 us
  local copies, waits for them, and re-layouts: 89 us -> 4.34 us
  waiting for transfers between devices: 114 us -> 49.6 us
  matrix products: 32.6 us -> 0 us
  loops' own time: 30.7 us -> 0 us
  other arithmetic: 28 us -> 1.28 us
  Pallas kernels: 0 us -> 25.8 us
  starting transfers between devices: 0.01 us -> 18.3 us
  between operations: 13.4 us -> 0.76 us
    all_to_all x1 -> x0, blocking collectives: 375 us -> none  [shards(): lax.all_to_all(reordered, 'aux', split_axis=0, concat_axis=1, tiled=True)]
    reduce_scatter x1 -> x0, waiting for transfers between devices: 114 us -> none  [shards(): lax.psum_scatter(regrouped, 'grp', scatter_dimension=0, tiled=True)]
    ppermute x0 -> x10, waiting for transfers between devices: none -> 43.7 us  [the longest x3 27.3 us: swap(): return lax.ppermute(x, 'aux', [(a, a ^ step) for a in range(aux_size)])]
    reshape x2 -> x0, local copies, waits for them, and re-layouts: 39.6 us -> none  [shards(): partial_value.reshape(group_size, aux_size, share, PDEV)]
    dot_general x24 -> x0, matrix products: 32.6 us -> none  [the longest x12 17.6 us: tile_term(): jnp.einsum('im,pmn->ipn', occ_block, tile, preferred_element_type=jnp.flo...]
    another operation x1 -> x0, loops' own time: 30.7 us -> none  [shards(): partial_value = lax.fori_loop(0, KMAX, padded_step, partial_value)]
    dynamic_update_slice x12 -> x0, other arithmetic: 28 us -> none  [add_tile(): lax.dynamic_update_slice_in_dim(partial_value, current + weight * term, s...]
    pallas_call x0 -> x5, Pallas kernels: none -> 25.8 us  [the longest x2 13.3 us: pair_transform(): pl.pallas_call(functools.partial(pair_kernel, kmax, pb, group), grid_spec...]
  transfers between devices with their start and end apart: 1 -> 12, of which waited for: 1 -> 5; matrix products, arithmetic and copies ran while one was open for 0% -> 3% of each run, Pallas kernels for 0% -> 13%
where the time goes in v2:
time: 101 us; the launch traced here: 100 us
  waiting for transfers between devices  49.6 us (49%)
  Pallas kernels  25.8 us (26%)
  starting transfers between devices  18.3 us (18%)
  local copies, waits for them, and re-layouts  4.34 us (4%)
  other arithmetic  1.28 us (1%)
    ppermute x3, waiting for transfers between devices, swap(): return lax.ppermute(x, 'aux', [(a, a ^ step) for a in range(aux_size)])  27.3 us
    ppermute x7, waiting for transfers between devices, hop(): lax.ppermute(x, 'grp', [(g, g ^ steps[g % 2]) for g in range(group_size)])  16.5 us
    pallas_call x2, Pallas kernels, pair_transform(): pl.pallas_call(functools.partial(pair_kernel, kmax, pb, group), grid_spec...  13.3 us
    pallas_call x1, Pallas kernels, half_transform(): pl.pallas_call(half_kernel, grid_spec=pltpu.PrefetchScalarGridSpec(num_sc...  7.38 us
    ppermute x7, starting transfers between devices, hop(): lax.ppermute(x, 'grp', [(g, g ^ steps[g % 2]) for g in range(group_size)])  7.03 us
    all_to_all x1, waiting for transfers between devices, shards(): occ = lax.all_to_all(occ, 'grp', split_axis=0, concat_axis=0, tiled=True)  5.91 us
    ppermute x3, starting transfers between devices, swap(): return lax.ppermute(x, 'aux', [(a, a ^ step) for a in range(aux_size)])  4.35 us
    all_to_all x1, starting transfers between devices, shards(): lax.all_to_all(halves, 'grp', split_axis=0, concat_axis=0, tiled=True)  3.56 us
  transfers between devices with their start and end apart: 12, of which 5 were waited for; matrix products, arithmetic and copies ran while one was open for 3% of the time, Pallas kernels for 13%

profile of v2, /device:TPU:0, one launch (start us, length us, event | category | flops | bytes accessed | tf_op | source)
XLA Modules:
  0.0 100.1 jit_solution(4272433395819553204)
XLA Ops:
  0.0 1.8 %vir_columns.1.refs_0_ = bf16[512,512]{1,0:T(8,128)(2,1)} custom-call(s32[1]{0:T(128)} %bitcast.1.where_ref, bf16[512,1024]{1,0:T(8,128)(2,1)} %in_ref.1), custom_call_target="tpu_custom_call" | custom-call | tf_op jit(solution)/shard_map/vir_columns/pallas_call | solution.py:245
  1.8 0.0 copy-start
  1.8 2.9 %collective-permute-start = (bf16[512,512]{1,0:T(8,128)(2,1)}, bf16[512,512]{1,0:T(8,128)(2,1)S(1)}, u32[]{:S(2)}, u32[]{:S(2)}) collective-permute-start(bf16[512,512]{1,0:T(8,128)(2,1)} %vir_columns.1.refs_0_), channel_id=1, source_target_pairs={{0,8},{4,20},{8,0},{12,28},{16,24},{20,4},{24,16},{28,12},{1,9},{5... | collective-permute-start | bytes 1572872 | tf_op jit(solution)/shard_map/ppermute | solution.py:271
  4.7 1.5 %collective-permute-start.1 = (bf16[512,512]{1,0:T(8,128)(2,1)}, bf16[512,512]{1,0:T(8,128)(2,1)S(1)}, u32[]{:S(2)}, u32[]{:S(2)}) collective-permute-start(bf16[512,512]{1,0:T(8,128)(2,1)} %vir_columns.1.refs_0_), channel_id=1, source_target_pairs={{0,16},{4,12},{8,24},{12,4},{16,0},{20,28},{24,8},{28,20},{1,17},{... | collective-permute-start | bytes 1572872 | tf_op jit(solution)/shard_map/ppermute | solution.py:271
  6.2 1.3 %broadcast_in_dim.2 = bf16[8,8,512]{2,1,0:T(8,128)(2,1)} broadcast(bf16[8,512]{1,0:T(8,128)(2,1)} %param.12), dimensions={1,2} | broadcast | bytes 73728 | tf_op jit(solution)/shard_map/broadcast_in_dim | solution.py:273
  7.6 3.4 %all-to-all-start = ((bf16[8,8,512]{2,1,0:T(8,128)(2,1)}), bf16[8,8,512]{2,1,0:T(8,128)(2,1)S(1)}, u32[]{:S(2)}, u32[]{:S(2)}) async-start(bf16[8,8,512]{2,1,0:T(8,128)(2,1)} %broadcast_in_dim.2), calls=%async_computation | async-start | bytes 131072 | tf_op jit(solution)/shard_map/all_to_all | solution.py:274
  11.6 1.3 %pad_add_fusion.index_ref = s32[37]{0:T(128)} fusion(s32[1]{0:T(128)} %bitcast.15, s32[12]{0:T(128)} %bitcast.17, s32[12]{0:T(128)} %bitcast.18, s32[12]{0:T(128)} %bitcast.19), kind=kLoop, calls=%fused_computation | loop fusion | flops 111 | bytes 296 | tf_op jit(solution)/shard_map/concatenate | solution.py:286
  12.9 5.9 %all-to-all-done.occ_ref = bf16[8,8,512]{2,1,0:T(8,128)(2,1)S(1)} async-done(((bf16[8,8,512]{2,1,0:T(8,128)(2,1)}), bf16[8,8,512]{2,1,0:T(8,128)(2,1)S(1)}, u32[]{:S(2)}, u32[]{:S(2)}) %all-to-all-start) | async-done | bytes 65568 | tf_op jit(solution)/shard_map/all_to_all | solution.py:274
  18.8 0.0 copy-start.4
  18.8 0.0 collective-permute-done.refs_1_
  18.8 0.0 collective-permute-done.1.refs_2_
  18.8 0.6 copy-done.4
  19.4 7.4 %half_transform.1 = bf16[8,400,128]{2,1,0:T(8,128)(2,1)} custom-call(s32[37]{0:T(128)} %pad_add_fusion.index_ref, bf16[8,8,512]{2,1,0:T(8,128)(2,1)} %copy-done.4, bf16[12,32,128,128]{3,2,1,0:T(8,128)(2,1)} %bitcast.16), custom_call_target="tpu_custom_call" | custom-call | flops 201326592 | bytes 12582912 | tf_op jit(solution)/shard_map/half_transform/pallas_call | solution.py:83
  26.8 3.6 %all-to-all-start.1 = ((bf16[8,400,128]{2,1,0:T(8,128)(2,1)}), bf16[8,400,128]{2,1,0:T(8,128)(2,1)S(1)}, u32[]{:S(2)}, u32[]{:S(2)}) async-start(bf16[8,400,128]{2,1,0:T(8,128)(2,1)} %half_transform.1), calls=%async_computation.1 | async-start | bytes 1638400 | tf_op jit(solution)/shard_map/all_to_all | solution.py:287
  30.4 1.9 %collective-permute-start.2 = (bf16[512,512]{1,0:T(8,128)(2,1)S(1)}, bf16[512,512]{1,0:T(8,128)(2,1)}, u32[]{:S(2)}, u32[]{:S(2)}) collective-permute-start(bf16[512,512]{1,0:T(8,128)(2,1)S(1)} %collective-permute-done.refs_1_), channel_id=1, source_target_pairs={{0,16},{4,12},{8,24},{12,4},{16,0},{20,28},{24,8},{28,20},{1,17},{... | collective-permute-start | bytes 1572872 | tf_op jit(solution)/shard_map/ppermute | solution.py:271
  32.3 0.0 copy-done
  32.3 0.0 collective-permute-start.3
  32.3 0.5 collective-permute-start.4
  32.8 0.0 collective-permute-start.5
  32.8 15.2 %collective-permute-done.2.refs_3_ = bf16[512,512]{1,0:T(8,128)(2,1)} collective-permute-done((bf16[512,512]{1,0:T(8,128)(2,1)S(1)}, bf16[512,512]{1,0:T(8,128)(2,1)}, u32[]{:S(2)}, u32[]{:S(2)}) %collective-permute-start.2) | collective-permute-done | bytes 524320 | tf_op jit(solution)/shard_map/ppermute | solution.py:271
  48.0 0.1 collective-permute-start.6
  48.1 0.0 all-to-all-done.1.half_ref
  48.1 0.8 collective-permute-start.7
  48.9 0.1 stack.43.where_ref
  49.0 0.0 copy-start.3
  49.0 0.0 collective-permute-done.3.refs_4_
  49.0 0.0 collective-permute-done.4.refs_5_
  49.0 0.0 collective-permute-done.5.refs_6_
  49.0 1.3 %collective-permute-done.6.refs_7_ = bf16[512,512]{1,0:T(8,128)(2,1)} collective-permute-done((bf16[512,512]{1,0:T(8,128)(2,1)}, bf16[512,512]{1,0:T(8,128)(2,1)}, u32[]{:S(2)}, u32[]{:S(2)}) %collective-permute-start.6) | collective-permute-done | bytes 524320 | tf_op jit(solution)/shard_map/ppermute | solution.py:271
  50.3 6.6 %pair_transform.2 = (f32[256,512]{1,0:T(8,128)S(1)}, bf16[1,256,512]{2,1,0:T(8,128)(2,1)S(1)}) custom-call(s32[10]{0:T(128)S(1)} %stack.43.where_ref, bf16[8,400,128]{2,1,0:T(8,128)(2,1)S(1)} %all-to-all-done.1.half_ref, bf16[512,512]{1,0:T(8,128)(2,1)S(1)} %copy-done, bf16[512,512]{1,0:T(8,128)(2,1)S(1)} %collective-permute-done.refs_1_, ...), custom_call_target="tpu_custom_call" | custom-call | flops 4294967296 | bytes 5013504 | tf_op jit(solution)/shard_map/pair_transform/pallas_call | solution.py:162
  56.9 0.0 copy-start.1
  56.9 0.8 copy-done.1
  57.7 3.3 %collective-permute-start.8 = (bf16[1,256,512]{2,1,0:T(8,128)(2,1)S(1)}, bf16[1,256,512]{2,1,0:T(8,128)(2,1)S(1)}, u32[]{:S(2)}, u32[]{:S(2)}) collective-permute-start(bf16[1,256,512]{2,1,0:T(8,128)(2,1)S(1)} %get-tuple-element.17), channel_id=1, source_target_pairs={{0,2},{1,3},{2,0},{3,1},{4,6},{5,7},{6,4},{7,5},{8,10},{9,11},{10,... | collective-permute-start | bytes 786440 | tf_op jit(solution)/shard_map/ppermute | solution.py:268
  61.0 13.3 %collective-permute-done.7.half_ref = bf16[8,400,128]{2,1,0:T(8,128)(2,1)S(1)} collective-permute-done((bf16[8,400,128]{2,1,0:T(8,128)(2,1)S(1)}, bf16[8,400,128]{2,1,0:T(8,128)(2,1)S(1)}, u32[]{:S(2)}, u32[]{:S(2)}) %collective-permute-start.7) | collective-permute-done | bytes 819232 | tf_op jit(solution)/shard_map/ppermute | solution.py:268
  74.3 6.6 %pair_transform.3 = (f32[256,512]{1,0:T(8,128)S(1)}, bf16[1,256,512]{2,1,0:T(8,128)(2,1)S(1)}) custom-call(s32[10]{0:T(128)S(1)} %stack.43.where_ref, bf16[8,400,128]{2,1,0:T(8,128)(2,1)S(1)} %collective-permute-done.7.half_ref, bf16[512,512]{1,0:T(8,128)(2,1)S(1)} %copy-done, bf16[512,512]{1,0:T(8,128)(2,1)S(1)} %collective-permute-done.refs_1_, ...), custom_call_target="tpu_custom_call" | custom-call | flops 4294967296 | bytes 5013504 | tf_op jit(solution)/shard_map/pair_transform/pallas_call | solution.py:162
  80.9 0.0 copy-done.3
  80.9 0.0 copy-start.2
  81.0 0.8 copy-done.2
  81.8 0.3 collective-permute-start.9
  82.1 0.0 collective-permute-done.8.got_first_ref
  82.1 0.0 copy-start.5
  82.1 13.9 %collective-permute-done.9.got_second_ref = bf16[1,256,512]{2,1,0:T(8,128)(2,1)S(1)} collective-permute-done((bf16[1,256,512]{2,1,0:T(8,128)(2,1)S(1)}, bf16[1,256,512]{2,1,0:T(8,128)(2,1)S(1)}, u32[]{:S(2)}, u32[]{:S(2)}) %collective-permute-start.9) | collective-permute-done | bytes 262176 | tf_op jit(solution)/shard_map/ppermute | solution.py:268
  96.0 0.0 copy-start.6
  96.0 0.0 copy-done.5
  96.0 0.7 copy-done.6
  96.7 3.4 %place.1 = f32[256,2048]{1,0:T(8,128)} custom-call(s32[10]{0:T(128)} %copy-done.3, f32[256,512]{1,0:T(8,128)} %copy-done.1, f32[256,512]{1,0:T(8,128)} %copy-done.2, bf16[1,256,512]{2,1,0:T(8,128)(2,1)} %copy-done.5, bf16[1,256,512]{2,1,0:T(8,128)(2,1)} %copy-done.6), custom_call_target="tpu_custom_call" | custom-call | bytes 4194304 | tf_op jit(solution)/shard_map/place/pallas_call | solution.py:216
Async XLA Ops:
  1.8 30.5 %copy-start = (bf16[512,512]{1,0:T(8,128)(2,1)S(1)}, bf16[512,512]{1,0:T(8,128)(2,1)}, u32[]{:S(2)}) copy-start(bf16[512,512]{1,0:T(8,128)(2,1)} %vir_columns.1.refs_0_) | copy-start | bytes 1572868
  1.8 17.0 %collective-permute-start = (bf16[512,512]{1,0:T(8,128)(2,1)}, bf16[512,512]{1,0:T(8,128)(2,1)S(1)}, u32[]{:S(2)}, u32[]{:S(2)}) collective-permute-start(bf16[512,512]{1,0:T(8,128)(2,1)} %vir_columns.1.refs_0_), channel_id=1, source_target_pairs={{0,8},{4,20},{8,0},{12,28},{16,24},{20,4},{24,16},{28,12},{1,9},{5... | collective-permute-start | bytes 1572872 | tf_op jit(solution)/shard_map/ppermute | solution.py:271
  4.7 14.1 %collective-permute-start.1 = (bf16[512,512]{1,0:T(8,128)(2,1)}, bf16[512,512]{1,0:T(8,128)(2,1)S(1)}, u32[]{:S(2)}, u32[]{:S(2)}) collective-permute-start(bf16[512,512]{1,0:T(8,128)(2,1)} %vir_columns.1.refs_0_), channel_id=1, source_target_pairs={{0,16},{4,12},{8,24},{12,4},{16,0},{20,28},{24,8},{28,20},{1,17},{... | collective-permute-start | bytes 1572872 | tf_op jit(solution)/shard_map/ppermute | solution.py:271
  7.6 11.2 %all-to-all-start = ((bf16[8,8,512]{2,1,0:T(8,128)(2,1)}), bf16[8,8,512]{2,1,0:T(8,128)(2,1)S(1)}, u32[]{:S(2)}, u32[]{:S(2)}) async-start(bf16[8,8,512]{2,1,0:T(8,128)(2,1)} %broadcast_in_dim.2), calls=%async_computation | async-start | bytes 131072 | tf_op jit(solution)/shard_map/all_to_all | solution.py:274
  18.8 0.6 copy-start.4
  26.8 21.3 %all-to-all-start.1 = ((bf16[8,400,128]{2,1,0:T(8,128)(2,1)}), bf16[8,400,128]{2,1,0:T(8,128)(2,1)S(1)}, u32[]{:S(2)}, u32[]{:S(2)}) async-start(bf16[8,400,128]{2,1,0:T(8,128)(2,1)} %half_transform.1), calls=%async_computation.1 | async-start | bytes 1638400 | tf_op jit(solution)/shard_map/all_to_all | solution.py:287
  30.4 17.6 %collective-permute-start.2 = (bf16[512,512]{1,0:T(8,128)(2,1)S(1)}, bf16[512,512]{1,0:T(8,128)(2,1)}, u32[]{:S(2)}, u32[]{:S(2)}) collective-permute-start(bf16[512,512]{1,0:T(8,128)(2,1)S(1)} %collective-permute-done.refs_1_), channel_id=1, source_target_pairs={{0,16},{4,12},{8,24},{12,4},{16,0},{20,28},{24,8},{28,20},{1,17},{... | collective-permute-start | bytes 1572872 | tf_op jit(solution)/shard_map/ppermute | solution.py:271
  32.3 16.7 %collective-permute-start.3 = (bf16[512,512]{1,0:T(8,128)(2,1)S(1)}, bf16[512,512]{1,0:T(8,128)(2,1)}, u32[]{:S(2)}, u32[]{:S(2)}) collective-permute-start(bf16[512,512]{1,0:T(8,128)(2,1)S(1)} %copy-done), channel_id=1, source_target_pairs={{0,4},{4,0},{8,12},{12,8},{16,20},{20,16},{24,28},{28,24},{1,5},{5... | collective-permute-start | bytes 1572872 | tf_op jit(solution)/shard_map/ppermute | solution.py:271
  32.3 16.7 %collective-permute-start.4 = (bf16[512,512]{1,0:T(8,128)(2,1)S(1)}, bf16[512,512]{1,0:T(8,128)(2,1)}, u32[]{:S(2)}, u32[]{:S(2)}) collective-permute-start(bf16[512,512]{1,0:T(8,128)(2,1)S(1)} %collective-permute-done.refs_1_), channel_id=1, source_target_pairs={{0,4},{4,0},{8,12},{12,8},{16,20},{20,16},{24,28},{28,24},{1,5},{5... | collective-permute-start | bytes 1572872 | tf_op jit(solution)/shard_map/ppermute | solution.py:271
  32.8 16.2 %collective-permute-start.5 = (bf16[512,512]{1,0:T(8,128)(2,1)S(1)}, bf16[512,512]{1,0:T(8,128)(2,1)}, u32[]{:S(2)}, u32[]{:S(2)}) collective-permute-start(bf16[512,512]{1,0:T(8,128)(2,1)S(1)} %collective-permute-done.1.refs_2_), channel_id=1, source_target_pairs={{0,4},{4,0},{8,12},{12,8},{16,20},{20,16},{24,28},{28,24},{1,5},{5... | collective-permute-start | bytes 1572872 | tf_op jit(solution)/shard_map/ppermute | solution.py:271
  48.0 2.3 %collective-permute-start.6 = (bf16[512,512]{1,0:T(8,128)(2,1)}, bf16[512,512]{1,0:T(8,128)(2,1)}, u32[]{:S(2)}, u32[]{:S(2)}) collective-permute-start(bf16[512,512]{1,0:T(8,128)(2,1)} %collective-permute-done.2.refs_3_), channel_id=1, source_target_pairs={{0,4},{4,0},{8,12},{12,8},{16,20},{20,16},{24,28},{28,24},{1,5},{5... | collective-permute-start | bytes 1572872 | tf_op jit(solution)/shard_map/ppermute | solution.py:271
  48.1 26.2 %collective-permute-start.7 = (bf16[8,400,128]{2,1,0:T(8,128)(2,1)S(1)}, bf16[8,400,128]{2,1,0:T(8,128)(2,1)S(1)}, u32[]{:S(2)}, u32[]{:S(2)}) collective-permute-start(bf16[8,400,128]{2,1,0:T(8,128)(2,1)S(1)} %all-to-all-done.1.half_ref), channel_id=1, source_target_pairs={{0,1},{1,0},{2,3},{3,2},{4,5},{5,4},{6,7},{7,6},{8,9},{9,8},{10,11... | collective-permute-start | bytes 2457608 | tf_op jit(solution)/shard_map/ppermute | solution.py:268
  49.0 32.0 %copy-start.3 = (s32[10]{0:T(128)}, s32[10]{0:T(128)S(1)}, u32[]{:S(2)}) copy-start(s32[10]{0:T(128)S(1)} %stack.43.where_ref) | copy-start | bytes 124
  56.9 0.8 copy-start.1
  57.7 24.4 %collective-permute-start.8 = (bf16[1,256,512]{2,1,0:T(8,128)(2,1)S(1)}, bf16[1,256,512]{2,1,0:T(8,128)(2,1)S(1)}, u32[]{:S(2)}, u32[]{:S(2)}) collective-permute-start(bf16[1,256,512]{2,1,0:T(8,128)(2,1)S(1)} %get-tuple-element.17), channel_id=1, source_target_pairs={{0,2},{1,3},{2,0},{3,1},{4,6},{5,7},{6,4},{7,5},{8,10},{9,11},{10,... | collective-permute-start | bytes 786440 | tf_op jit(solution)/shard_map/ppermute | solution.py:268
  80.9 0.8 copy-start.2
  81.8 14.3 %collective-permute-start.9 = (bf16[1,256,512]{2,1,0:T(8,128)(2,1)S(1)}, bf16[1,256,512]{2,1,0:T(8,128)(2,1)S(1)}, u32[]{:S(2)}, u32[]{:S(2)}) collective-permute-start(bf16[1,256,512]{2,1,0:T(8,128)(2,1)S(1)} %get-tuple-element.20), channel_id=1, source_target_pairs={{0,2},{1,3},{2,0},{3,1},{4,6},{5,7},{6,4},{7,5},{8,10},{9,11},{10,... | collective-permute-start | bytes 786440 | tf_op jit(solution)/shard_map/ppermute | solution.py:268
  82.1 14.0 %copy-start.5 = (bf16[1,256,512]{2,1,0:T(8,128)(2,1)}, bf16[1,256,512]{2,1,0:T(8,128)(2,1)S(1)}, u32[]{:S(2)}) copy-start(bf16[1,256,512]{2,1,0:T(8,128)(2,1)S(1)} %collective-permute-done.8.got_first_ref) | copy-start | bytes 786436
  96.0 0.7 copy-start.6

commit v3 on v2

v3 whole, which is shorter than its diff:
```python
import functools

import jax
import jax.numpy as jnp
from jax import lax
from jax.experimental import pallas as pl
from jax.experimental.pallas import tpu as pltpu
from jax.sharding import PartitionSpec as P

PDEV = 512
META = 16
PAIR_LIMIT = 40
PLACE_LIMIT = 40
FIELD = 16


def whole(shape):
    return pl.BlockSpec(shape, lambda n, *_: (0,) * len(shape))


def row_of(k, kmax, pb):
    return k * pb + (META if k >= kmax // 2 else 0)


def half_kernel(index_ref, occ_ref, tiles_hbm, half_ref, tile_ref, stage_ref, sems):
    kmax, pb, blk, _ = tile_ref.shape
    rows_ref, cols_ref, aux_ref = (index_ref.at[pl.ds(n * kmax, kmax)] for n in range(3))
    orbitals = half_ref.shape[0]
    ao_blocks = occ_ref.shape[2] // blk
    count = index_ref[3 * kmax]

    def fetch(k):
        return pltpu.make_async_copy(tiles_hbm.at[k], tile_ref.at[k], sems.at[k])

    for k in range(kmax):

        @pl.when(k < count)
        def _():
            fetch(k).start()

    lanes = lax.broadcasted_iota(jnp.int32, (META, blk), 1)
    meta = jnp.zeros((META, blk), jnp.int32)
    for k in range(kmax):
        again = jnp.bool_(False)
        for j in range(k):
            same = jnp.logical_and(cols_ref[j] == cols_ref[k], aux_ref[j] == aux_ref[k])
            again = jnp.logical_or(again, same)
        again = jnp.logical_and(again, k < count)
        row = aux_ref[k] * pb
        first = jnp.where(jnp.logical_or(again, k >= count), PDEV, row)
        for n, value in enumerate((first, cols_ref[k] * blk, again.astype(jnp.int32), row)):
            meta = jnp.where(lanes == n * FIELD + k, value, meta)
    meta = meta.astype(jnp.float32).astype(jnp.bfloat16)
    split = kmax // 2 * pb
    for i in range(orbitals):
        half_ref[i, split : split + META, :] = meta

    for k in range(kmax):
        at = row_of(k, kmax, pb)

        @pl.when(k < count)
        def _(k=k, at=at):
            row = rows_ref[k]
            lane = pl.multiple_of(row % ao_blocks * blk, blk)
            occ = occ_ref[row // ao_blocks, :, pl.ds(lane, blk)].astype(jnp.float32)
            zero = jnp.zeros_like(occ)
            upper = jnp.concatenate([occ, zero], axis=1)
            lower = jnp.concatenate([zero, occ], axis=1)
            pair = jnp.concatenate([upper, lower], axis=0).astype(jnp.bfloat16)
            stage = stage_ref.at[k % 2]
            fetch(k).wait()
            for p in range(0, pb, 2):
                rhs = tile_ref[k, p : p + 2].reshape(2 * blk, blk)
                stage[p * orbitals : (p + 2) * orbitals, :] = jnp.dot(
                    pair, rhs, preferred_element_type=jnp.float32
                )
            for i in range(orbitals):
                part = stage[pl.ds(i, pb, stride=orbitals), :].astype(jnp.bfloat16)
                half_ref[i, at : at + pb, :] = part

        @pl.when(k >= count)
        def _(at=at):
            empty = jnp.zeros((orbitals, pb, blk), jnp.bfloat16)
            half_ref[:, at : at + pb, :] = empty


def half_transform(tiles, index, occ):
    kmax, pb, blk, _ = tiles.shape
    orbitals = occ.shape[1]
    out = (orbitals, kmax * pb + META, blk)
    return pl.pallas_call(
        half_kernel,
        grid_spec=pltpu.PrefetchScalarGridSpec(
            num_scalar_prefetch=1,
            grid=(1,),
            in_specs=[whole(occ.shape), pl.BlockSpec(memory_space=pl.ANY)],
            out_specs=whole(out),
            scratch_shapes=[
                pltpu.VMEM(tiles.shape, jnp.bfloat16),
                pltpu.VMEM((2, pb * orbitals, blk), jnp.float32),
                pltpu.SemaphoreType.DMA((kmax,)),
            ],
        ),
        out_shape=jax.ShapeDtypeStruct(out, jnp.bfloat16),
        compiler_params=pltpu.CompilerParams(vmem_limit_bytes=52 << 20),
        cost_estimate=pl.CostEstimate(
            flops=4 * tiles.size * orbitals, bytes_accessed=tiles.size * 2, transcendentals=0
        ),
        name="half_transform",
    )(index, occ, tiles)


def pair_kernel(kmax, pb, group, vb, kind, inputs, side, where_ref, *refs):
    half_refs, refs = refs[:inputs], refs[inputs:]
    vir_hbm, refs = refs[:group], refs[group:]
    vir_ref, dense_ref, sum_ref, turn_ref, meta_ref, code_ref, again_ref, sem, sems = refs[-9:]
    results = refs[-9 - (2 if kind == "both" else 1) : -9]
    depth = vir_hbm[0].shape[0]
    blk = meta_ref.shape[1]
    low, high = columns_for(kind, vir_ref.shape[1] if kind == "both" else vir_hbm[0].shape[1], vb)
    fetches = [
        pltpu.make_async_copy(
            vir_hbm[d].at[:, pl.ds(low, high - low)], vir_ref.at[pl.ds(d * depth, depth), :], sems.at[d]
        )
        for d in range(group)
    ]
    for fetch in fetches:
        fetch.start()
    split = kmax // 2 * pb
    for g in range(group):
        meta_ref[g : g + 1, :] = (
            half_refs[0][g, split : split + META, :].astype(jnp.float32)[:1].astype(jnp.int32)
        )
    copy = pltpu.make_async_copy(meta_ref, code_ref, sem)
    copy.start()
    dense_ref[:PDEV, :] = jnp.zeros((PDEV, group * depth), jnp.bfloat16)
    copy.wait()

    def source(k):
        at = row_of(k, kmax, pb)
        if inputs == 2 and k >= kmax // 2:
            return half_refs[1], at - split - META
        return half_refs[0], at

    def scatter(step, repeats):
        g = where_ref[2 + step]
        for k in range(kmax):
            ref, at = source(k)
            row = pl.multiple_of(code_ref[g, k], pb)
            lane = pl.multiple_of(step * depth + code_ref[g, FIELD + k], blk)
            dense_ref[pl.ds(row, pb), pl.ds(lane, blk)] = ref[g, at : at + pb, :]
            again_ref[repeats] = step * kmax + k
            repeats = repeats + code_ref[g, 2 * FIELD + k]
        return repeats

    repeats = lax.fori_loop(0, group, scatter, jnp.int32(0))
    for fetch in fetches:
        fetch.wait()
    sum_ref[...] = jnp.dot(dense_ref[:PDEV, :], vir_ref[...], preferred_element_type=jnp.float32)

    def repeat(n, carry):
        slot = again_ref[n]
        step, k = slot // kmax, slot % kmax
        g = where_ref[2 + step]
        row = pl.multiple_of(code_ref[g, 3 * FIELD + k], pb)
        lane = pl.multiple_of(step * depth + code_ref[g, FIELD + k], blk)

        def add(ref, at):
            sum_ref[pl.ds(row, pb), :] += jnp.dot(
                ref[g, pl.ds(pl.multiple_of(at, META), pb), :],
                vir_ref[pl.ds(lane, blk), :],
                preferred_element_type=jnp.float32,
            )

        late = k >= kmax // 2

        @pl.when(late)
        def _():
            if inputs == 2:
                add(half_refs[1], k * pb - split)
            else:
                add(half_refs[0], k * pb + META)

        @pl.when(jnp.logical_not(late))
        def _():
            add(half_refs[0], k * pb)

        return carry

    lax.fori_loop(0, repeats, repeat, 0)
    turn_ref[...] = sum_ref[...].T
    offset = 0
    if kind != "send":
        offset = vb
        column = pl.multiple_of(where_ref[side] * PDEV, PDEV)
        copy = pltpu.make_async_copy(
            turn_ref.at[:vb], results[-1].at[:, pl.ds(column, PDEV)], sems.at[group]
        )
        copy.start()
    if kind != "own":
        for j in range(results[0].shape[0]):
            results[0][j] = turn_ref[offset + j * vb : offset + (j + 1) * vb].astype(jnp.bfloat16)
    if kind != "send":
        copy.wait()


def columns_for(kind, width, vb):
    return {"both": (0, width), "own": (0, vb), "send": (vb, width)}[kind]


def pair_transform(kind, halves, virs, where, kmax, pb, vb, columns=0, result=None):
    group, _, blk = halves[0].shape
    depth, width = virs[0].shape
    others = width // vb - 1
    low, high = columns_for(kind, width, vb)
    anywhere = pl.BlockSpec(memory_space=pl.ANY)
    out_specs, out_shape = [], []
    if kind != "own":
        out_specs.append(whole((others, vb, PDEV)))
        out_shape.append(jax.ShapeDtypeStruct((others, vb, PDEV), jnp.bfloat16))
    if kind != "send":
        out_specs.append(anywhere)
        out_shape.append(jax.ShapeDtypeStruct((vb, columns), jnp.float32))
    return pl.pallas_call(
        functools.partial(pair_kernel, kmax, pb, group, vb, kind, len(halves), int(result is not None)),
        grid_spec=pltpu.PrefetchScalarGridSpec(
            num_scalar_prefetch=1,
            grid=(1,),
            in_specs=[whole(x.shape) for x in halves] + [anywhere] * (group + (result is not None)),
            out_specs=out_specs,
            scratch_shapes=[
                pltpu.VMEM((group * depth, high - low), jnp.bfloat16),
                pltpu.VMEM((PDEV + pb, group * depth), jnp.bfloat16),
                pltpu.VMEM((PDEV, high - low), jnp.float32),
                pltpu.VMEM((high - low, PDEV), jnp.float32),
                pltpu.VMEM((group, blk), jnp.int32),
                pltpu.SMEM((group, blk), jnp.int32),
                pltpu.SMEM((group * kmax + 1,), jnp.int32),
                pltpu.SemaphoreType.DMA,
                pltpu.SemaphoreType.DMA((group + 1,)),
            ],
        ),
        out_shape=out_shape,
        input_output_aliases={} if result is None else {1 + len(halves) + group: 0},
        compiler_params=pltpu.CompilerParams(vmem_limit_bytes=PAIR_LIMIT << 20),
        cost_estimate=pl.CostEstimate(
            flops=4 * PDEV * group * depth * (high - low),
            bytes_accessed=group * depth * (high - low) * 2 + halves[0].size * 2,
            transcendentals=0,
        ),
        name=kind + "_part",
    )(where, *halves, *virs, *([] if result is None else [result]))


def place_kernel(side, where_ref, got_ref, _, out_hbm, wide_ref, sems):
    copies = []
    for j in range(got_ref.shape[0]):
        wide_ref[j] = got_ref[j].astype(jnp.float32)
        block = jnp.bitwise_xor(where_ref[side], 2 * (j + 1))
        lane = pl.multiple_of(block * PDEV, PDEV)
        copies.append(pltpu.make_async_copy(wide_ref.at[j], out_hbm.at[:, pl.ds(lane, PDEV)], sems.at[j]))
        copies[-1].start()
    for copy in copies:
        copy.wait()


def place(where, got, result, side):
    return pl.pallas_call(
        functools.partial(place_kernel, side),
        grid_spec=pltpu.PrefetchScalarGridSpec(
            num_scalar_prefetch=1,
            grid=(1,),
            in_specs=[whole(got.shape), pl.BlockSpec(memory_space=pl.ANY)],
            out_specs=pl.BlockSpec(memory_space=pl.ANY),
            scratch_shapes=[
                pltpu.VMEM(got.shape, jnp.float32),
                pltpu.SemaphoreType.DMA((got.shape[0],)),
            ],
        ),
        out_shape=jax.ShapeDtypeStruct(result.shape, jnp.float32),
        input_output_aliases={2: 0},
        cost_estimate=pl.CostEstimate(flops=0, bytes_accessed=got.size * 6, transcendentals=0),
        compiler_params=pltpu.CompilerParams(vmem_limit_bytes=PLACE_LIMIT << 20),
        name="place",
    )(where, got, result)


def open_kernel(vb, vir_hbm, occ_ref, occ_out_ref, out_ref, sems):
    aux = lax.axis_index("aux")
    copies = []
    for j in range(out_ref.shape[1] // vb):
        block = jnp.bitwise_xor(aux // 2, j) * 2 + aux % 2
        copies.append(
            pltpu.make_async_copy(
                vir_hbm.at[:, pl.ds(pl.multiple_of(block * vb, vb), vb)],
                out_ref.at[:, pl.ds(j * vb, vb)],
                sems.at[j],
            )
        )
        copies[-1].start()
    occ_out_ref[...] = jnp.broadcast_to(occ_ref[...][None], occ_out_ref.shape)
    for copy in copies:
        copy.wait()


def opening(vir, occ, group_size, aux, aux_size, vb):
    rows = vir.shape[0]
    parts = aux_size // 2
    copies = (group_size, *occ.shape)
    if vb % 128:
        order = jnp.bitwise_xor(aux // 2, jnp.arange(parts)) * 2 + aux % 2
        chosen = jnp.take(vir.reshape(rows, aux_size, vb), order, axis=1)
        return jnp.broadcast_to(occ[None], copies), chosen.reshape(rows, -1)
    vmem = pl.BlockSpec(memory_space=pltpu.VMEM)
    return pl.pallas_call(
        functools.partial(open_kernel, vb),
        in_specs=[pl.BlockSpec(memory_space=pl.ANY), vmem],
        out_specs=[vmem, vmem],
        scratch_shapes=[pltpu.SemaphoreType.DMA((parts,))],
        out_shape=[
            jax.ShapeDtypeStruct(copies, occ.dtype),
            jax.ShapeDtypeStruct((rows, parts * vb), vir.dtype),
        ],
        compiler_params=pltpu.CompilerParams(vmem_limit_bytes=60 << 20),
        name="opening",
    )(vir, occ)


def shards(integral_tiles, row_blocks, col_blocks, aux_blocks, tile_counts, occ_coeffs, vir_coeffs):
    group_size = lax.axis_size("grp")
    aux_size = lax.axis_size("aux")
    aux = lax.axis_index("aux")
    kmax, pb = integral_tiles.shape[2:4]
    orbitals = occ_coeffs.shape[0]
    virtuals = vir_coeffs.shape[1]
    vb = virtuals * orbitals // (group_size * aux_size)

    def swap(x, step):
        return lax.ppermute(x, "aux", [(a, a ^ step) for a in range(aux_size)])

    def hop(x, steps):
        return lax.ppermute(x, "grp", [(g, g ^ steps[g % 2]) for g in range(group_size)])

    occ, own = opening(vir_coeffs, occ_coeffs, group_size, aux, aux_size, vb)
    occ = lax.all_to_all(occ, "grp", split_axis=0, concat_axis=0, tiled=True)

    core = lax.axis_index("grp") % 2
    near = hop(own, (2, 4))
    far = hop(own, (4, 2))
    occ, near, far = lax.optimization_barrier((occ, near, far))
    across = hop(near, (4, 2))
    virs = [own, near, far, across]
    virs = virs + [hop(vir, (1, 1)) for vir in virs]

    index = [x[0, 0] for x in (row_blocks, col_blocks, aux_blocks)] + [tile_counts[0]]
    halves = half_transform(integral_tiles[0, 0], jnp.concatenate(index), occ)
    others = swap(halves, 1)
    halves = lax.all_to_all(halves, "grp", split_axis=0, concat_axis=0, tiled=True)
    others, halves = lax.optimization_barrier((others, halves))
    others = lax.all_to_all(others, "grp", split_axis=0, concat_axis=0, tiled=True)

    moved = [0, 2 + 2 * core, 4 - 2 * core, 6, 1, 5 - 2 * core, 3 + 2 * core, 7]
    moved = [jnp.bitwise_xor(lax.axis_index("grp"), step) for step in moved]
    where = jnp.stack([aux, jnp.bitwise_xor(aux, 1)] + moved).astype(jnp.int32)

    def trade(send):
        if aux_size == 4:
            return swap(send, 2)
        return jnp.stack([swap(send[j - 1], 2 * j) for j in range(1, aux_size // 2)])

    sizes = (kmax, pb, vb)
    columns = aux_size * PDEV
    if vb % 128:
        send_first, result = pair_transform("both", [halves], virs, where, *sizes, columns=columns)
        send_second, own_second = pair_transform("both", [others], virs, where, *sizes, columns=columns)
        got_first = trade(send_first)
        block = (jnp.bitwise_xor(aux, 1) * PDEV).astype(jnp.int32)
        own_second = lax.dynamic_slice_in_dim(own_second, (aux * PDEV).astype(jnp.int32), PDEV, 1)
        result = lax.dynamic_update_slice_in_dim(result, own_second, block, 1)
    else:
        (send_first,) = pair_transform("send", [halves], virs, where, *sizes)
        got_first = trade(send_first)
        others, _ = lax.optimization_barrier((others, send_first))
        (send_second,) = pair_transform("send", [others], virs, where, *sizes)
        others, halves, _ = lax.optimization_barrier((others, halves, send_second))
        (result,) = pair_transform("own", [halves], virs, where, *sizes, columns=columns)
        (result,) = pair_transform("own", [others], virs, where, *sizes, columns=columns, result=result)
    result = place(where, got_first, result, 0)
    return place(where, trade(send_second), result, 1)


def solution(mesh):
    in_specs = (
        P("grp", "aux", None, None, None, None),
        P("grp", "aux", None),
        P("grp", "aux", None),
        P("grp", "aux", None),
        P("grp", "aux"),
        P(None, "grp"),
        P("grp", None),
    )
    out_specs = P(("grp", "aux"), None)
    return jax.shard_map(shards, mesh=mesh, in_specs=in_specs, out_specs=out_specs, check_vma=False)
```

time: 101 us -> 85.3 us (0.84)
  waiting for transfers between devices: 49.6 us -> 29.2 us
  starting transfers between devices: 18.3 us -> 24.7 us
  local copies, waits for them, and re-layouts: 4.34 us -> 0.09 us
  Pallas kernels: 25.8 us -> 29.5 us
    ppermute x3, waiting for transfers between devices: 27.3 us -> 1.61 us  [swap(): return lax.ppermute(x, 'aux', [(a, a ^ step) for a in range(aux_size)])]
    pallas_call x4 -> x7, Pallas kernels: 18.4 us -> 23.4 us  [the longest x4 18.1 us: pair_transform(): pl.pallas_call(functools.partial(pair_kernel, kmax, pb, group, vb, kind,...]
    all_to_all x0 -> x1, waiting for transfers between devices: none -> 4.95 us  [shards(): lax.all_to_all(others, 'grp', split_axis=0, concat_axis=0, tiled=True)]
    all_to_all x0 -> x1, starting transfers between devices: none -> 3.55 us  [shards(): lax.all_to_all(others, 'grp', split_axis=0, concat_axis=0, tiled=True)]
    unnamed x14 -> x2, local copies, waits for them, and re-layouts: 2.92 us -> 0.01 us
    all_to_all x1, waiting for transfers between devices: 5.91 us -> 7.75 us  [shards(): occ = lax.all_to_all(occ, 'grp', split_axis=0, concat_axis=0, tiled=True)]
    ppermute x7, waiting for transfers between devices: 16.5 us -> 14.9 us  [hop(): lax.ppermute(x, 'grp', [(g, g ^ steps[g % 2]) for g in range(group_size)])]
    broadcast_in_dim x1 -> x0, local copies, waits for them, and re-layouts: 1.33 us -> none  [shards(): occ = jnp.broadcast_to(occ_coeffs[None], (group_size, *occ_coeffs.shape))]
  transfers between devices with their start and end apart: 12 -> 13, of which waited for: 5 -> 4; matrix products, arithmetic and copies ran while one was open for 3% -> 1% of each run, Pallas kernels for 13% -> 23%
where the time goes in v3:
time: 85.3 us; the launch traced here: 85.1 us
  Pallas kernels  29.5 us (35%)
  waiting for transfers between devices  29.2 us (34%)
  starting transfers between devices  24.7 us (29%)
    pallas_call x4, Pallas kernels, pair_transform(): pl.pallas_call(functools.partial(pair_kernel, kmax, pb, group, vb, kind,...  18.1 us
    ppermute x7, waiting for transfers between devices, hop(): lax.ppermute(x, 'grp', [(g, g ^ steps[g % 2]) for g in range(group_size)])  14.9 us
    all_to_all x1, waiting for transfers between devices, shards(): occ = lax.all_to_all(occ, 'grp', split_axis=0, concat_axis=0, tiled=True)  7.75 us
    ppermute x7, starting transfers between devices, hop(): lax.ppermute(x, 'grp', [(g, g ^ steps[g % 2]) for g in range(group_size)])  7.45 us
    pallas_call x1, Pallas kernels, half_transform(): pl.pallas_call(half_kernel, grid_spec=pltpu.PrefetchScalarGridSpec(num_sc...  6.13 us
    ppermute x3, starting transfers between devices, swap(): return lax.ppermute(x, 'aux', [(a, a ^ step) for a in range(aux_size)])  5.57 us
    all_to_all x1, waiting for transfers between devices, shards(): lax.all_to_all(others, 'grp', split_axis=0, concat_axis=0, tiled=True)  4.95 us
    all_to_all x1, starting transfers between devices, shards(): lax.all_to_all(halves, 'grp', split_axis=0, concat_axis=0, tiled=True)  4.75 us
  transfers between devices with their start and end apart: 13, of which 4 were waited for; matrix products, arithmetic and copies ran while one was open for 1% of the time, Pallas kernels for 23%

profile of v3, /device:TPU:0, one launch (start us, length us, event | category | flops | bytes accessed | tf_op | source)
XLA Modules:
  0.0 85.1 jit_solution(13078903888115873973)
XLA Ops:
  0.0 2.6 %opening.1 = (bf16[8,8,512]{2,1,0:T(8,128)(2,1)}, bf16[512,512]{1,0:T(8,128)(2,1)}) custom-call(bf16[512,1024]{1,0:T(8,128)(2,1)} %vir_hbm.1, bf16[8,512]{1,0:T(8,128)(2,1)} %occ_ref.1), custom_call_target="tpu_custom_call" | custom-call | tf_op jit(solution)/shard_map/opening/pallas_call | solution.py:315
  2.6 3.0 %collective-permute-start.1 = (bf16[512,512]{1,0:T(8,128)(2,1)}, bf16[512,512]{1,0:T(8,128)(2,1)S(1)}, u32[]{:S(2)}, u32[]{:S(2)}) collective-permute-start(bf16[512,512]{1,0:T(8,128)(2,1)} %get-tuple-element.16.refs_1_), channel_id=1, source_target_pairs={{0,16},{4,12},{8,24},{12,4},{16,0},{20,28},{24,8},{28,20},{1,17},{... | collective-permute-start | bytes 1572872 | tf_op jit(solution)/shard_map/ppermute | solution.py:342
  5.6 1.5 %collective-permute-start = (bf16[512,512]{1,0:T(8,128)(2,1)}, bf16[512,512]{1,0:T(8,128)(2,1)S(1)}, u32[]{:S(2)}, u32[]{:S(2)}) collective-permute-start(bf16[512,512]{1,0:T(8,128)(2,1)} %get-tuple-element.16.refs_1_), channel_id=1, source_target_pairs={{0,8},{4,20},{8,0},{12,28},{16,24},{20,4},{24,16},{28,12},{1,9},{5... | collective-permute-start | bytes 1572872 | tf_op jit(solution)/shard_map/ppermute | solution.py:342
  7.1 3.4 %all-to-all-start = ((bf16[8,8,512]{2,1,0:T(8,128)(2,1)}), bf16[8,8,512]{2,1,0:T(8,128)(2,1)S(1)}, u32[]{:S(2)}, u32[]{:S(2)}) async-start(bf16[8,8,512]{2,1,0:T(8,128)(2,1)} %get-tuple-element.15), calls=%async_computation | async-start | bytes 131072 | tf_op jit(solution)/shard_map/all_to_all | solution.py:345
  11.1 0.8 pad_add_fusion.index_ref
  11.9 7.7 %all-to-all-done.occ_ref = bf16[8,8,512]{2,1,0:T(8,128)(2,1)S(1)} async-done(((bf16[8,8,512]{2,1,0:T(8,128)(2,1)}), bf16[8,8,512]{2,1,0:T(8,128)(2,1)S(1)}, u32[]{:S(2)}, u32[]{:S(2)}) %all-to-all-start) | async-done | bytes 65568 | tf_op jit(solution)/shard_map/all_to_all | solution.py:345
  19.6 0.0 collective-permute-done.1.refs_3_
  19.6 0.0 collective-permute-done.refs_2_
  19.6 0.0 copy-start
  19.6 6.1 %half_transform.1 = bf16[8,400,128]{2,1,0:T(8,128)(2,1)} custom-call(s32[37]{0:T(128)S(1)} %pad_add_fusion.index_ref, bf16[8,8,512]{2,1,0:T(8,128)(2,1)S(1)} %all-to-all-done.occ_ref, bf16[12,32,128,128]{3,2,1,0:T(8,128)(2,1)} %bitcast.16), custom_call_target="tpu_custom_call" | custom-call | flops 201326592 | bytes 12582912 | tf_op jit(solution)/shard_map/half_transform/pallas_call | solution.py:91
  25.8 0.1 collective-permute-start.2
  25.8 4.8 %all-to-all-start.1 = ((bf16[8,400,128]{2,1,0:T(8,128)(2,1)}), bf16[8,400,128]{2,1,0:T(8,128)(2,1)S(1)}, u32[]{:S(2)}, u32[]{:S(2)}) async-start(bf16[8,400,128]{2,1,0:T(8,128)(2,1)} %half_transform.1), calls=%async_computation.1 | async-start | bytes 1638400 | tf_op jit(solution)/shard_map/all_to_all | solution.py:358
  30.6 2.3 %collective-permute-start.3 = (bf16[512,512]{1,0:T(8,128)(2,1)S(1)}, bf16[512,512]{1,0:T(8,128)(2,1)}, u32[]{:S(2)}, u32[]{:S(2)}) collective-permute-start(bf16[512,512]{1,0:T(8,128)(2,1)S(1)} %collective-permute-done.refs_2_), channel_id=1, source_target_pairs={{0,16},{4,12},{8,24},{12,4},{16,0},{20,28},{24,8},{28,20},{1,17},{... | collective-permute-start | bytes 1572872 | tf_op jit(solution)/shard_map/ppermute | solution.py:342
  32.9 0.0 copy-done
  32.9 0.0 collective-permute-start.4
  32.9 0.5 collective-permute-start.5
  33.4 0.0 collective-permute-start.6
  33.4 14.9 %collective-permute-done.3.refs_4_ = bf16[512,512]{1,0:T(8,128)(2,1)} collective-permute-done((bf16[512,512]{1,0:T(8,128)(2,1)S(1)}, bf16[512,512]{1,0:T(8,128)(2,1)}, u32[]{:S(2)}, u32[]{:S(2)}) %collective-permute-start.3) | collective-permute-done | bytes 524320 | tf_op jit(solution)/shard_map/ppermute | solution.py:342
  48.3 0.1 collective-permute-start.7
  48.4 0.0 all-to-all-done.1.refs_0_
  48.4 0.0 collective-permute-done.2
  48.4 3.5 %all-to-all-start.2 = ((bf16[8,400,128]{2,1,0:T(8,128)(2,1)}), bf16[8,400,128]{2,1,0:T(8,128)(2,1)S(1)}, u32[]{:S(2)}, u32[]{:S(2)}) async-start(bf16[8,400,128]{2,1,0:T(8,128)(2,1)} %collective-permute-done.2), calls=%async_computation.2 | async-start | bytes 1638400 | tf_op jit(solution)/shard_map/all_to_all | solution.py:360
  52.0 0.1 stack.43.where_ref
  52.1 0.0 collective-permute-done.4.refs_5_
  52.1 0.0 collective-permute-done.6.refs_7_
  52.1 0.0 collective-permute-done.5.refs_6_
  52.1 0.0 collective-permute-done.7.refs_8_
  52.1 4.5 %send_part.2 = bf16[1,256,512]{2,1,0:T(8,128)(2,1)} custom-call(s32[10]{0:T(128)S(1)} %stack.43.where_ref, bf16[8,400,128]{2,1,0:T(8,128)(2,1)S(1)} %all-to-all-done.1.refs_0_, bf16[512,512]{1,0:T(8,128)(2,1)S(1)} %copy-done, bf16[512,512]{1,0:T(8,128)(2,1)S(1)} %collective-permute-done.refs_2_, bf16[512,512]{1,0:T(8,128)(2,1)S(1)} %collective-permute-done.1.refs_3_, ...), custom_call_target="tpu_custom_call" | custom-call | flops 2147483648 | bytes 2916352 | tf_op jit(solution)/shard_map/send_part/pallas_call | solution.py:224
  56.6 3.3 %collective-permute-start.9 = (bf16[1,256,512]{2,1,0:T(8,128)(2,1)}, bf16[1,256,512]{2,1,0:T(8,128)(2,1)S(1)}, u32[]{:S(2)}, u32[]{:S(2)}) collective-permute-start(bf16[1,256,512]{2,1,0:T(8,128)(2,1)} %send_part.2), channel_id=1, source_target_pairs={{0,2},{1,3},{2,0},{3,1},{4,6},{5,7},{6,4},{7,5},{8,10},{9,11},{10,... | collective-permute-start | bytes 786440 | tf_op jit(solution)/shard_map/ppermute | solution.py:339
  59.9 5.0 %all-to-all-done.2.refs_0_ = bf16[8,400,128]{2,1,0:T(8,128)(2,1)S(1)} async-done(((bf16[8,400,128]{2,1,0:T(8,128)(2,1)}), bf16[8,400,128]{2,1,0:T(8,128)(2,1)S(1)}, u32[]{:S(2)}, u32[]{:S(2)}) %all-to-all-start.2) | async-done | bytes 819232 | tf_op jit(solution)/shard_map/all_to_all | solution.py:360
  64.9 4.0 %send_part.3 = bf16[1,256,512]{2,1,0:T(8,128)(2,1)S(1)} custom-call(s32[10]{0:T(128)S(1)} %stack.43.where_ref, bf16[8,400,128]{2,1,0:T(8,128)(2,1)S(1)} %all-to-all-done.2.refs_0_, bf16[512,512]{1,0:T(8,128)(2,1)S(1)} %copy-done, bf16[512,512]{1,0:T(8,128)(2,1)S(1)} %collective-permute-done.refs_2_, bf16[512,512]{1,0:T(8,128)(2,1)S(1)} %collective-permute-done.1.refs_3_, ...), custom_call_target="tpu_custom_call" | custom-call | flops 2147483648 | bytes 2916352 | tf_op jit(solution)/shard_map/send_part/pallas_call | solution.py:224
  68.9 2.2 %collective-permute-start.8 = (bf16[1,256,512]{2,1,0:T(8,128)(2,1)S(1)}, bf16[1,256,512]{2,1,0:T(8,128)(2,1)S(1)}, u32[]{:S(2)}, u32[]{:S(2)}) collective-permute-start(bf16[1,256,512]{2,1,0:T(8,128)(2,1)S(1)} %send_part.3), channel_id=1, source_target_pairs={{0,2},{1,3},{2,0},{3,1},{4,6},{5,7},{6,4},{7,5},{8,10},{9,11},{10,... | collective-permute-start | bytes 786440 | tf_op jit(solution)/shard_map/ppermute | solution.py:339
  71.1 4.6 %own_part.2.refs_9_ = f32[256,2048]{1,0:T(8,128)} custom-call(s32[10]{0:T(128)S(1)} %stack.43.where_ref, bf16[8,400,128]{2,1,0:T(8,128)(2,1)S(1)} %all-to-all-done.1.refs_0_, bf16[512,512]{1,0:T(8,128)(2,1)S(1)} %copy-done, bf16[512,512]{1,0:T(8,128)(2,1)S(1)} %collective-permute-done.refs_2_, bf16[512,512]{1,0:T(8,128)(2,1)S(1)} %collective-permute-done.1.refs_3_, ...), custom_call_target="tpu_custom_call" | custom-call | flops 2147483648 | bytes 2916352 | tf_op jit(solution)/shard_map/own_part/pallas_call | solution.py:224
  75.8 4.9 %own_part.3._ = f32[256,2048]{1,0:T(8,128)} custom-call(s32[10]{0:T(128)S(1)} %stack.43.where_ref, bf16[8,400,128]{2,1,0:T(8,128)(2,1)S(1)} %all-to-all-done.2.refs_0_, bf16[512,512]{1,0:T(8,128)(2,1)S(1)} %copy-done, bf16[512,512]{1,0:T(8,128)(2,1)S(1)} %collective-permute-done.refs_2_, ...), custom_call_target="tpu_custom_call", output_to_operand_aliasing={{}: (10, {})} | custom-call | flops 2147483648 | bytes 2916352 | tf_op jit(solution)/shard_map/own_part/pallas_call | solution.py:224
  80.7 0.0 collective-permute-done.9.got_ref
  80.7 1.4 %place.2._ = f32[256,2048]{1,0:T(8,128)} custom-call(s32[10]{0:T(128)S(1)} %stack.43.where_ref, bf16[1,256,512]{2,1,0:T(8,128)(2,1)S(1)} %collective-permute-done.9.got_ref, f32[256,2048]{1,0:T(8,128)} %own_part.3._), custom_call_target="tpu_custom_call", output_to_operand_aliasing={{}: (2, {})} | custom-call | bytes 786432 | tf_op jit(solution)/shard_map/place/pallas_call | solution.py:268
  82.1 1.6 %collective-permute-done.8.got_ref = bf16[1,256,512]{2,1,0:T(8,128)(2,1)S(1)} collective-permute-done((bf16[1,256,512]{2,1,0:T(8,128)(2,1)S(1)}, bf16[1,256,512]{2,1,0:T(8,128)(2,1)S(1)}, u32[]{:S(2)}, u32[]{:S(2)}) %collective-permute-start.8) | collective-permute-done | bytes 262176 | tf_op jit(solution)/shard_map/ppermute | solution.py:339
  83.7 1.4 %place.3 = f32[256,2048]{1,0:T(8,128)} custom-call(s32[10]{0:T(128)S(1)} %stack.43.where_ref, bf16[1,256,512]{2,1,0:T(8,128)(2,1)S(1)} %collective-permute-done.8.got_ref, f32[256,2048]{1,0:T(8,128)} %place.2._), custom_call_target="tpu_custom_call", output_to_operand_aliasing={{}: (2, {})} | custom-call | bytes 786432 | tf_op jit(solution)/shard_map/place/pallas_call | solution.py:268
Async XLA Ops:
  2.6 17.0 %collective-permute-start.1 = (bf16[512,512]{1,0:T(8,128)(2,1)}, bf16[512,512]{1,0:T(8,128)(2,1)S(1)}, u32[]{:S(2)}, u32[]{:S(2)}) collective-permute-start(bf16[512,512]{1,0:T(8,128)(2,1)} %get-tuple-element.16.refs_1_), channel_id=1, source_target_pairs={{0,16},{4,12},{8,24},{12,4},{16,0},{20,28},{24,8},{28,20},{1,17},{... | collective-permute-start | bytes 1572872 | tf_op jit(solution)/shard_map/ppermute | solution.py:342
  5.6 14.0 %collective-permute-start = (bf16[512,512]{1,0:T(8,128)(2,1)}, bf16[512,512]{1,0:T(8,128)(2,1)S(1)}, u32[]{:S(2)}, u32[]{:S(2)}) collective-permute-start(bf16[512,512]{1,0:T(8,128)(2,1)} %get-tuple-element.16.refs_1_), channel_id=1, source_target_pairs={{0,8},{4,20},{8,0},{12,28},{16,24},{20,4},{24,16},{28,12},{1,9},{5... | collective-permute-start | bytes 1572872 | tf_op jit(solution)/shard_map/ppermute | solution.py:342
  7.1 12.5 %all-to-all-start = ((bf16[8,8,512]{2,1,0:T(8,128)(2,1)}), bf16[8,8,512]{2,1,0:T(8,128)(2,1)S(1)}, u32[]{:S(2)}, u32[]{:S(2)}) async-start(bf16[8,8,512]{2,1,0:T(8,128)(2,1)} %get-tuple-element.15), calls=%async_computation | async-start | bytes 131072 | tf_op jit(solution)/shard_map/all_to_all | solution.py:345
  19.6 13.3 %copy-start = (bf16[512,512]{1,0:T(8,128)(2,1)S(1)}, bf16[512,512]{1,0:T(8,128)(2,1)}, u32[]{:S(2)}) copy-start(bf16[512,512]{1,0:T(8,128)(2,1)} %get-tuple-element.16.refs_1_) | copy-start | bytes 1572868
  25.8 22.7 %collective-permute-start.2 = (bf16[8,400,128]{2,1,0:T(8,128)(2,1)}, bf16[8,400,128]{2,1,0:T(8,128)(2,1)}, u32[]{:S(2)}, u32[]{:S(2)}) collective-permute-start(bf16[8,400,128]{2,1,0:T(8,128)(2,1)} %half_transform.1), channel_id=1, source_target_pairs={{0,1},{1,0},{2,3},{3,2},{4,5},{5,4},{6,7},{7,6},{8,9},{9,8},{10,11... | collective-permute-start | bytes 2457608 | tf_op jit(solution)/shard_map/ppermute | solution.py:339
  25.8 22.6 %all-to-all-start.1 = ((bf16[8,400,128]{2,1,0:T(8,128)(2,1)}), bf16[8,400,128]{2,1,0:T(8,128)(2,1)S(1)}, u32[]{:S(2)}, u32[]{:S(2)}) async-start(bf16[8,400,128]{2,1,0:T(8,128)(2,1)} %half_transform.1), calls=%async_computation.1 | async-start | bytes 1638400 | tf_op jit(solution)/shard_map/all_to_all | solution.py:358
  30.6 17.7 %collective-permute-start.3 = (bf16[512,512]{1,0:T(8,128)(2,1)S(1)}, bf16[512,512]{1,0:T(8,128)(2,1)}, u32[]{:S(2)}, u32[]{:S(2)}) collective-permute-start(bf16[512,512]{1,0:T(8,128)(2,1)S(1)} %collective-permute-done.refs_2_), channel_id=1, source_target_pairs={{0,16},{4,12},{8,24},{12,4},{16,0},{20,28},{24,8},{28,20},{1,17},{... | collective-permute-start | bytes 1572872 | tf_op jit(solution)/shard_map/ppermute | solution.py:342
  32.9 19.2 %collective-permute-start.4 = (bf16[512,512]{1,0:T(8,128)(2,1)S(1)}, bf16[512,512]{1,0:T(8,128)(2,1)}, u32[]{:S(2)}, u32[]{:S(2)}) collective-permute-start(bf16[512,512]{1,0:T(8,128)(2,1)S(1)} %copy-done), channel_id=1, source_target_pairs={{0,4},{4,0},{8,12},{12,8},{16,20},{20,16},{24,28},{28,24},{1,5},{5... | collective-permute-start | bytes 1572872 | tf_op jit(solution)/shard_map/ppermute | solution.py:342
  32.9 19.2 %collective-permute-start.5 = (bf16[512,512]{1,0:T(8,128)(2,1)S(1)}, bf16[512,512]{1,0:T(8,128)(2,1)}, u32[]{:S(2)}, u32[]{:S(2)}) collective-permute-start(bf16[512,512]{1,0:T(8,128)(2,1)S(1)} %collective-permute-done.refs_2_), channel_id=1, source_target_pairs={{0,4},{4,0},{8,12},{12,8},{16,20},{20,16},{24,28},{28,24},{1,5},{5... | collective-permute-start | bytes 1572872 | tf_op jit(solution)/shard_map/ppermute | solution.py:342
  33.4 18.7 %collective-permute-start.6 = (bf16[512,512]{1,0:T(8,128)(2,1)S(1)}, bf16[512,512]{1,0:T(8,128)(2,1)}, u32[]{:S(2)}, u32[]{:S(2)}) collective-permute-start(bf16[512,512]{1,0:T(8,128)(2,1)S(1)} %collective-permute-done.1.refs_3_), channel_id=1, source_target_pairs={{0,4},{4,0},{8,12},{12,8},{16,20},{20,16},{24,28},{28,24},{1,5},{5... | collective-permute-start | bytes 1572872 | tf_op jit(solution)/shard_map/ppermute | solution.py:342
  48.3 3.8 %collective-permute-start.7 = (bf16[512,512]{1,0:T(8,128)(2,1)}, bf16[512,512]{1,0:T(8,128)(2,1)}, u32[]{:S(2)}, u32[]{:S(2)}) collective-permute-start(bf16[512,512]{1,0:T(8,128)(2,1)} %collective-permute-done.3.refs_4_), channel_id=1, source_target_pairs={{0,4},{4,0},{8,12},{12,8},{16,20},{20,16},{24,28},{28,24},{1,5},{5... | collective-permute-start | bytes 1572872 | tf_op jit(solution)/shard_map/ppermute | solution.py:342
  48.4 16.4 %all-to-all-start.2 = ((bf16[8,400,128]{2,1,0:T(8,128)(2,1)}), bf16[8,400,128]{2,1,0:T(8,128)(2,1)S(1)}, u32[]{:S(2)}, u32[]{:S(2)}) async-start(bf16[8,400,128]{2,1,0:T(8,128)(2,1)} %collective-permute-done.2), calls=%async_computation.2 | async-start | bytes 1638400 | tf_op jit(solution)/shard_map/all_to_all | solution.py:360
  56.6 24.1 %collective-permute-start.9 = (bf16[1,256,512]{2,1,0:T(8,128)(2,1)}, bf16[1,256,512]{2,1,0:T(8,128)(2,1)S(1)}, u32[]{:S(2)}, u32[]{:S(2)}) collective-permute-start(bf16[1,256,512]{2,1,0:T(8,128)(2,1)} %send_part.2), channel_id=1, source_target_pairs={{0,2},{1,3},{2,0},{3,1},{4,6},{5,7},{6,4},{7,5},{8,10},{9,11},{10,... | collective-permute-start | bytes 786440 | tf_op jit(solution)/shard_map/ppermute | solution.py:339
  68.9 14.8 %collective-permute-start.8 = (bf16[1,256,512]{2,1,0:T(8,128)(2,1)S(1)}, bf16[1,256,512]{2,1,0:T(8,128)(2,1)S(1)}, u32[]{:S(2)}, u32[]{:S(2)}) collective-permute-start(bf16[1,256,512]{2,1,0:T(8,128)(2,1)S(1)} %send_part.3), channel_id=1, source_target_pairs={{0,2},{1,3},{2,0},{3,1},{4,6},{5,7},{6,4},{7,5},{8,10},{9,11},{10,... | collective-permute-start | bytes 786440 | tf_op jit(solution)/shard_map/ppermute | solution.py:339

commit v4 on v3

--- a/solution.py
+++ b/solution.py
@@ -22,12 +22,11 @@
     return k * pb + (META if k >= kmax // 2 else 0)
 
 
-def half_kernel(index_ref, occ_ref, tiles_hbm, half_ref, tile_ref, stage_ref, sems):
+def half_kernel(rows_ref, cols_ref, aux_ref, count_ref, occ_ref, tiles_hbm, half_ref, tile_ref, stage_ref, sems):
     kmax, pb, blk, _ = tile_ref.shape
-    rows_ref, cols_ref, aux_ref = (index_ref.at[pl.ds(n * kmax, kmax)] for n in range(3))
     orbitals = half_ref.shape[0]
     ao_blocks = occ_ref.shape[2] // blk
-    count = index_ref[3 * kmax]
+    count = count_ref[0]
 
     def fetch(k):
         return pltpu.make_async_copy(tiles_hbm.at[k], tile_ref.at[k], sems.at[k])
@@ -38,17 +37,19 @@
         def _():
             fetch(k).start()
 
+    targets = []
+    for k in range(kmax):
+        target = jnp.int32(k)
+        for j in reversed(range(k)):
+            same = jnp.logical_and(cols_ref[j] == cols_ref[k], aux_ref[j] == aux_ref[k])
+            target = jnp.where(same, j, target)
+        targets.append(target)
     lanes = lax.broadcasted_iota(jnp.int32, (META, blk), 1)
     meta = jnp.zeros((META, blk), jnp.int32)
     for k in range(kmax):
-        again = jnp.bool_(False)
-        for j in range(k):
-            same = jnp.logical_and(cols_ref[j] == cols_ref[k], aux_ref[j] == aux_ref[k])
-            again = jnp.logical_or(again, same)
-        again = jnp.logical_and(again, k < count)
-        row = aux_ref[k] * pb
-        first = jnp.where(jnp.logical_or(again, k >= count), PDEV, row)
-        for n, value in enumerate((first, cols_ref[k] * blk, again.astype(jnp.int32), row)):
+        kept = jnp.logical_and(k < count, targets[k] == k)
+        row = jnp.where(kept, aux_ref[k] * pb, PDEV)
+        for n, value in enumerate((row, cols_ref[k] * blk)):
             meta = jnp.where(lanes == n * FIELD + k, value, meta)
     meta = meta.astype(jnp.float32).astype(jnp.bfloat16)
     split = kmax // 2 * pb
@@ -67,54 +68,67 @@
             upper = jnp.concatenate([occ, zero], axis=1)
             lower = jnp.concatenate([zero, occ], axis=1)
             pair = jnp.concatenate([upper, lower], axis=0).astype(jnp.bfloat16)
-            stage = stage_ref.at[k % 2]
             fetch(k).wait()
+            stage = stage_ref.at[k]
             for p in range(0, pb, 2):
                 rhs = tile_ref[k, p : p + 2].reshape(2 * blk, blk)
-                stage[p * orbitals : (p + 2) * orbitals, :] = jnp.dot(
-                    pair, rhs, preferred_element_type=jnp.float32
+                part = jnp.dot(pair, rhs, preferred_element_type=jnp.float32)
+                stage[p * orbitals : (p + 2) * orbitals, :] = part.astype(jnp.bfloat16).astype(
+                    jnp.float32
                 )
             for i in range(orbitals):
-                part = stage[pl.ds(i, pb, stride=orbitals), :].astype(jnp.bfloat16)
-                half_ref[i, at : at + pb, :] = part
+                half_ref[i, at : at + pb, :] = stage[
+                    pl.ds(i, pb, stride=orbitals), :
+                ].astype(jnp.bfloat16)
+
+        if k:
+
+            @pl.when(jnp.logical_and(k < count, targets[k] < k))
+            def _(k=k):
+                target = targets[k]
+                total = stage_ref.at[target]
+                total[...] += stage_ref[k]
+                start = target * pb + jnp.where(target >= kmax // 2, META, 0)
+                start = pl.multiple_of(start, META)
+                for i in range(orbitals):
+                    half_ref[i, pl.ds(start, pb), :] = total[
+                        pl.ds(i, pb, stride=orbitals), :
+                    ].astype(jnp.bfloat16)
 
         @pl.when(k >= count)
         def _(at=at):
-            empty = jnp.zeros((orbitals, pb, blk), jnp.bfloat16)
-            half_ref[:, at : at + pb, :] = empty
-
-
-def half_transform(tiles, index, occ):
+            half_ref[:, at : at + pb, :] = jnp.zeros((orbitals, pb, blk), jnp.bfloat16)
+
+
+def half_transform(tiles, rows, cols, auxs, count, occ):
     kmax, pb, blk, _ = tiles.shape
     orbitals = occ.shape[1]
     out = (orbitals, kmax * pb + META, blk)
+    scalars = pl.BlockSpec(memory_space=pltpu.SMEM)
     return pl.pallas_call(
         half_kernel,
-        grid_spec=pltpu.PrefetchScalarGridSpec(
-            num_scalar_prefetch=1,
-            grid=(1,),
-            in_specs=[whole(occ.shape), pl.BlockSpec(memory_space=pl.ANY)],
-            out_specs=whole(out),
-            scratch_shapes=[
-                pltpu.VMEM(tiles.shape, jnp.bfloat16),
-                pltpu.VMEM((2, pb * orbitals, blk), jnp.float32),
-                pltpu.SemaphoreType.DMA((kmax,)),
-            ],
-        ),
+        in_specs=[scalars] * 4
+        + [pl.BlockSpec(memory_space=pltpu.VMEM), pl.BlockSpec(memory_space=pl.ANY)],
+        out_specs=pl.BlockSpec(memory_space=pltpu.VMEM),
+        scratch_shapes=[
+            pltpu.VMEM(tiles.shape, jnp.bfloat16),
+            pltpu.VMEM((kmax, pb * orbitals, blk), jnp.float32),
+            pltpu.SemaphoreType.DMA((kmax,)),
+        ],
         out_shape=jax.ShapeDtypeStruct(out, jnp.bfloat16),
-        compiler_params=pltpu.CompilerParams(vmem_limit_bytes=52 << 20),
+        compiler_params=pltpu.CompilerParams(vmem_limit_bytes=56 << 20),
         cost_estimate=pl.CostEstimate(
             flops=4 * tiles.size * orbitals, bytes_accessed=tiles.size * 2, transcendentals=0
         ),
         name="half_transform",
-    )(index, occ, tiles)
+    )(rows, cols, auxs, count, occ, tiles)
 
 
 def pair_kernel(kmax, pb, group, vb, kind, inputs, side, where_ref, *refs):
     half_refs, refs = refs[:inputs], refs[inputs:]
     vir_hbm, refs = refs[:group], refs[group:]
-    vir_ref, dense_ref, sum_ref, turn_ref, meta_ref, code_ref, again_ref, sem, sems = refs[-9:]
-    results = refs[-9 - (2 if kind == "both" else 1) : -9]
+    vir_ref, dense_ref, sum_ref, turn_ref, meta_ref, code_ref, sem, sems = refs[-8:]
+    results = refs[-8 - (2 if kind == "both" else 1) : -8]
     depth = vir_hbm[0].shape[0]
     blk = meta_ref.shape[1]
     low, high = columns_for(kind, vir_ref.shape[1] if kind == "both" else vir_hbm[0].shape[1], vb)
@@ -142,52 +156,19 @@
             return half_refs[1], at - split - META
         return half_refs[0], at
 
-    def scatter(step, repeats):
+    def scatter(step, carry):
         g = where_ref[2 + step]
         for k in range(kmax):
             ref, at = source(k)
             row = pl.multiple_of(code_ref[g, k], pb)
             lane = pl.multiple_of(step * depth + code_ref[g, FIELD + k], blk)
             dense_ref[pl.ds(row, pb), pl.ds(lane, blk)] = ref[g, at : at + pb, :]
-            again_ref[repeats] = step * kmax + k
-            repeats = repeats + code_ref[g, 2 * FIELD + k]
-        return repeats
-
-    repeats = lax.fori_loop(0, group, scatter, jnp.int32(0))
+        return carry
+
+    lax.fori_loop(0, group, scatter, 0)
     for fetch in fetches:
         fetch.wait()
     sum_ref[...] = jnp.dot(dense_ref[:PDEV, :], vir_ref[...], preferred_element_type=jnp.float32)
-
-    def repeat(n, carry):
-        slot = again_ref[n]
-        step, k = slot // kmax, slot % kmax
-        g = where_ref[2 + step]
-        row = pl.multiple_of(code_ref[g, 3 * FIELD + k], pb)
-        lane = pl.multiple_of(step * depth + code_ref[g, FIELD + k], blk)
-
-        def add(ref, at):
-            sum_ref[pl.ds(row, pb), :] += jnp.dot(
-                ref[g, pl.ds(pl.multiple_of(at, META), pb), :],
-                vir_ref[pl.ds(lane, blk), :],
-                preferred_element_type=jnp.float32,
-            )
-
-        late = k >= kmax // 2
-
-        @pl.when(late)
-        def _():
-            if inputs == 2:
-                add(half_refs[1], k * pb - split)
-            else:
-                add(half_refs[0], k * pb + META)
-
-        @pl.when(jnp.logical_not(late))
-        def _():
-            add(half_refs[0], k * pb)
-
-        return carry
-
-    lax.fori_loop(0, repeats, repeat, 0)
     turn_ref[...] = sum_ref[...].T
     offset = 0
     if kind != "send":
@@ -235,7 +216,6 @@
                 pltpu.VMEM((high - low, PDEV), jnp.float32),
                 pltpu.VMEM((group, blk), jnp.int32),
                 pltpu.SMEM((group, blk), jnp.int32),
-                pltpu.SMEM((group * kmax + 1,), jnp.int32),
                 pltpu.SemaphoreType.DMA,
                 pltpu.SemaphoreType.DMA((group + 1,)),
             ],
@@ -347,14 +327,16 @@
     core = lax.axis_index("grp") % 2
     near = hop(own, (2, 4))
     far = hop(own, (4, 2))
-    occ, near, far = lax.optimization_barrier((occ, near, far))
+    occ, near = lax.optimization_barrier((occ, near))
     across = hop(near, (4, 2))
+    halves = half_transform(
+        integral_tiles[0, 0], row_blocks[0, 0], col_blocks[0, 0], aux_blocks[0, 0], tile_counts[0], occ
+    )
+    others = swap(halves, 1)
+    halves, far, across = lax.optimization_barrier((halves, far, across))
     virs = [own, near, far, across]
     virs = virs + [hop(vir, (1, 1)) for vir in virs]
 
-    index = [x[0, 0] for x in (row_blocks, col_blocks, aux_blocks)] + [tile_counts[0]]
-    halves = half_transform(integral_tiles[0, 0], jnp.concatenate(index), occ)
-    others = swap(halves, 1)
     halves = lax.all_to_all(halves, "grp", split_axis=0, concat_axis=0, tiled=True)
     others, halves = lax.optimization_barrier((others, halves))
     others = lax.all_to_all(others, "grp", split_axis=0, concat_axis=0, tiled=True)

time: 85.3 us -> 81.7 us (0.958)
  starting transfers between devices: 24.7 us -> 19.8 us
  waiting for transfers between devices: 29.2 us -> 32.4 us
  Pallas kernels: 29.5 us -> 27 us
  local copies, waits for them, and re-layouts: 0.09 us -> 0.98 us
    ppermute x3, waiting for transfers between devices: 1.61 us -> 17.6 us  [swap(): return lax.ppermute(x, 'aux', [(a, a ^ step) for a in range(aux_size)])]
    ppermute x7, waiting for transfers between devices: 14.9 us -> 1.67 us  [hop(): lax.ppermute(x, 'grp', [(g, g ^ steps[g % 2]) for g in range(group_size)])]
    pallas_call x4, Pallas kernels: 18.1 us -> 15.4 us  [pair_transform(): pl.pallas_call(functools.partial(pair_kernel, kmax, pb, group, vb, kind,...]
    ppermute x3, starting transfers between devices: 5.57 us -> 2.96 us  [swap(): return lax.ppermute(x, 'aux', [(a, a ^ step) for a in range(aux_size)])]
    all_to_all x1, waiting for transfers between devices: 4.95 us -> 7.49 us  [shards(): lax.all_to_all(others, 'grp', split_axis=0, concat_axis=0, tiled=True)]
    all_to_all x1, waiting for transfers between devices: 7.75 us -> 5.63 us  [shards(): occ = lax.all_to_all(occ, 'grp', split_axis=0, concat_axis=0, tiled=True)]
    all_to_all x1, starting transfers between devices: 4.75 us -> 3.55 us  [shards(): lax.all_to_all(halves, 'grp', split_axis=0, concat_axis=0, tiled=True)]
    ppermute x7, starting transfers between devices: 7.45 us -> 6.42 us  [hop(): lax.ppermute(x, 'grp', [(g, g ^ steps[g % 2]) for g in range(group_size)])]
  transfers between devices with their start and end apart: 13 -> 13, of which waited for: 4 -> 5; matrix products, arithmetic and copies ran while one was open for 1% -> 0% of each run, Pallas kernels for 23% -> 28%
where the time goes in v4:
time: 81.7 us; the launch traced here: 81 us
  waiting for transfers between devices  32.4 us (40%)
  Pallas kernels  27 us (33%)
  starting transfers between devices  19.8 us (24%)
  local copies, waits for them, and re-layouts  0.98 us (1%)
  between operations  0.82 us (1%)
    ppermute x3, waiting for transfers between devices, swap(): return lax.ppermute(x, 'aux', [(a, a ^ step) for a in range(aux_size)])  17.6 us
    pallas_call x4, Pallas kernels, pair_transform(): pl.pallas_call(functools.partial(pair_kernel, kmax, pb, group, vb, kind,...  15.4 us
    all_to_all x1, waiting for transfers between devices, shards(): lax.all_to_all(others, 'grp', split_axis=0, concat_axis=0, tiled=True)  7.49 us
    ppermute x7, starting transfers between devices, hop(): lax.ppermute(x, 'grp', [(g, g ^ steps[g % 2]) for g in range(group_size)])  6.42 us
    pallas_call x1, Pallas kernels, half_transform(): pl.pallas_call(half_kernel, in_specs=[scalars] * 4 + [pl.BlockSpec(memory...  6.24 us
    all_to_all x1, waiting for transfers between devices, shards(): occ = lax.all_to_all(occ, 'grp', split_axis=0, concat_axis=0, tiled=True)  5.63 us
    all_to_all x1, starting transfers between devices, shards(): lax.all_to_all(halves, 'grp', split_axis=0, concat_axis=0, tiled=True)  3.55 us
    all_to_all x1, starting transfers between devices, shards(): lax.all_to_all(others, 'grp', split_axis=0, concat_axis=0, tiled=True)  3.55 us
  transfers between devices with their start and end apart: 13, of which 5 were waited for; matrix products, arithmetic and copies ran while one was open for 0% of the time, Pallas kernels for 28%

profile of v4, /device:TPU:0, one launch (start us, length us, event | category | flops | bytes accessed | tf_op | source)
XLA Modules:
  0.0 81.0 jit_solution(7975947341044127903)
XLA Ops:
  0.0 2.6 %opening.1 = (bf16[8,8,512]{2,1,0:T(8,128)(2,1)}, bf16[512,512]{1,0:T(8,128)(2,1)}) custom-call(bf16[512,1024]{1,0:T(8,128)(2,1)} %vir_hbm.1, bf16[8,512]{1,0:T(8,128)(2,1)} %occ_ref.1), custom_call_target="tpu_custom_call" | custom-call | tf_op jit(solution)/shard_map/opening/pallas_call | solution.py:295
  2.6 3.0 %collective-permute-start = (bf16[512,512]{1,0:T(8,128)(2,1)}, bf16[512,512]{1,0:T(8,128)(2,1)S(1)}, u32[]{:S(2)}, u32[]{:S(2)}) collective-permute-start(bf16[512,512]{1,0:T(8,128)(2,1)} %get-tuple-element.18.refs_1_), channel_id=1, source_target_pairs={{0,8},{4,20},{8,0},{12,28},{16,24},{20,4},{24,16},{28,12},{1,9},{5... | collective-permute-start | bytes 1572872 | tf_op jit(solution)/shard_map/ppermute | solution.py:322
  5.6 3.4 %all-to-all-start = ((bf16[8,8,512]{2,1,0:T(8,128)(2,1)}), bf16[8,8,512]{2,1,0:T(8,128)(2,1)S(1)}, u32[]{:S(2)}, u32[]{:S(2)}) async-start(bf16[8,8,512]{2,1,0:T(8,128)(2,1)} %get-tuple-element.17), calls=%async_computation | async-start | bytes 131072 | tf_op jit(solution)/shard_map/all_to_all | solution.py:325
  8.9 1.9 %collective-permute-start.2 = (bf16[512,512]{1,0:T(8,128)(2,1)}, bf16[512,512]{1,0:T(8,128)(2,1)S(1)}, u32[]{:S(2)}, u32[]{:S(2)}) collective-permute-start(bf16[512,512]{1,0:T(8,128)(2,1)} %get-tuple-element.18.refs_1_), channel_id=1, source_target_pairs={{0,16},{4,12},{8,24},{12,4},{16,0},{20,28},{24,8},{28,20},{1,17},{... | collective-permute-start | bytes 1572872 | tf_op jit(solution)/shard_map/ppermute | solution.py:322
  10.9 5.6 %all-to-all-done.occ_ref = bf16[8,8,512]{2,1,0:T(8,128)(2,1)S(1)} async-done(((bf16[8,8,512]{2,1,0:T(8,128)(2,1)}), bf16[8,8,512]{2,1,0:T(8,128)(2,1)S(1)}, u32[]{:S(2)}, u32[]{:S(2)}) %all-to-all-start) | async-done | bytes 65568 | tf_op jit(solution)/shard_map/all_to_all | solution.py:325
  16.5 0.0 copy-start.2
  16.5 0.0 collective-permute-done.refs_2_
  16.5 0.4 collective-permute-start.3
  17.6 0.0 copy-done.2
  17.6 0.0 copy-start
  17.6 6.2 %half_transform.1 = bf16[8,400,128]{2,1,0:T(8,128)(2,1)} custom-call(s32[12]{0:T(128)} %bitcast.17, s32[12]{0:T(128)} %bitcast.18, s32[12]{0:T(128)} %bitcast.19, s32[1]{0:T(128)} %bitcast.15.count_ref, bf16[8,8,512]{2,1,0:T(8,128)(2,1)} %copy-done.2, bf16[12,32,128,128]{3,2,1,0:T(8,128)(2,1)} %bitcast.16), custom_call_target="tpu_custom_call" | custom-call | flops 201326592 | bytes 12582912 | tf_op jit(solution)/shard_map/half_transform/pallas_call | solution.py:108
  23.8 0.3 collective-permute-start.1
  24.1 0.0 collective-permute-done.2.refs_3_
  24.2 1.7 %collective-permute-done.3.refs_4_ = bf16[512,512]{1,0:T(8,128)(2,1)} collective-permute-done((bf16[512,512]{1,0:T(8,128)(2,1)S(1)}, bf16[512,512]{1,0:T(8,128)(2,1)}, u32[]{:S(2)}, u32[]{:S(2)}) %collective-permute-start.3) | collective-permute-done | bytes 524320 | tf_op jit(solution)/shard_map/ppermute | solution.py:322
  25.8 3.5 %all-to-all-start.1 = ((bf16[8,400,128]{2,1,0:T(8,128)(2,1)}), bf16[8,400,128]{2,1,0:T(8,128)(2,1)S(1)}, u32[]{:S(2)}, u32[]{:S(2)}) async-start(bf16[8,400,128]{2,1,0:T(8,128)(2,1)} %half_transform.1), calls=%async_computation.1 | async-start | bytes 1638400 | tf_op jit(solution)/shard_map/all_to_all | solution.py:340
  29.4 0.0 copy-done
  29.4 0.4 collective-permute-start.4
  29.8 0.2 collective-permute-start.5
  30.0 0.3 collective-permute-start.6
  30.3 0.2 collective-permute-start.7
  30.5 14.5 %collective-permute-done.1 = bf16[8,400,128]{2,1,0:T(8,128)(2,1)S(1)} collective-permute-done((bf16[8,400,128]{2,1,0:T(8,128)(2,1)}, bf16[8,400,128]{2,1,0:T(8,128)(2,1)S(1)}, u32[]{:S(2)}, u32[]{:S(2)}) %collective-permute-start.1) | collective-permute-done | bytes 819232 | tf_op jit(solution)/shard_map/ppermute | solution.py:319
  44.9 0.0 copy-start.1
  44.9 0.9 %copy-done.1 = bf16[8,400,128]{2,1,0:T(8,128)(2,1)} copy-done((bf16[8,400,128]{2,1,0:T(8,128)(2,1)}, bf16[8,400,128]{2,1,0:T(8,128)(2,1)S(1)}, u32[]{:S(2)}) %copy-start.1) | copy-done | bytes 819224
  45.8 0.0 all-to-all-done.1.refs_0_
  45.8 3.5 %all-to-all-start.2 = ((bf16[8,400,128]{2,1,0:T(8,128)(2,1)}), bf16[8,400,128]{2,1,0:T(8,128)(2,1)S(1)}, u32[]{:S(2)}, u32[]{:S(2)}) async-start(bf16[8,400,128]{2,1,0:T(8,128)(2,1)} %copy-done.1), calls=%async_computation.2 | async-start | bytes 1638400 | tf_op jit(solution)/shard_map/all_to_all | solution.py:342
  49.4 0.1 stack.43.where_ref
  49.5 0.0 collective-permute-done.4.refs_5_
  49.5 0.0 collective-permute-done.5.refs_6_
  49.5 0.0 collective-permute-done.6.refs_7_
  49.5 0.0 collective-permute-done.7.refs_8_
  49.5 4.0 %send_part.2 = bf16[1,256,512]{2,1,0:T(8,128)(2,1)} custom-call(s32[10]{0:T(128)S(1)} %stack.43.where_ref, bf16[8,400,128]{2,1,0:T(8,128)(2,1)S(1)} %all-to-all-done.1.refs_0_, bf16[512,512]{1,0:T(8,128)(2,1)S(1)} %copy-done, bf16[512,512]{1,0:T(8,128)(2,1)S(1)} %collective-permute-done.refs_2_, bf16[512,512]{1,0:T(8,128)(2,1)S(1)} %collective-permute-done.2.refs_3_, ...), custom_call_target="tpu_custom_call" | custom-call | flops 2147483648 | bytes 2916352 | tf_op jit(solution)/shard_map/send_part/pallas_call | solution.py:205
  53.5 1.3 %collective-permute-start.9 = (bf16[1,256,512]{2,1,0:T(8,128)(2,1)}, bf16[1,256,512]{2,1,0:T(8,128)(2,1)S(1)}, u32[]{:S(2)}, u32[]{:S(2)}) collective-permute-start(bf16[1,256,512]{2,1,0:T(8,128)(2,1)} %send_part.2), channel_id=1, source_target_pairs={{0,2},{1,3},{2,0},{3,1},{4,6},{5,7},{6,4},{7,5},{8,10},{9,11},{10,... | collective-permute-start | bytes 786440 | tf_op jit(solution)/shard_map/ppermute | solution.py:319
  54.8 7.5 %all-to-all-done.2.refs_0_ = bf16[8,400,128]{2,1,0:T(8,128)(2,1)S(1)} async-done(((bf16[8,400,128]{2,1,0:T(8,128)(2,1)}), bf16[8,400,128]{2,1,0:T(8,128)(2,1)S(1)}, u32[]{:S(2)}, u32[]{:S(2)}) %all-to-all-start.2) | async-done | bytes 819232 | tf_op jit(solution)/shard_map/all_to_all | solution.py:342
  62.3 3.3 %send_part.3 = bf16[1,256,512]{2,1,0:T(8,128)(2,1)S(1)} custom-call(s32[10]{0:T(128)S(1)} %stack.43.where_ref, bf16[8,400,128]{2,1,0:T(8,128)(2,1)S(1)} %all-to-all-done.2.refs_0_, bf16[512,512]{1,0:T(8,128)(2,1)S(1)} %copy-done, bf16[512,512]{1,0:T(8,128)(2,1)S(1)} %collective-permute-done.refs_2_, bf16[512,512]{1,0:T(8,128)(2,1)S(1)} %collective-permute-done.2.refs_3_, ...), custom_call_target="tpu_custom_call" | custom-call | flops 2147483648 | bytes 2916352 | tf_op jit(solution)/shard_map/send_part/pallas_call | solution.py:205
  65.5 1.4 %collective-permute-start.8 = (bf16[1,256,512]{2,1,0:T(8,128)(2,1)S(1)}, bf16[1,256,512]{2,1,0:T(8,128)(2,1)S(1)}, u32[]{:S(2)}, u32[]{:S(2)}) collective-permute-start(bf16[1,256,512]{2,1,0:T(8,128)(2,1)S(1)} %send_part.3), channel_id=1, source_target_pairs={{0,2},{1,3},{2,0},{3,1},{4,6},{5,7},{6,4},{7,5},{8,10},{9,11},{10,... | collective-permute-start | bytes 786440 | tf_op jit(solution)/shard_map/ppermute | solution.py:319
  66.9 4.1 %own_part.2.refs_9_ = f32[256,2048]{1,0:T(8,128)} custom-call(s32[10]{0:T(128)S(1)} %stack.43.where_ref, bf16[8,400,128]{2,1,0:T(8,128)(2,1)S(1)} %all-to-all-done.1.refs_0_, bf16[512,512]{1,0:T(8,128)(2,1)S(1)} %copy-done, bf16[512,512]{1,0:T(8,128)(2,1)S(1)} %collective-permute-done.refs_2_, bf16[512,512]{1,0:T(8,128)(2,1)S(1)} %collective-permute-done.2.refs_3_, ...), custom_call_target="tpu_custom_call" | custom-call | flops 2147483648 | bytes 2916352 | tf_op jit(solution)/shard_map/own_part/pallas_call | solution.py:205
  71.0 4.1 %own_part.3._ = f32[256,2048]{1,0:T(8,128)} custom-call(s32[10]{0:T(128)S(1)} %stack.43.where_ref, bf16[8,400,128]{2,1,0:T(8,128)(2,1)S(1)} %all-to-all-done.2.refs_0_, bf16[512,512]{1,0:T(8,128)(2,1)S(1)} %copy-done, bf16[512,512]{1,0:T(8,128)(2,1)S(1)} %collective-permute-done.refs_2_, ...), custom_call_target="tpu_custom_call", output_to_operand_aliasing={{}: (10, {})} | custom-call | flops 2147483648 | bytes 2916352 | tf_op jit(solution)/shard_map/own_part/pallas_call | solution.py:205
  75.1 0.0 collective-permute-done.9.got_ref
  75.1 1.4 %place.2._ = f32[256,2048]{1,0:T(8,128)} custom-call(s32[10]{0:T(128)S(1)} %stack.43.where_ref, bf16[1,256,512]{2,1,0:T(8,128)(2,1)S(1)} %collective-permute-done.9.got_ref, f32[256,2048]{1,0:T(8,128)} %own_part.3._), custom_call_target="tpu_custom_call", output_to_operand_aliasing={{}: (2, {})} | custom-call | bytes 786432 | tf_op jit(solution)/shard_map/place/pallas_call | solution.py:248
  76.5 3.1 %collective-permute-done.8.got_ref = bf16[1,256,512]{2,1,0:T(8,128)(2,1)S(1)} collective-permute-done((bf16[1,256,512]{2,1,0:T(8,128)(2,1)S(1)}, bf16[1,256,512]{2,1,0:T(8,128)(2,1)S(1)}, u32[]{:S(2)}, u32[]{:S(2)}) %collective-permute-start.8) | collective-permute-done | bytes 262176 | tf_op jit(solution)/shard_map/ppermute | solution.py:319
  79.6 1.4 %place.3 = f32[256,2048]{1,0:T(8,128)} custom-call(s32[10]{0:T(128)S(1)} %stack.43.where_ref, bf16[1,256,512]{2,1,0:T(8,128)(2,1)S(1)} %collective-permute-done.8.got_ref, f32[256,2048]{1,0:T(8,128)} %place.2._), custom_call_target="tpu_custom_call", output_to_operand_aliasing={{}: (2, {})} | custom-call | bytes 786432 | tf_op jit(solution)/shard_map/place/pallas_call | solution.py:248
Async XLA Ops:
  2.6 13.9 %collective-permute-start = (bf16[512,512]{1,0:T(8,128)(2,1)}, bf16[512,512]{1,0:T(8,128)(2,1)S(1)}, u32[]{:S(2)}, u32[]{:S(2)}) collective-permute-start(bf16[512,512]{1,0:T(8,128)(2,1)} %get-tuple-element.18.refs_1_), channel_id=1, source_target_pairs={{0,8},{4,20},{8,0},{12,28},{16,24},{20,4},{24,16},{28,12},{1,9},{5... | collective-permute-start | bytes 1572872 | tf_op jit(solution)/shard_map/ppermute | solution.py:322
  5.6 10.9 %all-to-all-start = ((bf16[8,8,512]{2,1,0:T(8,128)(2,1)}), bf16[8,8,512]{2,1,0:T(8,128)(2,1)S(1)}, u32[]{:S(2)}, u32[]{:S(2)}) async-start(bf16[8,8,512]{2,1,0:T(8,128)(2,1)} %get-tuple-element.17), calls=%async_computation | async-start | bytes 131072 | tf_op jit(solution)/shard_map/all_to_all | solution.py:325
  8.9 15.2 %collective-permute-start.2 = (bf16[512,512]{1,0:T(8,128)(2,1)}, bf16[512,512]{1,0:T(8,128)(2,1)S(1)}, u32[]{:S(2)}, u32[]{:S(2)}) collective-permute-start(bf16[512,512]{1,0:T(8,128)(2,1)} %get-tuple-element.18.refs_1_), channel_id=1, source_target_pairs={{0,16},{4,12},{8,24},{12,4},{16,0},{20,28},{24,8},{28,20},{1,17},{... | collective-permute-start | bytes 1572872 | tf_op jit(solution)/shard_map/ppermute | solution.py:322
  16.5 1.0 %copy-start.2 = (bf16[8,8,512]{2,1,0:T(8,128)(2,1)}, bf16[8,8,512]{2,1,0:T(8,128)(2,1)S(1)}, u32[]{:S(2)}) copy-start(bf16[8,8,512]{2,1,0:T(8,128)(2,1)S(1)} %all-to-all-done.occ_ref) | copy-start | bytes 196612
  16.5 9.3 %collective-permute-start.3 = (bf16[512,512]{1,0:T(8,128)(2,1)S(1)}, bf16[512,512]{1,0:T(8,128)(2,1)}, u32[]{:S(2)}, u32[]{:S(2)}) collective-permute-start(bf16[512,512]{1,0:T(8,128)(2,1)S(1)} %collective-permute-done.refs_2_), channel_id=1, source_target_pairs={{0,16},{4,12},{8,24},{12,4},{16,0},{20,28},{24,8},{28,20},{1,17},{... | collective-permute-start | bytes 1572872 | tf_op jit(solution)/shard_map/ppermute | solution.py:322
  17.6 11.8 %copy-start = (bf16[512,512]{1,0:T(8,128)(2,1)S(1)}, bf16[512,512]{1,0:T(8,128)(2,1)}, u32[]{:S(2)}) copy-start(bf16[512,512]{1,0:T(8,128)(2,1)} %get-tuple-element.18.refs_1_) | copy-start | bytes 1572868
  23.8 21.1 %collective-permute-start.1 = (bf16[8,400,128]{2,1,0:T(8,128)(2,1)}, bf16[8,400,128]{2,1,0:T(8,128)(2,1)S(1)}, u32[]{:S(2)}, u32[]{:S(2)}) collective-permute-start(bf16[8,400,128]{2,1,0:T(8,128)(2,1)} %half_transform.1), channel_id=1, source_target_pairs={{0,1},{1,0},{2,3},{3,2},{4,5},{5,4},{6,7},{7,6},{8,9},{9,8},{10,11... | collective-permute-start | bytes 2457608 | tf_op jit(solution)/shard_map/ppermute | solution.py:319
  25.8 20.0 %all-to-all-start.1 = ((bf16[8,400,128]{2,1,0:T(8,128)(2,1)}), bf16[8,400,128]{2,1,0:T(8,128)(2,1)S(1)}, u32[]{:S(2)}, u32[]{:S(2)}) async-start(bf16[8,400,128]{2,1,0:T(8,128)(2,1)} %half_transform.1), calls=%async_computation.1 | async-start | bytes 1638400 | tf_op jit(solution)/shard_map/all_to_all | solution.py:340
  29.4 20.1 %collective-permute-start.4 = (bf16[512,512]{1,0:T(8,128)(2,1)S(1)}, bf16[512,512]{1,0:T(8,128)(2,1)}, u32[]{:S(2)}, u32[]{:S(2)}) collective-permute-start(bf16[512,512]{1,0:T(8,128)(2,1)S(1)} %copy-done), channel_id=1, source_target_pairs={{0,4},{4,0},{8,12},{12,8},{16,20},{20,16},{24,28},{28,24},{1,5},{5... | collective-permute-start | bytes 1572872 | tf_op jit(solution)/shard_map/ppermute | solution.py:322
  29.8 19.7 %collective-permute-start.5 = (bf16[512,512]{1,0:T(8,128)(2,1)S(1)}, bf16[512,512]{1,0:T(8,128)(2,1)}, u32[]{:S(2)}, u32[]{:S(2)}) collective-permute-start(bf16[512,512]{1,0:T(8,128)(2,1)S(1)} %collective-permute-done.refs_2_), channel_id=1, source_target_pairs={{0,4},{4,0},{8,12},{12,8},{16,20},{20,16},{24,28},{28,24},{1,5},{5... | collective-permute-start | bytes 1572872 | tf_op jit(solution)/shard_map/ppermute | solution.py:322
  30.0 19.5 %collective-permute-start.6 = (bf16[512,512]{1,0:T(8,128)(2,1)S(1)}, bf16[512,512]{1,0:T(8,128)(2,1)}, u32[]{:S(2)}, u32[]{:S(2)}) collective-permute-start(bf16[512,512]{1,0:T(8,128)(2,1)S(1)} %collective-permute-done.2.refs_3_), channel_id=1, source_target_pairs={{0,4},{4,0},{8,12},{12,8},{16,20},{20,16},{24,28},{28,24},{1,5},{5... | collective-permute-start | bytes 1572872 | tf_op jit(solution)/shard_map/ppermute | solution.py:322
  30.3 19.2 %collective-permute-start.7 = (bf16[512,512]{1,0:T(8,128)(2,1)}, bf16[512,512]{1,0:T(8,128)(2,1)}, u32[]{:S(2)}, u32[]{:S(2)}) collective-permute-start(bf16[512,512]{1,0:T(8,128)(2,1)} %collective-permute-done.3.refs_4_), channel_id=1, source_target_pairs={{0,4},{4,0},{8,12},{12,8},{16,20},{20,16},{24,28},{28,24},{1,5},{5... | collective-permute-start | bytes 1572872 | tf_op jit(solution)/shard_map/ppermute | solution.py:322
  44.9 0.9 %copy-start.1 = (bf16[8,400,128]{2,1,0:T(8,128)(2,1)}, bf16[8,400,128]{2,1,0:T(8,128)(2,1)S(1)}, u32[]{:S(2)}) copy-start(bf16[8,400,128]{2,1,0:T(8,128)(2,1)S(1)} %collective-permute-done.1) | copy-start | bytes 2457604
  45.8 16.4 %all-to-all-start.2 = ((bf16[8,400,128]{2,1,0:T(8,128)(2,1)}), bf16[8,400,128]{2,1,0:T(8,128)(2,1)S(1)}, u32[]{:S(2)}, u32[]{:S(2)}) async-start(bf16[8,400,128]{2,1,0:T(8,128)(2,1)} %copy-done.1), calls=%async_computation.2 | async-start | bytes 1638400 | tf_op jit(solution)/shard_map/all_to_all | solution.py:342
  53.5 21.6 %collective-permute-start.9 = (bf16[1,256,512]{2,1,0:T(8,128)(2,1)}, bf16[1,256,512]{2,1,0:T(8,128)(2,1)S(1)}, u32[]{:S(2)}, u32[]{:S(2)}) collective-permute-start(bf16[1,256,512]{2,1,0:T(8,128)(2,1)} %send_part.2), channel_id=1, source_target_pairs={{0,2},{1,3},{2,0},{3,1},{4,6},{5,7},{6,4},{7,5},{8,10},{9,11},{10,... | collective-permute-start | bytes 786440 | tf_op jit(solution)/shard_map/ppermute | solution.py:319
  65.5 14.1 %collective-permute-start.8 = (bf16[1,256,512]{2,1,0:T(8,128)(2,1)S(1)}, bf16[1,256,512]{2,1,0:T(8,128)(2,1)S(1)}, u32[]{:S(2)}, u32[]{:S(2)}) collective-permute-start(bf16[1,256,512]{2,1,0:T(8,128)(2,1)S(1)} %send_part.3), channel_id=1, source_target_pairs={{0,2},{1,3},{2,0},{3,1},{4,6},{5,7},{6,4},{7,5},{8,10},{9,11},{10,... | collective-permute-start | bytes 786440 | tf_op jit(solution)/shard_map/ppermute | solution.py:319

commit v5 on v4

--- a/solution.py
+++ b/solution.py
@@ -22,7 +22,7 @@
     return k * pb + (META if k >= kmax // 2 else 0)
 
 
-def half_kernel(rows_ref, cols_ref, aux_ref, count_ref, occ_ref, tiles_hbm, half_ref, tile_ref, stage_ref, sems):
+def half_kernel(rows_ref, cols_ref, aux_ref, count_ref, occ_hbm, tiles_hbm, half_ref, occ_ref, tile_ref, stage_ref, sems):
     kmax, pb, blk, _ = tile_ref.shape
     orbitals = half_ref.shape[0]
     ao_blocks = occ_ref.shape[2] // blk
@@ -31,6 +31,8 @@
     def fetch(k):
         return pltpu.make_async_copy(tiles_hbm.at[k], tile_ref.at[k], sems.at[k])
 
+    fetch_occ = pltpu.make_async_copy(occ_hbm, occ_ref, sems.at[kmax])
+    fetch_occ.start()
     for k in range(kmax):
 
         @pl.when(k < count)
@@ -55,6 +57,7 @@
     split = kmax // 2 * pb
     for i in range(orbitals):
         half_ref[i, split : split + META, :] = meta
+    fetch_occ.wait()
 
     for k in range(kmax):
         at = row_of(k, kmax, pb)
@@ -108,17 +111,18 @@
     return pl.pallas_call(
         half_kernel,
         in_specs=[scalars] * 4
-        + [pl.BlockSpec(memory_space=pltpu.VMEM), pl.BlockSpec(memory_space=pl.ANY)],
+        + [pl.BlockSpec(memory_space=pl.ANY)] * 2,
         out_specs=pl.BlockSpec(memory_space=pltpu.VMEM),
         scratch_shapes=[
+            pltpu.VMEM(occ.shape, jnp.bfloat16),
             pltpu.VMEM(tiles.shape, jnp.bfloat16),
             pltpu.VMEM((kmax, pb * orbitals, blk), jnp.float32),
-            pltpu.SemaphoreType.DMA((kmax,)),
+            pltpu.SemaphoreType.DMA((kmax + 1,)),
         ],
         out_shape=jax.ShapeDtypeStruct(out, jnp.bfloat16),
-        compiler_params=pltpu.CompilerParams(vmem_limit_bytes=56 << 20),
+        compiler_params=pltpu.CompilerParams(vmem_limit_bytes=63 << 20),
         cost_estimate=pl.CostEstimate(
-            flops=4 * tiles.size * orbitals, bytes_accessed=tiles.size * 2, transcendentals=0
+            flops=160 * tiles.size * orbitals, bytes_accessed=tiles.size * 80, transcendentals=0
         ),
         name="half_transform",
     )(rows, cols, auxs, count, occ, tiles)
@@ -265,22 +269,33 @@
     )(where, got, result)
 
 
-def open_kernel(vb, vir_hbm, occ_ref, occ_out_ref, out_ref, sems):
+def open_kernel(vb, vir_hbm, occ_hbm, occ_out_hbm, out_hbm, vir_ref, occ_ref, in_sems, out_sems):
     aux = lax.axis_index("aux")
-    copies = []
-    for j in range(out_ref.shape[1] // vb):
+    parts = out_hbm.shape[1] // vb
+    fetch_occ = pltpu.make_async_copy(occ_hbm, occ_ref, in_sems.at[parts])
+    fetch_occ.start()
+    fetches = []
+    for j in range(parts):
         block = jnp.bitwise_xor(aux // 2, j) * 2 + aux % 2
-        copies.append(
+        fetches.append(
             pltpu.make_async_copy(
-                vir_hbm.at[:, pl.ds(pl.multiple_of(block * vb, vb), vb)],
-                out_ref.at[:, pl.ds(j * vb, vb)],
-                sems.at[j],
+                vir_hbm.at[:, pl.ds(pl.multiple_of(block * vb, vb), vb)], vir_ref.at[j], in_sems.at[j]
             )
         )
-        copies[-1].start()
-    occ_out_ref[...] = jnp.broadcast_to(occ_ref[...][None], occ_out_ref.shape)
-    for copy in copies:
-        copy.wait()
+        fetches[-1].start()
+    stores = [
+        pltpu.make_async_copy(vir_ref.at[j], out_hbm.at[:, pl.ds(j * vb, vb)], out_sems.at[j])
+        for j in range(parts)
+    ]
+    fetch_occ.wait()
+    for g in range(occ_out_hbm.shape[0]):
+        stores.append(pltpu.make_async_copy(occ_ref, occ_out_hbm.at[g], out_sems.at[parts + g]))
+        stores[-1].start()
+    for j in range(parts):
+        fetches[j].wait()
+        stores[j].start()
+    for store in stores:
+        store.wait()
 
 
 def opening(vir, occ, group_size, aux, aux_size, vb):
@@ -291,17 +306,22 @@
         order = jnp.bitwise_xor(aux // 2, jnp.arange(parts)) * 2 + aux % 2
         chosen = jnp.take(vir.reshape(rows, aux_size, vb), order, axis=1)
         return jnp.broadcast_to(occ[None], copies), chosen.reshape(rows, -1)
-    vmem = pl.BlockSpec(memory_space=pltpu.VMEM)
+    anywhere = pl.BlockSpec(memory_space=pl.ANY)
     return pl.pallas_call(
         functools.partial(open_kernel, vb),
-        in_specs=[pl.BlockSpec(memory_space=pl.ANY), vmem],
-        out_specs=[vmem, vmem],
-        scratch_shapes=[pltpu.SemaphoreType.DMA((parts,))],
+        in_specs=[anywhere] * 2,
+        out_specs=[anywhere] * 2,
+        scratch_shapes=[
+            pltpu.VMEM((parts, rows, vb), vir.dtype),
+            pltpu.VMEM(occ.shape, occ.dtype),
+            pltpu.SemaphoreType.DMA((parts + 1,)),
+            pltpu.SemaphoreType.DMA((parts + group_size,)),
+        ],
         out_shape=[
             jax.ShapeDtypeStruct(copies, occ.dtype),
             jax.ShapeDtypeStruct((rows, parts * vb), vir.dtype),
         ],
-        compiler_params=pltpu.CompilerParams(vmem_limit_bytes=60 << 20),
+        compiler_params=pltpu.CompilerParams(vmem_limit_bytes=63 << 20),
         name="opening",
     )(vir, occ)
 
@@ -327,7 +347,6 @@
     core = lax.axis_index("grp") % 2
     near = hop(own, (2, 4))
     far = hop(own, (4, 2))
-    occ, near = lax.optimization_barrier((occ, near))
     across = hop(near, (4, 2))
     halves = half_transform(
         integral_tiles[0, 0], row_blocks[0, 0], col_blocks[0, 0], aux_blocks[0, 0], tile_counts[0], occ

time: 81.7 us -> 78.3 us (0.958)
  starting transfers between devices: 19.8 us -> 28.4 us
  waiting for transfers between devices: 32.4 us -> 24.5 us
  Pallas kernels: 27 us -> 23.1 us
    ppermute x3, starting transfers between devices: 2.96 us -> 9.36 us  [swap(): return lax.ppermute(x, 'aux', [(a, a ^ step) for a in range(aux_size)])]
    all_to_all x1, waiting for transfers between devices: 5.63 us -> 0.03 us  [shards(): occ = lax.all_to_all(occ, 'grp', split_axis=0, concat_axis=0, tiled=True)]
    ppermute x3, waiting for transfers between devices: 17.6 us -> 14.7 us  [swap(): return lax.ppermute(x, 'aux', [(a, a ^ step) for a in range(aux_size)])]
    pallas_call x1, Pallas kernels: 6.24 us -> 3.6 us  [half_transform(): pl.pallas_call(half_kernel, in_specs=[scalars] * 4 + [pl.BlockSpec(memory...]
    ppermute x7, starting transfers between devices: 6.42 us -> 8.13 us  [hop(): lax.ppermute(x, 'grp', [(g, g ^ steps[g % 2]) for g in range(group_size)])]
    ppermute x7, waiting for transfers between devices: 1.67 us -> 2.86 us  [hop(): lax.ppermute(x, 'grp', [(g, g ^ steps[g % 2]) for g in range(group_size)])]
  transfers between devices with their start and end apart: 13 -> 13, of which waited for: 5 -> 4; matrix products, arithmetic and copies ran while one was open for 0% -> 0% of each run, Pallas kernels for 28% -> 26%
where the time goes in v5:
time: 78.3 us; the launch traced here: 77.5 us
  starting transfers between devices  28.4 us (36%)
  waiting for transfers between devices  24.5 us (31%)
  Pallas kernels  23.1 us (30%)
  between operations  0.79 us (1%)
    pallas_call x4, Pallas kernels, pair_transform(): pl.pallas_call(functools.partial(pair_kernel, kmax, pb, group, vb, kind,...  14.9 us
    ppermute x3, waiting for transfers between devices, swap(): return lax.ppermute(x, 'aux', [(a, a ^ step) for a in range(aux_size)])  14.7 us
    ppermute x3, starting transfers between devices, swap(): return lax.ppermute(x, 'aux', [(a, a ^ step) for a in range(aux_size)])  9.36 us
    ppermute x7, starting transfers between devices, hop(): lax.ppermute(x, 'grp', [(g, g ^ steps[g % 2]) for g in range(group_size)])  8.13 us
    all_to_all x1, waiting for transfers between devices, shards(): lax.all_to_all(others, 'grp', split_axis=0, concat_axis=0, tiled=True)  6.89 us
    all_to_all x1, starting transfers between devices, shards(): lax.all_to_all(halves, 'grp', split_axis=0, concat_axis=0, tiled=True)  3.97 us
    pallas_call x1, Pallas kernels, half_transform(): pl.pallas_call(half_kernel, in_specs=[scalars] * 4 + [pl.BlockSpec(memory...  3.6 us
    all_to_all x1, starting transfers between devices, shards(): lax.all_to_all(others, 'grp', split_axis=0, concat_axis=0, tiled=True)  3.55 us
  transfers between devices with their start and end apart: 13, of which 4 were waited for; matrix products, arithmetic and copies ran while one was open for 0% of the time, Pallas kernels for 26%

profile of v5, /device:TPU:0, one launch (start us, length us, event | category | flops | bytes accessed | tf_op | source)
XLA Modules:
  0.0 77.5 jit_solution(10808686326235686762)
XLA Ops:
  0.0 1.9 %opening.1 = (bf16[8,8,512]{2,1,0:T(8,128)(2,1)}, bf16[512,512]{1,0:T(8,128)(2,1)}) custom-call(bf16[512,1024]{1,0:T(8,128)(2,1)} %vir_hbm.1, bf16[8,512]{1,0:T(8,128)(2,1)} %occ_hbm.1), custom_call_target="tpu_custom_call" | custom-call | tf_op jit(solution)/shard_map/opening/pallas_call | solution.py:310
  1.9 3.0 %collective-permute-start.2 = (bf16[512,512]{1,0:T(8,128)(2,1)}, bf16[512,512]{1,0:T(8,128)(2,1)}, u32[]{:S(2)}, u32[]{:S(2)}) collective-permute-start(bf16[512,512]{1,0:T(8,128)(2,1)} %get-tuple-element.16.refs_1_), channel_id=1, source_target_pairs={{0,8},{4,20},{8,0},{12,28},{16,24},{20,4},{24,16},{28,12},{1,9},{5... | collective-permute-start | bytes 1572872 | tf_op jit(solution)/shard_map/ppermute | solution.py:342
  4.9 3.4 %all-to-all-start = ((bf16[8,8,512]{2,1,0:T(8,128)(2,1)}), bf16[8,8,512]{2,1,0:T(8,128)(2,1)S(1)}, u32[]{:S(2)}, u32[]{:S(2)}) async-start(bf16[8,8,512]{2,1,0:T(8,128)(2,1)} %get-tuple-element.15), calls=%async_computation | async-start | bytes 131072 | tf_op jit(solution)/shard_map/all_to_all | solution.py:345
  8.3 1.9 %collective-permute-start.1 = (bf16[512,512]{1,0:T(8,128)(2,1)}, bf16[512,512]{1,0:T(8,128)(2,1)}, u32[]{:S(2)}, u32[]{:S(2)}) collective-permute-start(bf16[512,512]{1,0:T(8,128)(2,1)} %get-tuple-element.16.refs_1_), channel_id=1, source_target_pairs={{0,16},{4,12},{8,24},{12,4},{16,0},{20,28},{24,8},{28,20},{1,17},{... | collective-permute-start | bytes 1572872 | tf_op jit(solution)/shard_map/ppermute | solution.py:342
  10.9 2.8 %collective-permute-done.2.refs_2_ = bf16[512,512]{1,0:T(8,128)(2,1)} collective-permute-done((bf16[512,512]{1,0:T(8,128)(2,1)}, bf16[512,512]{1,0:T(8,128)(2,1)}, u32[]{:S(2)}, u32[]{:S(2)}) %collective-permute-start.2) | collective-permute-done | bytes 524320 | tf_op jit(solution)/shard_map/ppermute | solution.py:342
  13.7 2.1 %collective-permute-start.3 = (bf16[512,512]{1,0:T(8,128)(2,1)}, bf16[512,512]{1,0:T(8,128)(2,1)}, u32[]{:S(2)}, u32[]{:S(2)}) collective-permute-start(bf16[512,512]{1,0:T(8,128)(2,1)} %collective-permute-done.2.refs_2_), channel_id=1, source_target_pairs={{0,16},{4,12},{8,24},{12,4},{16,0},{20,28},{24,8},{28,20},{1,17},{... | collective-permute-start | bytes 1572872 | tf_op jit(solution)/shard_map/ppermute | solution.py:342
  15.8 0.0 all-to-all-done.occ_hbm
  15.9 0.0 copy-start.1
  15.9 0.6 copy-done.1
  16.5 0.0 copy-start
  16.5 3.6 %half_transform.1 = bf16[8,400,128]{2,1,0:T(8,128)(2,1)} custom-call(s32[12]{0:T(128)} %bitcast.17, s32[12]{0:T(128)} %bitcast.18, s32[12]{0:T(128)} %bitcast.19, s32[1]{0:T(128)} %bitcast.15.count_ref, bf16[8,8,512]{2,1,0:T(8,128)(2,1)} %copy-done.1, bf16[12,32,128,128]{3,2,1,0:T(8,128)(2,1)} %bitcast.16), custom_call_target="tpu_custom_call" | custom-call | flops 8053063680 | bytes 503316480 | tf_op jit(solution)/shard_map/half_transform/pallas_call | solution.py:111
  20.1 4.2 %collective-permute-start = (bf16[8,400,128]{2,1,0:T(8,128)(2,1)}, bf16[8,400,128]{2,1,0:T(8,128)(2,1)}, u32[]{:S(2)}, u32[]{:S(2)}) collective-permute-start(bf16[8,400,128]{2,1,0:T(8,128)(2,1)} %half_transform.1), channel_id=1, source_target_pairs={{0,1},{1,0},{2,3},{3,2},{4,5},{5,4},{6,7},{7,6},{8,9},{9,8},{10,11... | collective-permute-start | bytes 2457608 | tf_op jit(solution)/shard_map/ppermute | solution.py:339
  24.3 0.0 collective-permute-done.1.refs_3_
  24.3 0.0 collective-permute-done.3.refs_4_
  24.3 4.0 %all-to-all-start.1 = ((bf16[8,400,128]{2,1,0:T(8,128)(2,1)}), bf16[8,400,128]{2,1,0:T(8,128)(2,1)S(1)}, u32[]{:S(2)}, u32[]{:S(2)}) async-start(bf16[8,400,128]{2,1,0:T(8,128)(2,1)} %half_transform.1), calls=%async_computation.1 | async-start | bytes 1638400 | tf_op jit(solution)/shard_map/all_to_all | solution.py:359
  28.3 0.0 copy-done
  28.3 0.5 collective-permute-start.4
  28.8 0.1 collective-permute-start.5
  28.9 0.4 collective-permute-start.6
  29.3 0.1 collective-permute-start.7
  29.4 13.3 %collective-permute-done = bf16[8,400,128]{2,1,0:T(8,128)(2,1)} collective-permute-done((bf16[8,400,128]{2,1,0:T(8,128)(2,1)}, bf16[8,400,128]{2,1,0:T(8,128)(2,1)}, u32[]{:S(2)}, u32[]{:S(2)}) %collective-permute-start) | collective-permute-done | bytes 819232 | tf_op jit(solution)/shard_map/ppermute | solution.py:339
  42.7 0.0 all-to-all-done.1.refs_0_
  42.7 3.5 %all-to-all-start.2 = ((bf16[8,400,128]{2,1,0:T(8,128)(2,1)}), bf16[8,400,128]{2,1,0:T(8,128)(2,1)S(1)}, u32[]{:S(2)}, u32[]{:S(2)}) async-start(bf16[8,400,128]{2,1,0:T(8,128)(2,1)} %collective-permute-done), calls=%async_computation.2 | async-start | bytes 1638400 | tf_op jit(solution)/shard_map/all_to_all | solution.py:361
  46.3 0.1 stack.43.where_ref
  46.3 0.0 collective-permute-done.4.refs_5_
  46.3 0.0 collective-permute-done.5.refs_6_
  46.4 0.0 collective-permute-done.6.refs_7_
  46.4 0.0 collective-permute-done.7.refs_8_
  46.4 3.3 %send_part.2 = bf16[1,256,512]{2,1,0:T(8,128)(2,1)S(1)} custom-call(s32[10]{0:T(128)S(1)} %stack.43.where_ref, bf16[8,400,128]{2,1,0:T(8,128)(2,1)S(1)} %all-to-all-done.1.refs_0_, bf16[512,512]{1,0:T(8,128)(2,1)S(1)} %copy-done, bf16[512,512]{1,0:T(8,128)(2,1)} %collective-permute-done.2.refs_2_, bf16[512,512]{1,0:T(8,128)(2,1)} %collective-permute-done.1.refs_3_, ...), custom_call_target="tpu_custom_call" | custom-call | flops 2147483648 | bytes 2916352 | tf_op jit(solution)/shard_map/send_part/pallas_call | solution.py:209
  49.7 2.5 %collective-permute-start.9 = (bf16[1,256,512]{2,1,0:T(8,128)(2,1)S(1)}, bf16[1,256,512]{2,1,0:T(8,128)(2,1)S(1)}, u32[]{:S(2)}, u32[]{:S(2)}) collective-permute-start(bf16[1,256,512]{2,1,0:T(8,128)(2,1)S(1)} %send_part.2), channel_id=1, source_target_pairs={{0,2},{1,3},{2,0},{3,1},{4,6},{5,7},{6,4},{7,5},{8,10},{9,11},{10,... | collective-permute-start | bytes 786440 | tf_op jit(solution)/shard_map/ppermute | solution.py:339
  52.2 6.9 %all-to-all-done.2.refs_0_ = bf16[8,400,128]{2,1,0:T(8,128)(2,1)S(1)} async-done(((bf16[8,400,128]{2,1,0:T(8,128)(2,1)}), bf16[8,400,128]{2,1,0:T(8,128)(2,1)S(1)}, u32[]{:S(2)}, u32[]{:S(2)}) %all-to-all-start.2) | async-done | bytes 819232 | tf_op jit(solution)/shard_map/all_to_all | solution.py:361
  59.1 3.3 %send_part.3 = bf16[1,256,512]{2,1,0:T(8,128)(2,1)S(1)} custom-call(s32[10]{0:T(128)S(1)} %stack.43.where_ref, bf16[8,400,128]{2,1,0:T(8,128)(2,1)S(1)} %all-to-all-done.2.refs_0_, bf16[512,512]{1,0:T(8,128)(2,1)S(1)} %copy-done, bf16[512,512]{1,0:T(8,128)(2,1)} %collective-permute-done.2.refs_2_, bf16[512,512]{1,0:T(8,128)(2,1)} %collective-permute-done.1.refs_3_, ...), custom_call_target="tpu_custom_call" | custom-call | flops 2147483648 | bytes 2916352 | tf_op jit(solution)/shard_map/send_part/pallas_call | solution.py:209
  62.4 2.6 %collective-permute-start.8 = (bf16[1,256,512]{2,1,0:T(8,128)(2,1)S(1)}, bf16[1,256,512]{2,1,0:T(8,128)(2,1)S(1)}, u32[]{:S(2)}, u32[]{:S(2)}) collective-permute-start(bf16[1,256,512]{2,1,0:T(8,128)(2,1)S(1)} %send_part.3), channel_id=1, source_target_pairs={{0,2},{1,3},{2,0},{3,1},{4,6},{5,7},{6,4},{7,5},{8,10},{9,11},{10,... | collective-permute-start | bytes 786440 | tf_op jit(solution)/shard_map/ppermute | solution.py:339
  65.0 4.1 %own_part.2.refs_9_ = f32[256,2048]{1,0:T(8,128)} custom-call(s32[10]{0:T(128)S(1)} %stack.43.where_ref, bf16[8,400,128]{2,1,0:T(8,128)(2,1)S(1)} %all-to-all-done.1.refs_0_, bf16[512,512]{1,0:T(8,128)(2,1)S(1)} %copy-done, bf16[512,512]{1,0:T(8,128)(2,1)} %collective-permute-done.2.refs_2_, bf16[512,512]{1,0:T(8,128)(2,1)} %collective-permute-done.1.refs_3_, ...), custom_call_target="tpu_custom_call" | custom-call | flops 2147483648 | bytes 2916352 | tf_op jit(solution)/shard_map/own_part/pallas_call | solution.py:209
  69.2 4.1 %own_part.3._ = f32[256,2048]{1,0:T(8,128)} custom-call(s32[10]{0:T(128)S(1)} %stack.43.where_ref, bf16[8,400,128]{2,1,0:T(8,128)(2,1)S(1)} %all-to-all-done.2.refs_0_, bf16[512,512]{1,0:T(8,128)(2,1)S(1)} %copy-done, bf16[512,512]{1,0:T(8,128)(2,1)} %collective-permute-done.2.refs_2_, ...), custom_call_target="tpu_custom_call", output_to_operand_aliasing={{}: (10, {})} | custom-call | flops 2147483648 | bytes 2916352 | tf_op jit(solution)/shard_map/own_part/pallas_call | solution.py:209
  73.3 0.0 collective-permute-done.9.got_ref
  73.3 1.4 %place.2._ = f32[256,2048]{1,0:T(8,128)} custom-call(s32[10]{0:T(128)S(1)} %stack.43.where_ref, bf16[1,256,512]{2,1,0:T(8,128)(2,1)S(1)} %collective-permute-done.9.got_ref, f32[256,2048]{1,0:T(8,128)} %own_part.3._), custom_call_target="tpu_custom_call", output_to_operand_aliasing={{}: (2, {})} | custom-call | bytes 786432 | tf_op jit(solution)/shard_map/place/pallas_call | solution.py:252
  74.7 1.4 %collective-permute-done.8.got_ref = bf16[1,256,512]{2,1,0:T(8,128)(2,1)S(1)} collective-permute-done((bf16[1,256,512]{2,1,0:T(8,128)(2,1)S(1)}, bf16[1,256,512]{2,1,0:T(8,128)(2,1)S(1)}, u32[]{:S(2)}, u32[]{:S(2)}) %collective-permute-start.8) | collective-permute-done | bytes 262176 | tf_op jit(solution)/shard_map/ppermute | solution.py:339
  76.1 1.4 %place.3 = f32[256,2048]{1,0:T(8,128)} custom-call(s32[10]{0:T(128)S(1)} %stack.43.where_ref, bf16[1,256,512]{2,1,0:T(8,128)(2,1)S(1)} %collective-permute-done.8.got_ref, f32[256,2048]{1,0:T(8,128)} %place.2._), custom_call_target="tpu_custom_call", output_to_operand_aliasing={{}: (2, {})} | custom-call | bytes 786432 | tf_op jit(solution)/shard_map/place/pallas_call | solution.py:252
Async XLA Ops:
  1.9 11.8 %collective-permute-start.2 = (bf16[512,512]{1,0:T(8,128)(2,1)}, bf16[512,512]{1,0:T(8,128)(2,1)}, u32[]{:S(2)}, u32[]{:S(2)}) collective-permute-start(bf16[512,512]{1,0:T(8,128)(2,1)} %get-tuple-element.16.refs_1_), channel_id=1, source_target_pairs={{0,8},{4,20},{8,0},{12,28},{16,24},{20,4},{24,16},{28,12},{1,9},{5... | collective-permute-start | bytes 1572872 | tf_op jit(solution)/shard_map/ppermute | solution.py:342
  4.9 10.9 %all-to-all-start = ((bf16[8,8,512]{2,1,0:T(8,128)(2,1)}), bf16[8,8,512]{2,1,0:T(8,128)(2,1)S(1)}, u32[]{:S(2)}, u32[]{:S(2)}) async-start(bf16[8,8,512]{2,1,0:T(8,128)(2,1)} %get-tuple-element.15), calls=%async_computation | async-start | bytes 131072 | tf_op jit(solution)/shard_map/all_to_all | solution.py:345
  8.3 16.1 %collective-permute-start.1 = (bf16[512,512]{1,0:T(8,128)(2,1)}, bf16[512,512]{1,0:T(8,128)(2,1)}, u32[]{:S(2)}, u32[]{:S(2)}) collective-permute-start(bf16[512,512]{1,0:T(8,128)(2,1)} %get-tuple-element.16.refs_1_), channel_id=1, source_target_pairs={{0,16},{4,12},{8,24},{12,4},{16,0},{20,28},{24,8},{28,20},{1,17},{... | collective-permute-start | bytes 1572872 | tf_op jit(solution)/shard_map/ppermute | solution.py:342
  13.7 10.6 %collective-permute-start.3 = (bf16[512,512]{1,0:T(8,128)(2,1)}, bf16[512,512]{1,0:T(8,128)(2,1)}, u32[]{:S(2)}, u32[]{:S(2)}) collective-permute-start(bf16[512,512]{1,0:T(8,128)(2,1)} %collective-permute-done.2.refs_2_), channel_id=1, source_target_pairs={{0,16},{4,12},{8,24},{12,4},{16,0},{20,28},{24,8},{28,20},{1,17},{... | collective-permute-start | bytes 1572872 | tf_op jit(solution)/shard_map/ppermute | solution.py:342
  15.9 0.6 copy-start.1
  16.5 11.8 %copy-start = (bf16[512,512]{1,0:T(8,128)(2,1)S(1)}, bf16[512,512]{1,0:T(8,128)(2,1)}, u32[]{:S(2)}) copy-start(bf16[512,512]{1,0:T(8,128)(2,1)} %get-tuple-element.16.refs_1_) | copy-start | bytes 1572868
  20.1 22.6 %collective-permute-start = (bf16[8,400,128]{2,1,0:T(8,128)(2,1)}, bf16[8,400,128]{2,1,0:T(8,128)(2,1)}, u32[]{:S(2)}, u32[]{:S(2)}) collective-permute-start(bf16[8,400,128]{2,1,0:T(8,128)(2,1)} %half_transform.1), channel_id=1, source_target_pairs={{0,1},{1,0},{2,3},{3,2},{4,5},{5,4},{6,7},{7,6},{8,9},{9,8},{10,11... | collective-permute-start | bytes 2457608 | tf_op jit(solution)/shard_map/ppermute | solution.py:339
  24.3 18.3 %all-to-all-start.1 = ((bf16[8,400,128]{2,1,0:T(8,128)(2,1)}), bf16[8,400,128]{2,1,0:T(8,128)(2,1)S(1)}, u32[]{:S(2)}, u32[]{:S(2)}) async-start(bf16[8,400,128]{2,1,0:T(8,128)(2,1)} %half_transform.1), calls=%async_computation.1 | async-start | bytes 1638400 | tf_op jit(solution)/shard_map/all_to_all | solution.py:359
  28.3 18.0 %collective-permute-start.4 = (bf16[512,512]{1,0:T(8,128)(2,1)S(1)}, bf16[512,512]{1,0:T(8,128)(2,1)S(1)}, u32[]{:S(2)}, u32[]{:S(2)}) collective-permute-start(bf16[512,512]{1,0:T(8,128)(2,1)S(1)} %copy-done), channel_id=1, source_target_pairs={{0,4},{4,0},{8,12},{12,8},{16,20},{20,16},{24,28},{28,24},{1,5},{5... | collective-permute-start | bytes 1572872 | tf_op jit(solution)/shard_map/ppermute | solution.py:342
  28.8 17.5 %collective-permute-start.5 = (bf16[512,512]{1,0:T(8,128)(2,1)}, bf16[512,512]{1,0:T(8,128)(2,1)}, u32[]{:S(2)}, u32[]{:S(2)}) collective-permute-start(bf16[512,512]{1,0:T(8,128)(2,1)} %collective-permute-done.2.refs_2_), channel_id=1, source_target_pairs={{0,4},{4,0},{8,12},{12,8},{16,20},{20,16},{24,28},{28,24},{1,5},{5... | collective-permute-start | bytes 1572872 | tf_op jit(solution)/shard_map/ppermute | solution.py:342
  28.9 17.5 %collective-permute-start.6 = (bf16[512,512]{1,0:T(8,128)(2,1)}, bf16[512,512]{1,0:T(8,128)(2,1)}, u32[]{:S(2)}, u32[]{:S(2)}) collective-permute-start(bf16[512,512]{1,0:T(8,128)(2,1)} %collective-permute-done.1.refs_3_), channel_id=1, source_target_pairs={{0,4},{4,0},{8,12},{12,8},{16,20},{20,16},{24,28},{28,24},{1,5},{5... | collective-permute-start | bytes 1572872 | tf_op jit(solution)/shard_map/ppermute | solution.py:342
  29.3 17.0 %collective-permute-start.7 = (bf16[512,512]{1,0:T(8,128)(2,1)}, bf16[512,512]{1,0:T(8,128)(2,1)}, u32[]{:S(2)}, u32[]{:S(2)}) collective-permute-start(bf16[512,512]{1,0:T(8,128)(2,1)} %collective-permute-done.3.refs_4_), channel_id=1, source_target_pairs={{0,4},{4,0},{8,12},{12,8},{16,20},{20,16},{24,28},{28,24},{1,5},{5... | collective-permute-start | bytes 1572872 | tf_op jit(solution)/shard_map/ppermute | solution.py:342
  42.7 16.4 %all-to-all-start.2 = ((bf16[8,400,128]{2,1,0:T(8,128)(2,1)}), bf16[8,400,128]{2,1,0:T(8,128)(2,1)S(1)}, u32[]{:S(2)}, u32[]{:S(2)}) async-start(bf16[8,400,128]{2,1,0:T(8,128)(2,1)} %collective-permute-done), calls=%async_computation.2 | async-start | bytes 1638400 | tf_op jit(solution)/shard_map/all_to_all | solution.py:361
  49.7 23.6 %collective-permute-start.9 = (bf16[1,256,512]{2,1,0:T(8,128)(2,1)S(1)}, bf16[1,256,512]{2,1,0:T(8,128)(2,1)S(1)}, u32[]{:S(2)}, u32[]{:S(2)}) collective-permute-start(bf16[1,256,512]{2,1,0:T(8,128)(2,1)S(1)} %send_part.2), channel_id=1, source_target_pairs={{0,2},{1,3},{2,0},{3,1},{4,6},{5,7},{6,4},{7,5},{8,10},{9,11},{10,... | collective-permute-start | bytes 786440 | tf_op jit(solution)/shard_map/ppermute | solution.py:339
  62.4 13.7 %collective-permute-start.8 = (bf16[1,256,512]{2,1,0:T(8,128)(2,1)S(1)}, bf16[1,256,512]{2,1,0:T(8,128)(2,1)S(1)}, u32[]{:S(2)}, u32[]{:S(2)}) collective-permute-start(bf16[1,256,512]{2,1,0:T(8,128)(2,1)S(1)} %send_part.3), channel_id=1, source_target_pairs={{0,2},{1,3},{2,0},{3,1},{4,6},{5,7},{6,4},{7,5},{8,10},{9,11},{10,... | collective-permute-start | bytes 786440 | tf_op jit(solution)/shard_map/ppermute | solution.py:339

commit v6 on v5

--- a/solution.py
+++ b/solution.py
@@ -9,6 +9,7 @@
 
 PDEV = 512
 META = 16
+PIECES = 4
 PAIR_LIMIT = 40
 PLACE_LIMIT = 40
 FIELD = 16
@@ -238,12 +239,19 @@
 
 def place_kernel(side, where_ref, got_ref, _, out_hbm, wide_ref, sems):
     copies = []
+    piece = got_ref.shape[1] // PIECES
     for j in range(got_ref.shape[0]):
-        wide_ref[j] = got_ref[j].astype(jnp.float32)
         block = jnp.bitwise_xor(where_ref[side], 2 * (j + 1))
         lane = pl.multiple_of(block * PDEV, PDEV)
-        copies.append(pltpu.make_async_copy(wide_ref.at[j], out_hbm.at[:, pl.ds(lane, PDEV)], sems.at[j]))
-        copies[-1].start()
+        for n in range(PIECES):
+            rows = pl.ds(n * piece, piece)
+            wide_ref[j, rows, :] = got_ref[j, rows, :].astype(jnp.float32)
+            copies.append(
+                pltpu.make_async_copy(
+                    wide_ref.at[j, rows], out_hbm.at[rows, pl.ds(lane, PDEV)], sems.at[j * PIECES + n]
+                )
+            )
+            copies[-1].start()
     for copy in copies:
         copy.wait()
 
@@ -258,7 +266,7 @@
             out_specs=pl.BlockSpec(memory_space=pl.ANY),
             scratch_shapes=[
                 pltpu.VMEM(got.shape, jnp.float32),
-                pltpu.SemaphoreType.DMA((got.shape[0],)),
+                pltpu.SemaphoreType.DMA((got.shape[0] * PIECES,)),
             ],
         ),
         out_shape=jax.ShapeDtypeStruct(result.shape, jnp.float32),

time: 78.3 us -> 78 us (level)
  starting transfers between devices: 28.4 us -> 24 us
  Pallas kernels: 23.1 us -> 26.2 us
  waiting for transfers between devices: 24.5 us -> 25.9 us
    ppermute x3, starting transfers between devices: 9.36 us -> 4.49 us  [swap(): return lax.ppermute(x, 'aux', [(a, a ^ step) for a in range(aux_size)])]
    pallas_call x1, Pallas kernels: 3.6 us -> 6.73 us  [half_transform(): pl.pallas_call(half_kernel, in_specs=[scalars] * 4 + [pl.BlockSpec(memory...]
    all_to_all x1, waiting for transfers between devices: 6.89 us -> 7.96 us  [shards(): lax.all_to_all(others, 'grp', split_axis=0, concat_axis=0, tiled=True)]
    all_to_all x1, starting transfers between devices: 3.55 us -> 4.44 us  [shards(): lax.all_to_all(others, 'grp', split_axis=0, concat_axis=0, tiled=True)]
  transfers between devices with their start and end apart: 13 -> 13, of which waited for: 4 -> 4; matrix products, arithmetic and copies ran while one was open for 0% -> 0% of each run, Pallas kernels for 26% -> 30%
where the time goes in v6:
time: 78 us; the launch traced here: 77.6 us
  Pallas kernels  26.2 us (34%)
  waiting for transfers between devices  25.9 us (33%)
  starting transfers between devices  24 us (31%)
  between operations  0.78 us (1%)
    ppermute x3, waiting for transfers between devices, swap(): return lax.ppermute(x, 'aux', [(a, a ^ step) for a in range(aux_size)])  15.1 us
    pallas_call x4, Pallas kernels, pair_transform(): pl.pallas_call(functools.partial(pair_kernel, kmax, pb, group, vb, kind,...  14.9 us
    ppermute x7, starting transfers between devices, hop(): lax.ppermute(x, 'grp', [(g, g ^ steps[g % 2]) for g in range(group_size)])  8.13 us
    all_to_all x1, waiting for transfers between devices, shards(): lax.all_to_all(others, 'grp', split_axis=0, concat_axis=0, tiled=True)  7.96 us
    pallas_call x1, Pallas kernels, half_transform(): pl.pallas_call(half_kernel, in_specs=[scalars] * 4 + [pl.BlockSpec(memory...  6.73 us
    ppermute x3, starting transfers between devices, swap(): return lax.ppermute(x, 'aux', [(a, a ^ step) for a in range(aux_size)])  4.49 us
    all_to_all x1, starting transfers between devices, shards(): lax.all_to_all(others, 'grp', split_axis=0, concat_axis=0, tiled=True)  4.44 us
    all_to_all x1, starting transfers between devices, shards(): lax.all_to_all(halves, 'grp', split_axis=0, concat_axis=0, tiled=True)  3.55 us
  transfers between devices with their start and end apart: 13, of which 4 were waited for; matrix products, arithmetic and copies ran while one was open for 0% of the time, Pallas kernels for 30%

profile of v6, /device:TPU:0, one launch (start us, length us, event | category | flops | bytes accessed | tf_op | source)
XLA Modules:
  0.0 77.6 jit_solution(1695374801384049568)
XLA Ops:
  0.0 1.9 %opening.1 = (bf16[8,8,512]{2,1,0:T(8,128)(2,1)}, bf16[512,512]{1,0:T(8,128)(2,1)}) custom-call(bf16[512,1024]{1,0:T(8,128)(2,1)} %vir_hbm.1, bf16[8,512]{1,0:T(8,128)(2,1)} %occ_hbm.1), custom_call_target="tpu_custom_call" | custom-call | tf_op jit(solution)/shard_map/opening/pallas_call | solution.py:318
  1.9 3.0 %collective-permute-start.2 = (bf16[512,512]{1,0:T(8,128)(2,1)}, bf16[512,512]{1,0:T(8,128)(2,1)}, u32[]{:S(2)}, u32[]{:S(2)}) collective-permute-start(bf16[512,512]{1,0:T(8,128)(2,1)} %get-tuple-element.16.refs_1_), channel_id=1, source_target_pairs={{0,8},{4,20},{8,0},{12,28},{16,24},{20,4},{24,16},{28,12},{1,9},{5... | collective-permute-start | bytes 1572872 | tf_op jit(solution)/shard_map/ppermute | solution.py:350
  4.9 3.4 %all-to-all-start = ((bf16[8,8,512]{2,1,0:T(8,128)(2,1)}), bf16[8,8,512]{2,1,0:T(8,128)(2,1)S(1)}, u32[]{:S(2)}, u32[]{:S(2)}) async-start(bf16[8,8,512]{2,1,0:T(8,128)(2,1)} %get-tuple-element.15), calls=%async_computation | async-start | bytes 131072 | tf_op jit(solution)/shard_map/all_to_all | solution.py:353
  8.3 1.9 %collective-permute-start.1 = (bf16[512,512]{1,0:T(8,128)(2,1)}, bf16[512,512]{1,0:T(8,128)(2,1)}, u32[]{:S(2)}, u32[]{:S(2)}) collective-permute-start(bf16[512,512]{1,0:T(8,128)(2,1)} %get-tuple-element.16.refs_1_), channel_id=1, source_target_pairs={{0,16},{4,12},{8,24},{12,4},{16,0},{20,28},{24,8},{28,20},{1,17},{... | collective-permute-start | bytes 1572872 | tf_op jit(solution)/shard_map/ppermute | solution.py:350
  10.9 2.8 %collective-permute-done.2.refs_2_ = bf16[512,512]{1,0:T(8,128)(2,1)} collective-permute-done((bf16[512,512]{1,0:T(8,128)(2,1)}, bf16[512,512]{1,0:T(8,128)(2,1)}, u32[]{:S(2)}, u32[]{:S(2)}) %collective-permute-start.2) | collective-permute-done | bytes 524320 | tf_op jit(solution)/shard_map/ppermute | solution.py:350
  13.7 2.1 %collective-permute-start.3 = (bf16[512,512]{1,0:T(8,128)(2,1)}, bf16[512,512]{1,0:T(8,128)(2,1)}, u32[]{:S(2)}, u32[]{:S(2)}) collective-permute-start(bf16[512,512]{1,0:T(8,128)(2,1)} %collective-permute-done.2.refs_2_), channel_id=1, source_target_pairs={{0,16},{4,12},{8,24},{12,4},{16,0},{20,28},{24,8},{28,20},{1,17},{... | collective-permute-start | bytes 1572872 | tf_op jit(solution)/shard_map/ppermute | solution.py:350
  15.8 0.0 all-to-all-done.occ_hbm
  15.9 0.0 copy-start.1
  15.9 0.6 copy-done.1
  16.5 0.0 copy-start
  16.5 6.7 %half_transform.1 = bf16[8,400,128]{2,1,0:T(8,128)(2,1)} custom-call(s32[12]{0:T(128)} %bitcast.17, s32[12]{0:T(128)} %bitcast.18, s32[12]{0:T(128)} %bitcast.19, s32[1]{0:T(128)} %bitcast.15.count_ref, bf16[8,8,512]{2,1,0:T(8,128)(2,1)} %copy-done.1, bf16[12,32,128,128]{3,2,1,0:T(8,128)(2,1)} %bitcast.16), custom_call_target="tpu_custom_call" | custom-call | flops 8053063680 | bytes 503316480 | tf_op jit(solution)/shard_map/half_transform/pallas_call | solution.py:112
  23.2 1.4 %collective-permute-start = (bf16[8,400,128]{2,1,0:T(8,128)(2,1)}, bf16[8,400,128]{2,1,0:T(8,128)(2,1)}, u32[]{:S(2)}, u32[]{:S(2)}) collective-permute-start(bf16[8,400,128]{2,1,0:T(8,128)(2,1)} %half_transform.1), channel_id=1, source_target_pairs={{0,1},{1,0},{2,3},{3,2},{4,5},{5,4},{6,7},{7,6},{8,9},{9,8},{10,11... | collective-permute-start | bytes 2457608 | tf_op jit(solution)/shard_map/ppermute | solution.py:347
  24.6 0.0 collective-permute-done.1.refs_3_
  24.6 0.0 collective-permute-done.3.refs_4_
  24.6 3.6 %all-to-all-start.1 = ((bf16[8,400,128]{2,1,0:T(8,128)(2,1)}), bf16[8,400,128]{2,1,0:T(8,128)(2,1)S(1)}, u32[]{:S(2)}, u32[]{:S(2)}) async-start(bf16[8,400,128]{2,1,0:T(8,128)(2,1)} %half_transform.1), calls=%async_computation.1 | async-start | bytes 1638400 | tf_op jit(solution)/shard_map/all_to_all | solution.py:367
  28.2 0.0 copy-done
  28.2 0.4 collective-permute-start.4
  28.6 0.2 collective-permute-start.5
  28.8 0.3 collective-permute-start.6
  29.1 0.2 collective-permute-start.7
  29.3 12.5 %collective-permute-done = bf16[8,400,128]{2,1,0:T(8,128)(2,1)} collective-permute-done((bf16[8,400,128]{2,1,0:T(8,128)(2,1)}, bf16[8,400,128]{2,1,0:T(8,128)(2,1)}, u32[]{:S(2)}, u32[]{:S(2)}) %collective-permute-start) | collective-permute-done | bytes 819232 | tf_op jit(solution)/shard_map/ppermute | solution.py:347
  41.8 0.0 all-to-all-done.1.refs_0_
  41.8 4.4 %all-to-all-start.2 = ((bf16[8,400,128]{2,1,0:T(8,128)(2,1)}), bf16[8,400,128]{2,1,0:T(8,128)(2,1)S(1)}, u32[]{:S(2)}, u32[]{:S(2)}) async-start(bf16[8,400,128]{2,1,0:T(8,128)(2,1)} %collective-permute-done), calls=%async_computation.2 | async-start | bytes 1638400 | tf_op jit(solution)/shard_map/all_to_all | solution.py:369
  46.3 0.1 stack.43.where_ref
  46.4 0.0 collective-permute-done.4.refs_5_
  46.4 0.0 collective-permute-done.5.refs_6_
  46.4 0.0 collective-permute-done.6.refs_7_
  46.4 0.0 collective-permute-done.7.refs_8_
  46.4 3.3 %send_part.2 = bf16[1,256,512]{2,1,0:T(8,128)(2,1)S(1)} custom-call(s32[10]{0:T(128)S(1)} %stack.43.where_ref, bf16[8,400,128]{2,1,0:T(8,128)(2,1)S(1)} %all-to-all-done.1.refs_0_, bf16[512,512]{1,0:T(8,128)(2,1)S(1)} %copy-done, bf16[512,512]{1,0:T(8,128)(2,1)} %collective-permute-done.2.refs_2_, bf16[512,512]{1,0:T(8,128)(2,1)} %collective-permute-done.1.refs_3_, ...), custom_call_target="tpu_custom_call" | custom-call | flops 2147483648 | bytes 2916352 | tf_op jit(solution)/shard_map/send_part/pallas_call | solution.py:210
  49.7 1.5 %collective-permute-start.9 = (bf16[1,256,512]{2,1,0:T(8,128)(2,1)S(1)}, bf16[1,256,512]{2,1,0:T(8,128)(2,1)S(1)}, u32[]{:S(2)}, u32[]{:S(2)}) collective-permute-start(bf16[1,256,512]{2,1,0:T(8,128)(2,1)S(1)} %send_part.2), channel_id=1, source_target_pairs={{0,2},{1,3},{2,0},{3,1},{4,6},{5,7},{6,4},{7,5},{8,10},{9,11},{10,... | collective-permute-start | bytes 786440 | tf_op jit(solution)/shard_map/ppermute | solution.py:347
  51.3 8.0 %all-to-all-done.2.refs_0_ = bf16[8,400,128]{2,1,0:T(8,128)(2,1)S(1)} async-done(((bf16[8,400,128]{2,1,0:T(8,128)(2,1)}), bf16[8,400,128]{2,1,0:T(8,128)(2,1)S(1)}, u32[]{:S(2)}, u32[]{:S(2)}) %all-to-all-start.2) | async-done | bytes 819232 | tf_op jit(solution)/shard_map/all_to_all | solution.py:369
  59.2 3.3 %send_part.3 = bf16[1,256,512]{2,1,0:T(8,128)(2,1)S(1)} custom-call(s32[10]{0:T(128)S(1)} %stack.43.where_ref, bf16[8,400,128]{2,1,0:T(8,128)(2,1)S(1)} %all-to-all-done.2.refs_0_, bf16[512,512]{1,0:T(8,128)(2,1)S(1)} %copy-done, bf16[512,512]{1,0:T(8,128)(2,1)} %collective-permute-done.2.refs_2_, bf16[512,512]{1,0:T(8,128)(2,1)} %collective-permute-done.1.refs_3_, ...), custom_call_target="tpu_custom_call" | custom-call | flops 2147483648 | bytes 2916352 | tf_op jit(solution)/shard_map/send_part/pallas_call | solution.py:210
  62.6 1.5 %collective-permute-start.8 = (bf16[1,256,512]{2,1,0:T(8,128)(2,1)S(1)}, bf16[1,256,512]{2,1,0:T(8,128)(2,1)S(1)}, u32[]{:S(2)}, u32[]{:S(2)}) collective-permute-start(bf16[1,256,512]{2,1,0:T(8,128)(2,1)S(1)} %send_part.3), channel_id=1, source_target_pairs={{0,2},{1,3},{2,0},{3,1},{4,6},{5,7},{6,4},{7,5},{8,10},{9,11},{10,... | collective-permute-start | bytes 786440 | tf_op jit(solution)/shard_map/ppermute | solution.py:347
  64.1 4.1 %own_part.2.refs_9_ = f32[256,2048]{1,0:T(8,128)} custom-call(s32[10]{0:T(128)S(1)} %stack.43.where_ref, bf16[8,400,128]{2,1,0:T(8,128)(2,1)S(1)} %all-to-all-done.1.refs_0_, bf16[512,512]{1,0:T(8,128)(2,1)S(1)} %copy-done, bf16[512,512]{1,0:T(8,128)(2,1)} %collective-permute-done.2.refs_2_, bf16[512,512]{1,0:T(8,128)(2,1)} %collective-permute-done.1.refs_3_, ...), custom_call_target="tpu_custom_call" | custom-call | flops 2147483648 | bytes 2916352 | tf_op jit(solution)/shard_map/own_part/pallas_call | solution.py:210
  68.2 4.1 %own_part.3._ = f32[256,2048]{1,0:T(8,128)} custom-call(s32[10]{0:T(128)S(1)} %stack.43.where_ref, bf16[8,400,128]{2,1,0:T(8,128)(2,1)S(1)} %all-to-all-done.2.refs_0_, bf16[512,512]{1,0:T(8,128)(2,1)S(1)} %copy-done, bf16[512,512]{1,0:T(8,128)(2,1)} %collective-permute-done.2.refs_2_, ...), custom_call_target="tpu_custom_call", output_to_operand_aliasing={{}: (10, {})} | custom-call | flops 2147483648 | bytes 2916352 | tf_op jit(solution)/shard_map/own_part/pallas_call | solution.py:210
  72.3 0.0 collective-permute-done.9.got_ref
  72.4 1.4 %place.2._ = f32[256,2048]{1,0:T(8,128)} custom-call(s32[10]{0:T(128)S(1)} %stack.43.where_ref, bf16[1,256,512]{2,1,0:T(8,128)(2,1)S(1)} %collective-permute-done.9.got_ref, f32[256,2048]{1,0:T(8,128)} %own_part.3._), custom_call_target="tpu_custom_call", output_to_operand_aliasing={{}: (2, {})} | custom-call | bytes 786432 | tf_op jit(solution)/shard_map/place/pallas_call | solution.py:260
  73.7 2.5 %collective-permute-done.8.got_ref = bf16[1,256,512]{2,1,0:T(8,128)(2,1)S(1)} collective-permute-done((bf16[1,256,512]{2,1,0:T(8,128)(2,1)S(1)}, bf16[1,256,512]{2,1,0:T(8,128)(2,1)S(1)}, u32[]{:S(2)}, u32[]{:S(2)}) %collective-permute-start.8) | collective-permute-done | bytes 262176 | tf_op jit(solution)/shard_map/ppermute | solution.py:347
  76.3 1.4 %place.3 = f32[256,2048]{1,0:T(8,128)} custom-call(s32[10]{0:T(128)S(1)} %stack.43.where_ref, bf16[1,256,512]{2,1,0:T(8,128)(2,1)S(1)} %collective-permute-done.8.got_ref, f32[256,2048]{1,0:T(8,128)} %place.2._), custom_call_target="tpu_custom_call", output_to_operand_aliasing={{}: (2, {})} | custom-call | bytes 786432 | tf_op jit(solution)/shard_map/place/pallas_call | solution.py:260
Async XLA Ops:
  1.9 11.8 %collective-permute-start.2 = (bf16[512,512]{1,0:T(8,128)(2,1)}, bf16[512,512]{1,0:T(8,128)(2,1)}, u32[]{:S(2)}, u32[]{:S(2)}) collective-permute-start(bf16[512,512]{1,0:T(8,128)(2,1)} %get-tuple-element.16.refs_1_), channel_id=1, source_target_pairs={{0,8},{4,20},{8,0},{12,28},{16,24},{20,4},{24,16},{28,12},{1,9},{5... | collective-permute-start | bytes 1572872 | tf_op jit(solution)/shard_map/ppermute | solution.py:350
  4.9 10.9 %all-to-all-start = ((bf16[8,8,512]{2,1,0:T(8,128)(2,1)}), bf16[8,8,512]{2,1,0:T(8,128)(2,1)S(1)}, u32[]{:S(2)}, u32[]{:S(2)}) async-start(bf16[8,8,512]{2,1,0:T(8,128)(2,1)} %get-tuple-element.15), calls=%async_computation | async-start | bytes 131072 | tf_op jit(solution)/shard_map/all_to_all | solution.py:353
  8.3 16.4 %collective-permute-start.1 = (bf16[512,512]{1,0:T(8,128)(2,1)}, bf16[512,512]{1,0:T(8,128)(2,1)}, u32[]{:S(2)}, u32[]{:S(2)}) collective-permute-start(bf16[512,512]{1,0:T(8,128)(2,1)} %get-tuple-element.16.refs_1_), channel_id=1, source_target_pairs={{0,16},{4,12},{8,24},{12,4},{16,0},{20,28},{24,8},{28,20},{1,17},{... | collective-permute-start | bytes 1572872 | tf_op jit(solution)/shard_map/ppermute | solution.py:350
  13.7 10.9 %collective-permute-start.3 = (bf16[512,512]{1,0:T(8,128)(2,1)}, bf16[512,512]{1,0:T(8,128)(2,1)}, u32[]{:S(2)}, u32[]{:S(2)}) collective-permute-start(bf16[512,512]{1,0:T(8,128)(2,1)} %collective-permute-done.2.refs_2_), channel_id=1, source_target_pairs={{0,16},{4,12},{8,24},{12,4},{16,0},{20,28},{24,8},{28,20},{1,17},{... | collective-permute-start | bytes 1572872 | tf_op jit(solution)/shard_map/ppermute | solution.py:350
  15.9 0.6 copy-start.1
  16.5 11.7 %copy-start = (bf16[512,512]{1,0:T(8,128)(2,1)S(1)}, bf16[512,512]{1,0:T(8,128)(2,1)}, u32[]{:S(2)}) copy-start(bf16[512,512]{1,0:T(8,128)(2,1)} %get-tuple-element.16.refs_1_) | copy-start | bytes 1572868
  23.2 18.6 %collective-permute-start = (bf16[8,400,128]{2,1,0:T(8,128)(2,1)}, bf16[8,400,128]{2,1,0:T(8,128)(2,1)}, u32[]{:S(2)}, u32[]{:S(2)}) collective-permute-start(bf16[8,400,128]{2,1,0:T(8,128)(2,1)} %half_transform.1), channel_id=1, source_target_pairs={{0,1},{1,0},{2,3},{3,2},{4,5},{5,4},{6,7},{7,6},{8,9},{9,8},{10,11... | collective-permute-start | bytes 2457608 | tf_op jit(solution)/shard_map/ppermute | solution.py:347
  24.6 17.2 %all-to-all-start.1 = ((bf16[8,400,128]{2,1,0:T(8,128)(2,1)}), bf16[8,400,128]{2,1,0:T(8,128)(2,1)S(1)}, u32[]{:S(2)}, u32[]{:S(2)}) async-start(bf16[8,400,128]{2,1,0:T(8,128)(2,1)} %half_transform.1), calls=%async_computation.1 | async-start | bytes 1638400 | tf_op jit(solution)/shard_map/all_to_all | solution.py:367
  28.2 18.2 %collective-permute-start.4 = (bf16[512,512]{1,0:T(8,128)(2,1)S(1)}, bf16[512,512]{1,0:T(8,128)(2,1)S(1)}, u32[]{:S(2)}, u32[]{:S(2)}) collective-permute-start(bf16[512,512]{1,0:T(8,128)(2,1)S(1)} %copy-done), channel_id=1, source_target_pairs={{0,4},{4,0},{8,12},{12,8},{16,20},{20,16},{24,28},{28,24},{1,5},{5... | collective-permute-start | bytes 1572872 | tf_op jit(solution)/shard_map/ppermute | solution.py:350
  28.6 17.8 %collective-permute-start.5 = (bf16[512,512]{1,0:T(8,128)(2,1)}, bf16[512,512]{1,0:T(8,128)(2,1)}, u32[]{:S(2)}, u32[]{:S(2)}) collective-permute-start(bf16[512,512]{1,0:T(8,128)(2,1)} %collective-permute-done.2.refs_2_), channel_id=1, source_target_pairs={{0,4},{4,0},{8,12},{12,8},{16,20},{20,16},{24,28},{28,24},{1,5},{5... | collective-permute-start | bytes 1572872 | tf_op jit(solution)/shard_map/ppermute | solution.py:350
  28.8 17.6 %collective-permute-start.6 = (bf16[512,512]{1,0:T(8,128)(2,1)}, bf16[512,512]{1,0:T(8,128)(2,1)}, u32[]{:S(2)}, u32[]{:S(2)}) collective-permute-start(bf16[512,512]{1,0:T(8,128)(2,1)} %collective-permute-done.1.refs_3_), channel_id=1, source_target_pairs={{0,4},{4,0},{8,12},{12,8},{16,20},{20,16},{24,28},{28,24},{1,5},{5... | collective-permute-start | bytes 1572872 | tf_op jit(solution)/shard_map/ppermute | solution.py:350
  29.1 17.3 %collective-permute-start.7 = (bf16[512,512]{1,0:T(8,128)(2,1)}, bf16[512,512]{1,0:T(8,128)(2,1)}, u32[]{:S(2)}, u32[]{:S(2)}) collective-permute-start(bf16[512,512]{1,0:T(8,128)(2,1)} %collective-permute-done.3.refs_4_), channel_id=1, source_target_pairs={{0,4},{4,0},{8,12},{12,8},{16,20},{20,16},{24,28},{28,24},{1,5},{5... | collective-permute-start | bytes 1572872 | tf_op jit(solution)/shard_map/ppermute | solution.py:350
  41.8 17.4 %all-to-all-start.2 = ((bf16[8,400,128]{2,1,0:T(8,128)(2,1)}), bf16[8,400,128]{2,1,0:T(8,128)(2,1)S(1)}, u32[]{:S(2)}, u32[]{:S(2)}) async-start(bf16[8,400,128]{2,1,0:T(8,128)(2,1)} %collective-permute-done), calls=%async_computation.2 | async-start | bytes 1638400 | tf_op jit(solution)/shard_map/all_to_all | solution.py:369
  49.7 22.6 %collective-permute-start.9 = (bf16[1,256,512]{2,1,0:T(8,128)(2,1)S(1)}, bf16[1,256,512]{2,1,0:T(8,128)(2,1)S(1)}, u32[]{:S(2)}, u32[]{:S(2)}) collective-permute-start(bf16[1,256,512]{2,1,0:T(8,128)(2,1)S(1)} %send_part.2), channel_id=1, source_target_pairs={{0,2},{1,3},{2,0},{3,1},{4,6},{5,7},{6,4},{7,5},{8,10},{9,11},{10,... | collective-permute-start | bytes 786440 | tf_op jit(solution)/shard_map/ppermute | solution.py:347
  62.6 13.7 %collective-permute-start.8 = (bf16[1,256,512]{2,1,0:T(8,128)(2,1)S(1)}, bf16[1,256,512]{2,1,0:T(8,128)(2,1)S(1)}, u32[]{:S(2)}, u32[]{:S(2)}) collective-permute-start(bf16[1,256,512]{2,1,0:T(8,128)(2,1)S(1)} %send_part.3), channel_id=1, source_target_pairs={{0,2},{1,3},{2,0},{3,1},{4,6},{5,7},{6,4},{7,5},{8,10},{9,11},{10,... | collective-permute-start | bytes 786440 | tf_op jit(solution)/shard_map/ppermute | solution.py:347
